TPU v7x, 32 devices: a whole 2x2x4 slice. The times are simulated.
32 devices in a mesh: section: 2 (over x), dp: 8 (over z, core), tensor: 2 (over y).
Axes of the slice: x: 2, y: 2, z: 4, core: 2. Of those that a mesh axis runs over, the one named last changes fastest.
Arguments:
- block_input: bfloat16 [8, 2, 512, 1536], P('dp', None, 'tensor'), may hold values from -6 to 6
- plan: int32 [8, 2], P('dp'), may hold values from 0 to 1, each once within a row
- lengths: int32 [8, 2], P('dp'), may hold values from 128 to 512, as said below
- norm_gain: float32 [2, 1536], P('section'), may hold values from 0.1 to 1.9
- gate_proj: bfloat16 [2, 1536, 3072], P('section', 'dp', 'tensor'), may hold values from -0.15625 to 0.15625
- value_proj: bfloat16 [2, 1536, 3072], P('section', 'dp', 'tensor'), may hold values from -0.15625 to 0.15625
- shared_proj: bfloat16 [2, 1536, 256], P('section', 'dp', 'tensor'), may hold values from -0.15625 to 0.15625
- step_proj: bfloat16 [2, 1536, 48], P('section', 'dp', 'tensor'), may hold values from -0.15625 to 0.15625
- conv_value: float32 [2, 5, 3072], P('section', None, 'tensor'), may hold values from -3 to 3
- conv_shared: float32 [2, 5, 256], P('section', None, 'tensor'), may hold values from -3 to 3
- head_params: float32 [2, 3, 48], P('section', None, 'tensor'), may hold values from -7 to 3, as said below
- gate_gain: float32 [2, 3072], P('section', 'tensor'), may hold values from 0.1 to 1.9
- out_proj: bfloat16 [2, 1536, 3072], P('section', 'dp', 'tensor'), may hold values from -0.109375 to 0.109375
- cotangent: bfloat16 [8, 2, 512, 1536], P('dp', None, 'tensor'), may hold values from -6 to 6
Outputs:
- relay_ends: float32 [2, 8, 2, 512, 1536], P('section', 'dp', None, 'tensor')
- grad_norm_gain: float32 [2, 1536], P('section')
- grad_gate_proj: float32 [2, 1536, 3072], P('section', 'dp', 'tensor')
- grad_value_proj: float32 [2, 1536, 3072], P('section', 'dp', 'tensor')
- grad_shared_proj: float32 [2, 1536, 256], P('section', 'dp', 'tensor')
- grad_step_proj: float32 [2, 1536, 48], P('section', 'dp', 'tensor')
- grad_conv_value: float32 [2, 5, 3072], P('section', None, 'tensor')
- grad_conv_shared: float32 [2, 5, 256], P('section', None, 'tensor')
- grad_head_params: float32 [2, 3, 48], P('section', None, 'tensor')
- grad_gate_gain: float32 [2, 3072], P('section', 'tensor')
- grad_out_proj: float32 [2, 1536, 3072], P('section', 'dp', 'tensor')
Inputs may be any that keep to these rules, and one draw needn't show every extreme that they name: lengths[d, k] valid tokens stand at the start of micro-batch plan[d, k]; in every row one entry equals 512. `plan`: each row names every micro-batch once. `head_params`: row 0: step biases; row 1: logarithms of the decay rates; row 2: skip weights.
All inputs are finite; a program needn't handle non-finite values.
Results may differ from a plain program's by a relative error of at most 0.015.
Values may be sent and summed in bfloat16 or wider, within the bound.
No kernel may reach another device: no remote copies, remote signals or barrier semaphores. Data moves between devices by JAX's collectives and lax.ppermute only.
A program may use at most 320 MiB of HBM per device.

v0:
```python
import jax
import jax.numpy as jnp
from jax import lax
from jax.sharding import PartitionSpec as P

DI = 3072
P_SIZE = 64
N = 128
CONV = 4
Q = 256


eps = 1e-05
highest = lax.Precision.HIGHEST


def passed_along(array, axis, by):
    size = lax.axis_size(axis)
    pairs = [(i, i + by) for i in range(size) if 0 <= i + by < size]
    return lax.ppermute(array, axis, pairs)


def rms_norm(residual, gain_vector):
    return (
        residual
        * lax.rsqrt(jnp.mean(residual * residual, axis=1, keepdims=True) + eps)
        * gain_vector
    )


def conv_silu(values, kernel):
    length = values.shape[0]
    padded = jnp.concatenate([jnp.zeros((CONV - 1, values.shape[1]), jnp.float32), values], axis=0)
    summed = kernel[CONV] + kernel[0] * padded[0:length]
    for offset in range(1, CONV):
        summed = summed + kernel[offset] * padded[offset : offset + length]
    return jax.nn.silu(summed)


def scan_state(carried, inputs):
    factor, update = inputs
    return (factor[:, None, None] * carried + update, carried)


def state_space(inputs_x, step_size, decay_rate, keys_b, reads_c):
    length, head_count, head_width = inputs_x.shape
    blocks = length // Q
    scaled = (step_size * decay_rate[None, :]).reshape(blocks, Q, head_count)
    running = jnp.cumsum(scaled, axis=1).transpose(0, 2, 1)
    weighted = (inputs_x * step_size[:, :, None]).reshape(blocks, Q, head_count, head_width)
    block_b = keys_b.reshape(blocks, Q, N)
    block_c = reads_c.reshape(blocks, Q, N)
    scores = jnp.einsum("bin,bjn->bij", block_c, block_b, precision=highest)
    rowpos = lax.broadcasted_iota(jnp.int32, (Q, Q), 0)
    colpos = lax.broadcasted_iota(jnp.int32, (Q, Q), 1)
    spread = running[:, :, :, None] - running[:, :, None, :]
    decays = jnp.exp(jnp.where(rowpos >= colpos, spread, -1e30))
    mixing = decays * scores[:, None, :, :]
    within_block = jnp.einsum("bhij,bjhp->bihp", mixing, weighted, precision=highest)
    tail_decay = jnp.exp(running[:, :, -1:] - running).transpose(0, 2, 1)
    tailed = weighted * tail_decay[:, :, :, None]
    states = jnp.einsum("bjn,bjhp->bhpn", block_b, tailed, precision=highest)
    factors = jnp.exp(running[:, :, -1])
    start_state = jnp.zeros((head_count, head_width, N), jnp.float32)
    unused, entering = lax.scan(scan_state, start_state, (factors, states))
    across_block = jnp.einsum("bin,bhpn->bihp", block_c, entering, precision=highest)
    across_block = across_block * jnp.exp(running).transpose(0, 2, 1)[:, :, :, None]
    return (within_block + across_block).reshape(length, head_count, head_width)


def mixer_core(pre_z, pre_x, pre_dt, shared_bc, kernel_x, head_values):
    length = pre_x.shape[0]
    head_count = pre_dt.shape[1]
    mixed_x = conv_silu(pre_x, kernel_x)
    step_size = jax.nn.softplus(pre_dt + head_values[0])
    decay_rate = -jnp.exp(head_values[1])
    heads_x = mixed_x.reshape(length, head_count, P_SIZE)
    result = state_space(heads_x, step_size, decay_rate, shared_bc[:, :N], shared_bc[:, N:])
    result = result + head_values[2][None, :, None] * heads_x
    gated = result.reshape(length, head_count * P_SIZE) * jax.nn.silu(pre_z)
    return (gated, jnp.sum(gated * gated, axis=1))


def gate_finish(gated, square_sum, gain_vector):
    return gated * lax.rsqrt(square_sum[:, None] / DI + eps) * gain_vector


def guarded(active, compute):
    return lax.cond(active, compute, lambda: jax.tree.map(jnp.zeros_like, compute()))


def contract_rows(left_side, right_side):
    return lax.dot_general(
        left_side, right_side, (((0,), (0,)), ((), ())), preferred_element_type=jnp.float32
    )


def contract_cols(left_side, right_side):
    return lax.dot_general(
        left_side, right_side, (((1,), (1,)), ((), ())), preferred_element_type=jnp.float32
    )


def local(
    block_input,
    plan,
    lengths,
    norm_gain,
    gate_proj,
    value_proj,
    shared_proj,
    step_proj,
    conv_value,
    conv_shared,
    head_params,
    gate_gain,
    out_proj,
    cotangent,
):
    section_index = lax.axis_index("section")
    tensor_index = lax.axis_index("tensor")
    tensor_count = lax.axis_size("tensor")
    micro_count = block_input.shape[1]
    half_rows = block_input.shape[2]
    model_width = block_input.shape[3]
    gate_all, value_all, shared_all, step_all, out_all = (
        lax.all_gather(gate_proj[0], "dp", axis=0, tiled=True),
        lax.all_gather(value_proj[0], "dp", axis=0, tiled=True),
        lax.all_gather(shared_proj[0], "dp", axis=0, tiled=True),
        lax.all_gather(step_proj[0], "dp", axis=0, tiled=True),
        lax.all_gather(out_proj[0], "dp", axis=0, tiled=True),
    )
    local_inner = gate_all.shape[1]
    local_shared = shared_all.shape[1]
    in_all = jnp.concatenate([gate_all, value_all, shared_all, step_all], axis=1)
    splits = (local_inner, 2 * local_inner, 2 * local_inner + local_shared)
    gain_norm = norm_gain[0]
    kernel_value = conv_value[0]
    kernel_shared = conv_shared[0]
    heads_local = head_params[0]
    gain_gate = gate_gain[0]
    row_ids = tensor_index * half_rows + lax.broadcasted_iota(jnp.int32, (half_rows, 1), 0)
    order = plan[0]
    valid_lengths = lengths[0]
    is_first = section_index == 0
    is_last = section_index == 1
    incoming = jnp.zeros((half_rows, model_width), jnp.float32)
    outputs_buf = jnp.zeros((micro_count, half_rows, model_width), jnp.float32)
    saved = []
    for tick in range(micro_count + 1):
        position = tick - section_index
        active = (position >= 0) & (position < micro_count)
        batch_id = order[jnp.clip(position, 0, micro_count - 1)]
        own_input = lax.dynamic_index_in_dim(block_input[0], batch_id, 0, keepdims=False).astype(
            jnp.float32
        )
        residual = jnp.where(is_first, own_input, incoming)
        normed = rms_norm(residual, gain_norm).astype(jnp.bfloat16)
        gathered = lax.all_gather(normed, "tensor", axis=0, tiled=True)
        projected = guarded(
            active, lambda: jnp.dot(gathered, in_all, preferred_element_type=jnp.float32)
        )
        pre_z, pre_x, pre_bc, pre_dt = jnp.split(projected, splits, axis=1)
        shared_half = conv_silu(pre_bc, kernel_shared)
        shared_bc = lax.all_gather(shared_half, "tensor", axis=1, tiled=True)
        gated, square_part = guarded(
            active, lambda: mixer_core(pre_z, pre_x, pre_dt, shared_bc, kernel_value, heads_local)
        )
        square_sum = lax.psum(square_part, "tensor")
        outgoing = gate_finish(gated, square_sum, gain_gate).astype(jnp.bfloat16)

        def out_rows(first_row, row_count, outgoing=outgoing, active=active):
            return guarded(active, lambda: contract_cols(outgoing, out_all))

        added = lax.psum_scatter(
            out_rows(jnp.int32(0), half_rows * lax.axis_size("tensor")),
            "tensor",
            scatter_dimension=0,
            tiled=True,
        )
        result = residual + added
        outputs_buf = jnp.where(
            active & is_last,
            lax.dynamic_update_index_in_dim(outputs_buf, result, batch_id, 0),
            outputs_buf,
        )
        incoming = passed_along(result, "section", 1)
        saved.append((residual, gathered, projected, shared_bc, gated, square_sum, outgoing))
    saved_stack = jax.tree.map(lambda *members: jnp.stack(members), *saved)
    rows_kept = []
    pre_kept = []
    back_kept = []
    sent_kept = []
    acc_norm = jnp.zeros_like(gain_norm)
    acc_value = jnp.zeros_like(kernel_value)
    acc_shared = jnp.zeros_like(kernel_shared)
    acc_heads = jnp.zeros_like(heads_local)
    acc_gate = jnp.zeros_like(gain_gate)
    returning = jnp.zeros((half_rows, model_width), jnp.float32)
    input_grads = jnp.zeros((micro_count, half_rows, model_width), jnp.float32)
    for tick in range(micro_count + 1):
        position = tick - 1 + section_index
        active = (position >= 0) & (position < micro_count)
        clipped = jnp.clip(position, 0, micro_count - 1)
        batch_id = order[clipped]
        limit = valid_lengths[clipped]
        residual, gathered, projected, shared_bc, gated, square_sum, outgoing = jax.tree.map(
            lambda stacked: lax.dynamic_index_in_dim(
                stacked, clipped + section_index, 0, keepdims=False
            ),
            saved_stack,
        )
        mask_rows = (row_ids < limit).astype(jnp.float32)
        own_grad = (
            lax.dynamic_index_in_dim(cotangent[0], batch_id, 0, keepdims=False).astype(jnp.float32)
            * mask_rows
        )
        upstream = jnp.where(active, jnp.where(is_last, own_grad, returning), 0.0)
        grad_rows_all = lax.all_gather(upstream.astype(jnp.bfloat16), "tensor", axis=0, tiled=True)
        grad_outgoing = guarded(
            active, lambda: jnp.dot(grad_rows_all, out_all, preferred_element_type=jnp.float32)
        )
        unused, finish_pull = jax.vjp(gate_finish, gated, square_sum, gain_gate)
        grad_gated, grad_square, grad_gain_gate = finish_pull(grad_outgoing)
        grad_square = lax.psum(grad_square, "tensor")

        def core_back(
            projected=projected, shared_bc=shared_bc, grad_gated=grad_gated, grad_square=grad_square
        ):
            pre_z, pre_x, pre_bc, pre_dt = jnp.split(projected, splits, axis=1)
            unused_out, core_pull = jax.vjp(
                mixer_core, pre_z, pre_x, pre_dt, shared_bc, kernel_value, heads_local
            )
            return core_pull((grad_gated, grad_square))

        grad_z, grad_x, grad_dt, grad_shared, grad_kernel_value, grad_heads = guarded(
            active, core_back
        )
        grad_shared_half = lax.psum_scatter(grad_shared, "tensor", scatter_dimension=1, tiled=True)
        pre_bc = projected[:, 2 * local_inner : 2 * local_inner + local_shared]
        unused, conv_pull = jax.vjp(conv_silu, pre_bc, kernel_shared)
        grad_bc, grad_kernel_shared = conv_pull(grad_shared_half)
        grad_pre = jnp.concatenate([grad_z, grad_x, grad_bc, grad_dt], axis=1).astype(jnp.bfloat16)

        def back_rows(first_row, row_count, grad_pre=grad_pre, active=active):
            return guarded(active, lambda: contract_cols(grad_pre, in_all))

        grad_normed = lax.psum_scatter(
            back_rows(jnp.int32(0), half_rows * lax.axis_size("tensor")),
            "tensor",
            scatter_dimension=0,
            tiled=True,
        )
        unused, norm_pull = jax.vjp(rms_norm, residual, gain_norm)
        grad_residual, grad_gain_norm = norm_pull(grad_normed)
        total_grad = upstream + grad_residual
        input_grads = jnp.where(
            active & is_first,
            lax.dynamic_update_index_in_dim(input_grads, total_grad, batch_id, 0),
            input_grads,
        )
        returning = passed_along(total_grad.astype(jnp.bfloat16), "section", -1).astype(
            total_grad.dtype
        )
        acc_norm = acc_norm + jnp.where(active, grad_gain_norm, 0.0)
        acc_value = acc_value + jnp.where(active, grad_kernel_value, 0.0)
        acc_shared = acc_shared + jnp.where(active, grad_kernel_shared, 0.0)
        acc_heads = acc_heads + jnp.where(active, grad_heads, 0.0)
        acc_gate = acc_gate + jnp.where(active, grad_gain_gate, 0.0)
        rows_kept.append(gathered)
        pre_kept.append(grad_pre)
        back_kept.append(grad_rows_all)
        sent_kept.append(outgoing)
    acc_in = contract_rows(jnp.concatenate(rows_kept, axis=0), jnp.concatenate(pre_kept, axis=0))
    acc_out = contract_rows(jnp.concatenate(back_kept, axis=0), jnp.concatenate(sent_kept, axis=0))
    shard_in, shard_out = (
        lax.psum_scatter(acc_in.astype(jnp.bfloat16), "dp", scatter_dimension=0, tiled=True).astype(
            jnp.float32
        ),
        lax.psum_scatter(
            acc_out.astype(jnp.bfloat16), "dp", scatter_dimension=0, tiled=True
        ).astype(jnp.float32),
    )
    grad_gate_w, grad_value_w, grad_shared_w, grad_step_w = jnp.split(shard_in, splits, axis=1)

    def widen(partial_value, axis_dim):
        full_shape = list(partial_value.shape)
        full_shape[axis_dim] = full_shape[axis_dim] * tensor_count
        return lax.dynamic_update_slice_in_dim(
            jnp.zeros(full_shape, jnp.float32),
            partial_value,
            tensor_index * partial_value.shape[axis_dim],
            axis_dim,
        )

    def narrow(summed, partial_value, axis_dim):
        return lax.dynamic_slice_in_dim(
            summed,
            tensor_index * partial_value.shape[axis_dim],
            partial_value.shape[axis_dim],
            axis_dim,
        )

    sum_norm, sum_value, sum_shared, sum_heads, sum_gate = lax.psum(
        (
            acc_norm,
            widen(acc_value, 1),
            widen(acc_shared, 1),
            widen(acc_heads, 1),
            widen(acc_gate, 0),
        ),
        ("dp", "tensor"),
    )
    relay_ends = jnp.where(is_first, input_grads, outputs_buf)[None, None]
    return (
        relay_ends,
        sum_norm[None],
        grad_gate_w[None],
        grad_value_w[None],
        grad_shared_w[None],
        grad_step_w[None],
        narrow(sum_value, acc_value, 1)[None],
        narrow(sum_shared, acc_shared, 1)[None],
        narrow(sum_heads, acc_heads, 1)[None],
        narrow(sum_gate, acc_gate, 0)[None],
        shard_out[None],
    )


def solution(mesh):
    placed = (
        P("dp", None, "tensor", None),
        P("dp", None),
        P("dp", None),
        P("section", None),
        P("section", "dp", "tensor"),
        P("section", "dp", "tensor"),
        P("section", "dp", "tensor"),
        P("section", "dp", "tensor"),
        P("section", None, "tensor"),
        P("section", None, "tensor"),
        P("section", None, "tensor"),
        P("section", "tensor"),
        P("section", "dp", "tensor"),
        P("dp", None, "tensor", None),
    )
    return jax.shard_map(
        local,
        mesh=mesh,
        in_specs=placed,
        out_specs=(
            P("section", "dp", None, "tensor", None),
            P("section", None),
            P("section", "dp", "tensor"),
            P("section", "dp", "tensor"),
            P("section", "dp", "tensor"),
            P("section", "dp", "tensor"),
            P("section", None, "tensor"),
            P("section", None, "tensor"),
            P("section", None, "tensor"),
            P("section", "tensor"),
            P("section", "dp", "tensor"),
        ),
        check_vma=False,
    )
```

profile of v0, /device:TPU:0, one launch (start us, length us, event | category | flops | bytes accessed | tf_op | source)
XLA Modules:
  0.0 2058.3 jit_solution(2900272470210095595)
XLA Ops:
  17.6 17.5 all-gather.3
  35.2 16.4 all-gather.2
  51.6 18.6 all-gather.29.cloned.1.call-done
  70.3 52.1 %all-gather.27.cloned.1.call-done = bf16[1,1536,1536]{2,1,0:T(8,128)(2,1)} async-done(((bf16[1,192,1536]{2,1,0:T(8,128)(2,1)}), bf16[1,1536,1536]{2,1,0:T(8,128)(2,1)}) %all-gather.27.cloned.1.call-update) | async-done | bytes 4718608 | tf_op jit(solution)/shard_map/all_gather | solution.py:127
  131.8 18.8 all-gather.15.cloned.1.call-done
  175.6 70.7 %conditional.19 = (f32[512]{0:T(512)S(1)}, f32[1,512,1536]{1,2,0:T(8,128)}, f32[512,1536]{1,0:T(8,128)}) conditional(s32[]{:T(128)} %convert_element_type.152, () %tuple.257, (f32[5,1536]{1,0:T(8,128)S(1)}, f32[512,3224]{0,1:T(8,128)}, f32[3,24]{1,0:T(4,128)S(1)}, f32[512,256]{1,0:T(8,128)S(1)}) %tuple.793), branch_computations={%region_3.4_spmd, %region_4.10_spmd} | conditional | flops 5074247168 | bytes 118578864 | solution.py:89
  201.2 15.1 fusion.12
  261.4 42.5 %reduce-scatter.12.cloned.1.call-done = f32[256,1536]{1,0:T(8,128)} async-done(((f32[512,1536]{1,0:T(8,128)}), f32[256,1536]{1,0:T(8,128)}) %reduce-scatter.12.cloned.1.call-update) | async-done | bytes 1572880 | tf_op jit(solution)/shard_map/reduce_scatter | solution.py:175
  314.5 30.8 %collective-permute-done = f32[256,1536]{1,0:T(8,128)} collective-permute-done((f32[256,1536]{1,0:T(8,128)}, f32[256,1536]{1,0:T(8,128)}, u32[]{:S(2)}, u32[]{:S(2)}) %collective-permute-start) | collective-permute-done | bytes 1572896 | tf_op jit(solution)/shard_map/ppermute | solution.py:20
  347.4 31.2 %all-gather.17.cloned.1.call-done = bf16[512,1536]{1,0:T(8,128)(2,1)} async-done(((bf16[256,1536]{1,0:T(8,128)(2,1)}), bf16[512,1536]{1,0:T(8,128)(2,1)}) %all-gather.17.cloned.1.call-update) | async-done | bytes 1572880 | tf_op jit(solution)/shard_map/all_gather | solution.py:159
  403.7 75.6 %conditional.22 = (f32[512]{0:T(512)S(1)}, f32[1,512,1536]{1,2,0:T(8,128)}, f32[512,1536]{1,0:T(8,128)}) conditional(s32[]{:T(128)} %convert_element_type.155, () %tuple.263, (f32[5,1536]{1,0:T(8,128)S(1)}, f32[512,3224]{0,1:T(8,128)}, f32[3,24]{1,0:T(4,128)S(1)}, f32[512,256]{1,0:T(8,128)S(1)}) %tuple.794), branch_computations={%region_17.18_spmd, %region_18.24_spmd} | conditional | flops 5074247168 | bytes 101146080 | solution.py:89
  427.5 15.1 fusion.34
  494.9 43.4 %reduce-scatter.14.cloned.1.call-done = f32[256,1536]{1,0:T(8,128)} async-done(((f32[512,1536]{1,0:T(8,128)}), f32[256,1536]{1,0:T(8,128)}) %reduce-scatter.14.cloned.1.call-update) | async-done | bytes 1572880 | tf_op jit(solution)/shard_map/reduce_scatter | solution.py:175
  554.4 25.8 %collective-permute-done.1 = f32[256,1536]{1,0:T(8,128)} collective-permute-done((f32[256,1536]{1,0:T(8,128)}, f32[256,1536]{1,0:T(8,128)}, u32[]{:S(2)}, u32[]{:S(2)}) %collective-permute-start.1) | collective-permute-done | bytes 1572896 | tf_op jit(solution)/shard_map/ppermute | solution.py:20
  592.0 21.5 %all-gather.19.cloned.1.call-done = bf16[512,1536]{1,0:T(8,128)(2,1)} async-done(((bf16[256,1536]{1,0:T(8,128)(2,1)}), bf16[512,1536]{1,0:T(8,128)(2,1)}) %all-gather.19.cloned.1.call-update) | async-done | bytes 1572880 | tf_op jit(solution)/shard_map/all_gather | solution.py:159
  618.1 16.0 pad_maximum_fusion
  724.7 276.6 %reduce-scatter.16.cloned.1.call-done = f32[512,128]{1,0:T(8,128)} async-done(((f32[512,256]{1,0:T(8,128)}), f32[512,128]{1,0:T(8,128)}) %reduce-scatter.16.cloned.1.call-update) | async-done | bytes 262160 | tf_op jit(solution)/shard_map/reduce_scatter | solution.py:239
  1013.9 45.2 %reduce-scatter.18.cloned.1.call-done = f32[256,1536]{1,0:T(8,128)} async-done(((f32[512,1536]{1,0:T(8,128)}), f32[256,1536]{1,0:T(8,128)}) %reduce-scatter.18.cloned.1.call-update) | async-done | bytes 1572880 | tf_op jit(solution)/shard_map/reduce_scatter | solution.py:248
  1070.3 17.3 collective-permute-done.2
  1099.0 16.4 all-gather.23.cloned.1.call-done
  1135.0 190.7 %conditional.30 = (f32[512,256]{1,0:T(8,128)}, f32[5,1536]{1,0:T(8,128)}, f32[3,24]{1,0:T(4,128)}, bf16[512,1536]{1,0:T(8,128)(2,1)}, bf16[512,1536]{1,0:T(8,128)(2,1)}, /*index=5*/bf16[512,24]{1,0:T(8,128)(2,1)}) conditional(s32[]{:T(128)} %convert_element_type.171, () %tuple.274, (f32[5,1536]{1,0:T(8,128)S(1)}, f32[512,3224]{1,0:T(8,128)}, ...), branch_computations={%region_80.82_spmd, %region_81.108_spmd} | conditional | flops 15220048896 | bytes 461547072 | solution.py:89
  1240.4 20.0 fusion.151
  1357.7 43.2 %reduce-scatter.22.cloned.1.call-done = f32[256,1536]{1,0:T(8,128)} async-done(((f32[512,1536]{1,0:T(8,128)}), f32[256,1536]{1,0:T(8,128)}) %reduce-scatter.22.cloned.1.call-update) | async-done | bytes 1572880 | tf_op jit(solution)/shard_map/reduce_scatter | solution.py:248
  1410.9 17.4 collective-permute-done.3
  1439.6 16.4 all-gather.25.cloned.1.call-done
  1475.4 191.8 %conditional.33 = (f32[512,256]{1,0:T(8,128)}, f32[5,1536]{1,0:T(8,128)}, f32[3,24]{1,0:T(4,128)}, bf16[512,1536]{1,0:T(8,128)(2,1)}, bf16[512,1536]{1,0:T(8,128)(2,1)}, /*index=5*/bf16[512,24]{1,0:T(8,128)(2,1)}) conditional(s32[]{:T(128)} %convert_element_type.178, () %tuple.280, (f32[5,1536]{1,0:T(8,128)S(1)}, f32[512,3224]{1,0:T(8,128)}, ...), branch_computations={%region_117.119_spmd, %region_118.145_spmd} | conditional | flops 15220048896 | bytes 396413248 | solution.py:89
  1581.7 19.8 fusion.218
  1709.4 30.5 %reduce-scatter.26.cloned.1.call-done = f32[256,1536]{1,0:T(8,128)} async-done(((f32[512,1536]{1,0:T(8,128)}), f32[256,1536]{1,0:T(8,128)}) %reduce-scatter.26.cloned.1.call-update) | async-done | bytes 1572880 | tf_op jit(solution)/shard_map/reduce_scatter | solution.py:248
  1759.9 34.1 %convolution_convert_fusion = bf16[1536,3224]{1,0:T(8,128)(2,1)} fusion(bf16[512,24]{1,0:T(8,128)(2,1)} %get-tuple-element.1373, bf16[512,128]{1,0:T(8,128)(2,1)S(1)} %fusion.366, bf16[512,1536]{1,0:T(8,128)(2,1)} %get-tuple-element.1372, bf16[512,1536]{1,0:T(8,128)(2,1)} %get-tuple-element.1371, bf16[512,24]{1,0:T(8,128)(2,1)} %get-tuple-element.1370, ...), kind=kOutput, calls=%fused_computation.583 | convolution fusion | flops 15350697984 | bytes 24526848 | tf_op jit(solution)/shard_map/dot_general | solution.py:93
  1807.4 71.8 %all-reduce.90.cloned.1.call-done = (f32[1,1536]{1,0:T(1,128)}, f32[5,3072]{1,0:T(8,128)}, f32[5,256]{1,0:T(8,128)}, f32[3,48]{1,0:T(4,128)}, f32[3072]{0:T(1024)}) async-done(((f32[1,1536]{1,0:T(1,128)}, f32[5,3072]{1,0:T(8,128)}, f32[5,256]{1,0:T(8,128)}, f32[3,48]{1,0:T(4,128)}, f32[3072]{0:T(1024)}), (f32[1,1536]{1,0:T(1,128)}, f32[5,3072]{1,0:T(8,128)}, f32[5,256]{1,0:T(8,128)}, f32[3,48]{1,0:T(4,128)}, ...) | async-done | bytes 85584 | tf_op jit(solution)/shard_map/psum | solution.py:304
  1884.6 53.7 %reduce-scatter.32.cloned.1.call-done = bf16[192,1536]{1,0:T(8,128)(2,1)} async-done(((bf16[1536,1536]{1,0:T(8,128)(2,1)}), bf16[192,1536]{1,0:T(8,128)(2,1)}) %reduce-scatter.32.cloned.1.call-update) | async-done | bytes 589840 | tf_op jit(solution)/shard_map/reduce_scatter | solution.py:280
  1940.5 105.6 %reduce-scatter.30.cloned.1.call-done = bf16[192,3224]{1,0:T(8,128)(2,1)} async-done(((bf16[1536,3224]{1,0:T(8,128)(2,1)}), bf16[192,3224]{1,0:T(8,128)(2,1)}) %reduce-scatter.30.cloned.1.call-update) | async-done | bytes 1238032 | tf_op jit(solution)/shard_map/reduce_scatter | solution.py:277
  (947 shorter events, 1013.9 us)
Async XLA Ops:
  7.2 63.0 %all-gather.29.cloned.1.call-start = ((), (), s32[]{:S(2)}) async-start(), calls=%async_computation.29 | async-start | bytes 5308416 | tf_op jit(solution)/shard_map/all_gather | solution.py:128
  8.0 114.4 %all-gather.27.cloned.1.call-start = ((), (), s32[]{:S(2)}) async-start(), calls=%async_computation.28 | async-start | bytes 5308416 | tf_op jit(solution)/shard_map/all_gather | solution.py:127
  8.7 141.9 %all-gather.15.cloned.1.call-start = ((), (), s32[]{:S(2)}) async-start(), calls=%async_computation.11 | async-start | bytes 2359296 | tf_op jit(solution)/shard_map/all_gather | solution.py:159
  16.8 237.9 %all-gather.31.cloned.1.call-start = ((), (), s32[]{:S(2)}) async-start(), calls=%async_computation.30 | async-start | bytes 5308416 | tf_op jit(solution)/shard_map/all_gather | solution.py:131
  17.3 286.6 %reduce-scatter.12.cloned.1.call-start = ((), (), s32[]{:S(2)}) async-start(), calls=%async_computation.12 | async-start | bytes 4718592 | tf_op jit(solution)/shard_map/reduce_scatter | solution.py:175
  17.6 647.2 %copy-start.181 = (f32[1,3,24]{2,1,0:T(4,128)}, f32[1,3,24]{2,1,0:T(4,128)S(1)}, u32[]{:S(2)}) copy-start(f32[1,3,24]{2,1,0:T(4,128)S(1)} %copy.771) | copy-start | bytes 868
  17.6 679.9 %copy-start.102 = (f32[1536]{0:T(1024)}, f32[1536]{0:T(1024)S(1)}, u32[]{:S(2)}) copy-start(f32[1536]{0:T(1024)S(1)} %reduce.55) | copy-start | bytes 18436
  51.6 604.3 %copy-start.182 = (f32[128]{0:T(128)}, f32[128]{0:T(128)S(1)}, u32[]{:S(2)}) copy-start(f32[128]{0:T(128)S(1)} %get-tuple-element.1769) | copy-start | bytes 1540
  51.6 604.3 %copy-start.183 = (f32[128]{0:T(128)}, f32[128]{0:T(128)S(1)}, u32[]{:S(2)}) copy-start(f32[128]{0:T(128)S(1)} %get-tuple-element.1770) | copy-start | bytes 1540
  51.6 604.3 %copy-start.184 = (f32[128]{0:T(128)}, f32[128]{0:T(128)S(1)}, u32[]{:S(2)}) copy-start(f32[128]{0:T(128)S(1)} %get-tuple-element.1771) | copy-start | bytes 1540
  51.6 604.3 %copy-start.185 = (f32[128]{0:T(128)}, f32[128]{0:T(128)S(1)}, u32[]{:S(2)}) copy-start(f32[128]{0:T(128)S(1)} %get-tuple-element.1772) | copy-start | bytes 1540
  51.6 604.3 %copy-start.213 = (f32[128]{0:T(128)}, f32[128]{0:T(128)S(1)}, u32[]{:S(2)}) copy-start(f32[128]{0:T(128)S(1)} %get-tuple-element.1768) | copy-start | bytes 1540
  261.3 117.2 %all-gather.17.cloned.1.call-start = ((), (), s32[]{:S(2)}) async-start(), calls=%async_computation.13 | async-start | bytes 2359296 | tf_op jit(solution)/shard_map/all_gather | solution.py:159
  308.0 37.3 %collective-permute-start = (f32[256,1536]{1,0:T(8,128)}, f32[256,1536]{1,0:T(8,128)}, u32[]{:S(2)}, u32[]{:S(2)}) collective-permute-start(f32[256,1536]{1,0:T(8,128)} %get-tuple-element.1642), channel_id=1, source_target_pairs={{0,16},{1,17},{2,18},{3,19},{4,20},{5,21},{6,22},{7,23},{8,24},{9,... | collective-permute-start | bytes 4718600 | tf_op jit(solution)/shard_map/ppermute | solution.py:20
  347.3 191.0 %reduce-scatter.14.cloned.1.call-start = ((), (), s32[]{:S(2)}) async-start(), calls=%async_computation.14 | async-start | bytes 4718592 | tf_op jit(solution)/shard_map/reduce_scatter | solution.py:175
  494.9 87.5 %all-gather.21.cloned.1.call-start = ((), (), s32[]{:S(2)}) async-start(), calls=%async_computation.16 | async-start | bytes 2359296 | tf_op jit(solution)/shard_map/all_gather | solution.py:219
  542.5 37.8 %collective-permute-start.1 = (f32[256,1536]{1,0:T(8,128)}, f32[256,1536]{1,0:T(8,128)}, u32[]{:S(2)}, u32[]{:S(2)}) collective-permute-start(f32[256,1536]{1,0:T(8,128)} %get-tuple-element.1640), channel_id=1, source_target_pairs={{0,16},{1,17},{2,18},{3,19},{4,20},{5,21},{6,22},{7,23},{8,24},{9,... | collective-permute-start | bytes 4718600 | tf_op jit(solution)/shard_map/ppermute | solution.py:20
  552.4 61.0 %all-gather.19.cloned.1.call-start = ((), (), s32[]{:S(2)}) async-start(), calls=%async_computation.15 | async-start | bytes 2359296 | tf_op jit(solution)/shard_map/all_gather | solution.py:159
  582.3 419.0 %reduce-scatter.16.cloned.1.call-start = ((), (), s32[]{:S(2)}) async-start(), calls=%async_computation.17 | async-start | bytes 786432 | tf_op jit(solution)/shard_map/reduce_scatter | solution.py:239
  723.7 335.4 %reduce-scatter.18.cloned.1.call-start = ((), (), s32[]{:S(2)}) async-start(), calls=%async_computation.18 | async-start | bytes 4718592 | tf_op jit(solution)/shard_map/reduce_scatter | solution.py:248
  1008.3 107.1 %all-gather.23.cloned.1.call-start = ((), (), s32[]{:S(2)}) async-start(), calls=%async_computation.19 | async-start | bytes 2359296 | tf_op jit(solution)/shard_map/all_gather | solution.py:219
  1066.5 21.2 %collective-permute-start.2 = (bf16[256,1536]{1,0:T(8,128)(2,1)S(1)}, bf16[256,1536]{1,0:T(8,128)(2,1)S(1)}, u32[]{:S(2)}, u32[]{:S(2)}) collective-permute-start(bf16[256,1536]{1,0:T(8,128)(2,1)S(1)} %get-tuple-element.1647), channel_id=1, source_target_pairs={{16,0},{17,1},{18,2},{19,3},{20,4},{21,5},{22,6},{23,7},{24,8},{25... | collective-permute-start | bytes 2359304 | tf_op jit(solution)/shard_map/ppermute | solution.py:20
  1088.9 251.5 %reduce-scatter.20.cloned.1.call-start = ((), (), s32[]{:S(2)}) async-start(), calls=%async_computation.20 | async-start | bytes 786432 | tf_op jit(solution)/shard_map/reduce_scatter | solution.py:239
  1325.7 75.2 %reduce-scatter.22.cloned.1.call-start = ((), (), s32[]{:S(2)}) async-start(), calls=%async_computation.21 | async-start | bytes 4718592 | tf_op jit(solution)/shard_map/reduce_scatter | solution.py:248
  1357.4 98.6 %all-gather.25.cloned.1.call-start = ((), (), s32[]{:S(2)}) async-start(), calls=%async_computation.22 | async-start | bytes 2359296 | tf_op jit(solution)/shard_map/all_gather | solution.py:219
  1407.1 21.2 %collective-permute-start.3 = (bf16[256,1536]{1,0:T(8,128)(2,1)S(1)}, bf16[256,1536]{1,0:T(8,128)(2,1)S(1)}, u32[]{:S(2)}, u32[]{:S(2)}) collective-permute-start(bf16[256,1536]{1,0:T(8,128)(2,1)S(1)} %get-tuple-element.1644), channel_id=1, source_target_pairs={{16,0},{17,1},{18,2},{19,3},{20,4},{21,5},{22,6},{23,7},{24,8},{25... | collective-permute-start | bytes 2359304 | tf_op jit(solution)/shard_map/ppermute | solution.py:20
  1429.5 251.5 %reduce-scatter.24.cloned.1.call-start = ((), (), s32[]{:S(2)}) async-start(), calls=%async_computation.23 | async-start | bytes 786432 | tf_op jit(solution)/shard_map/reduce_scatter | solution.py:239
  1667.2 72.8 %reduce-scatter.26.cloned.1.call-start = ((), (), s32[]{:S(2)}) async-start(), calls=%async_computation.24 | async-start | bytes 4718592 | tf_op jit(solution)/shard_map/reduce_scatter | solution.py:248
  1697.4 96.8 %reduce-scatter.28.cloned.1.call-start = ((), (), s32[]{:S(2)}) async-start(), calls=%async_computation.25 | async-start | bytes 4718592 | tf_op jit(solution)/shard_map/reduce_scatter | solution.py:175
  1699.6 179.6 %all-reduce.90.cloned.1.call-start = ((), (), s32[]{:S(2)}) async-start(), calls=%async_computation.31 | async-start | bytes 253952 | tf_op jit(solution)/shard_map/psum | solution.py:304
  1743.4 194.9 %reduce-scatter.32.cloned.1.call-start = ((), (), s32[]{:S(2)}) async-start(), calls=%async_computation.27 | async-start | bytes 5308416 | tf_op jit(solution)/shard_map/reduce_scatter | solution.py:280
  1754.9 291.2 %reduce-scatter.30.cloned.1.call-start = ((), (), s32[]{:S(2)}) async-start(), calls=%async_computation.26 | async-start | bytes 11501568 | tf_op jit(solution)/shard_map/reduce_scatter | solution.py:277
  (213 other events, 3176.3 us)
Sparse Core Ops, SparseCore 0:
  9.7 60.4 all-gather.28
  71.9 50.4 all-gather.26
  124.5 26.0 all-gather.14
  152.1 51.6 all-gather.30
  261.5 42.4 reduce-scatter.11
  347.5 31.0 all-gather.16
  495.0 43.3 reduce-scatter.13
  552.6 26.2 all-gather.20
  582.4 31.0 all-gather.18
  723.8 277.4 reduce-scatter.15
  1008.4 50.6 reduce-scatter.17
  1089.0 26.2 all-gather.22
  1325.8 14.5 reduce-scatter.19
  1357.5 43.3 reduce-scatter.21
  1429.7 26.2 all-gather.24
  1667.3 13.6 reduce-scatter.23
  1697.5 42.4 reduce-scatter.25
  1742.1 43.3 reduce-scatter.27
  1791.2 87.9 all-reduce.89
  1881.5 56.8 reduce-scatter.31
  1940.7 105.2 reduce-scatter.29
where the time goes:
time: 2070 us; the launch traced here: 2060 us
  waiting for transfers between devices  1010 us (49%)
  matrix products  326 us (16%)
  other arithmetic  296 us (14%)
  local copies, waits for them, and re-layouts  277 us (13%)
  blocking collectives  91.9 us (4%)
  between operations  27.7 us (1%)
    reduce_scatter x3, waiting for transfers between devices, local(): lax.psum_scatter(grad_shared, 'tensor', scatter_dimension=1, tiled=True)  303 us
    reduce_scatter x3, waiting for transfers between devices, local(): lax.psum_scatter(back_rows(jnp.int32(0), half_rows * lax.axis_size('tenso...  119 us
    dot_general x8, matrix products, state_space(): jnp.einsum('bhij,bjhp->bihp', mixing, weighted, precision=highest)  119 us
    reduce_scatter x1, waiting for transfers between devices, local(): lax.psum_scatter(acc_in.astype(jnp.bfloat16), 'dp', scatter_dimension=0,...  106 us
    ppermute x4, waiting for transfers between devices, passed_along(): return lax.ppermute(array, axis, pairs)  91.4 us
    reduce_scatter x3, waiting for transfers between devices, local(): lax.psum_scatter(out_rows(jnp.int32(0), half_rows * lax.axis_size('tensor...  86 us
    psum x1, waiting for transfers between devices, local(): lax.psum((acc_norm, widen(acc_value, 1), widen(acc_shared, 1), widen(acc_...  71.8 us
    all_gather x3, waiting for transfers between devices, local(): gathered = lax.all_gather(normed, 'tensor', axis=0, tiled=True)  71.4 us
  transfers between devices with their start and end apart: 25, of which 22 were waited for; matrix products, arithmetic and copies ran while one was open for 11% of the time, Pallas kernels for 0%

commit v1 on v0

v1 whole, which is shorter than its diff:
```python
import jax
import jax.numpy as jnp
from jax import lax
from jax.experimental import pallas as pl
from jax.experimental.pallas import tpu as pltpu
from jax.sharding import PartitionSpec as P

DI = 3072
P_SIZE = 64
N = 128
T = 128
LANES = 128
HP = 16
eps = 1e-05
bf16 = jnp.bfloat16
f32 = jnp.float32


def dot_nn(a, b):
    return lax.dot_general(a, b, (((1,), (0,)), ((), ())), preferred_element_type=f32)


def dot_nt(a, b):
    return lax.dot_general(a, b, (((1,), (1,)), ((), ())), preferred_element_type=f32)


def dot_tn(a, b):
    return lax.dot_general(a, b, (((0,), (0,)), ((), ())), preferred_element_type=f32)


def sigmoid(v):
    return 0.5 + 0.5 * jnp.tanh(0.5 * v)


def shifted(cat):
    return (
        pltpu.roll(cat, 3, 0)[8:],
        pltpu.roll(cat, 2, 0)[8:],
        pltpu.roll(cat, 1, 0)[8:],
        cat[8:],
    )


def conv(parts, taps):
    total = taps[4:5]
    for j in range(4):
        total = total + taps[j : j + 1] * parts[j]
    return total


def conv_back(ds, after, taps):
    cat = jnp.concatenate([ds, after], axis=0)
    rows = cat.shape[0]
    total = taps[3:4] * ds
    for j in range(3):
        total = total + taps[j : j + 1] * pltpu.roll(cat, rows - (3 - j), 0)[: ds.shape[0]]
    return total


def lane_ids(shape):
    return lax.broadcasted_iota(jnp.int32, shape, len(shape) - 1)


def running_sum(v, lane):
    step = 1
    while step < LANES:
        v = v + jnp.where(lane >= step, pltpu.roll(v, step, 1), 0.0)
        step *= 2
    return v


def running_sum_back(v, lane):
    step = 1
    while step < LANES:
        v = v + jnp.where(lane < LANES - step, pltpu.roll(v, LANES - step, 1), 0.0)
        step *= 2
    return v


def step_rows(pre_dt, heads):
    logits = jnp.transpose(pre_dt)[:HP] + heads[:, 0:1]
    small = jnp.exp(-jnp.abs(logits))
    log_part = jnp.where(small < 1e-3, small * (1.0 - small * (0.5 - small / 3.0)), jnp.log(1.0 + small))
    steps = jnp.maximum(logits, 0.0) + log_part
    run = running_sum(steps * heads[:, 1:2], lane_ids((HP, T)))
    return logits, steps, run


def columns(rows):
    have = rows.shape[0]
    return jnp.transpose(jnp.concatenate([rows, jnp.zeros((LANES - have, T), f32)], axis=0))


def fwd_kernel(order, pz, px, halo, taps_x, taps_bc, heads, skip, gain, og_ref, y_ref, s_ref, sq_ref, state):
    k = pl.program_id(1)
    width = pz.shape[1]
    pairs = width // LANES
    bc_at, dt_at = width, width + 2 * N

    @pl.when(k == 0)
    def _():
        state[...] = jnp.zeros_like(state)

    keep = jnp.where(k > 0, 1.0, 0.0)
    lane = lane_ids((T, LANES))
    low = lane < P_SIZE
    row = lax.broadcasted_iota(jnp.int32, (T, T), 0)
    seen = row >= lane
    logits, steps, run = step_rows(px[:, dt_at : dt_at + LANES], heads[...])
    tail = jnp.exp(run[:, T - 1 : T] - run) * steps
    cols = columns(jnp.concatenate([run, tail], axis=0))
    bc_cat = jnp.concatenate([halo[:, bc_at : bc_at + 2 * N] * keep, px[:, bc_at : bc_at + 2 * N]], axis=0)
    s_bc = conv(shifted(bc_cat), taps_bc[...])
    bc = s_bc * sigmoid(s_bc)
    keys = bc[:, :N]
    keys_t = jnp.transpose(keys).astype(bf16)
    reads = bc[:, N:].astype(bf16)
    scores = jnp.where(seen, dot_nt(reads, keys.astype(bf16)), 0.0)
    squares = jnp.zeros((T, LANES), f32)
    for p in range(pairs):
        at = slice(p * LANES, (p + 1) * LANES)
        x_cat = jnp.concatenate([halo[:, at] * keep, px[:, at]], axis=0)
        s_x = conv(shifted(x_cat), taps_x[:, at])
        xs = s_x * sigmoid(s_x)
        xr = xs.astype(bf16)
        mixes = []
        wide = []
        for h in (2 * p, 2 * p + 1):
            ci = jnp.broadcast_to(cols[:, h : h + 1], (T, T))
            decay = jnp.exp(jnp.minimum(ci - run[h : h + 1], 0.0))
            mixes.append((decay * steps[h : h + 1] * scores).astype(bf16))
            wide.append(ci)
        c_pair = jnp.where(low, wide[0], wide[1])
        w_pair = jnp.where(low, cols[:, HP + 2 * p : HP + 2 * p + 1], cols[:, HP + 2 * p + 1 : HP + 2 * p + 2])
        e_pair = jnp.exp(c_pair)
        zero = jnp.zeros_like(xr)
        y = dot_nn(
            jnp.concatenate(mixes, axis=1),
            jnp.concatenate([jnp.where(low, xr, zero), jnp.where(low, zero, xr)], axis=0),
        )
        entering = state[:, at]
        entering_r = entering.astype(bf16)
        s_ref[0, :, at] = entering_r
        y = y + e_pair * dot_nn(reads, entering_r)
        state[:, at] = e_pair[T - 1 : T] * entering + dot_nn(keys_t, (xs * w_pair).astype(bf16))
        y_ref[:, at] = y
        z = pz[:, at]
        g = (y + skip[:, at] * xs) * (z * sigmoid(z))
        squares = squares + g * g
        og_ref[:, at] = (g * gain[:, at]).astype(bf16)
    sq_ref[0] = jnp.broadcast_to(jnp.sum(jnp.transpose(squares), axis=0, keepdims=True), (8, T))


def bwd_kernel(
    order, pz, px, halo, y_ref, s_ref, d_ref, stats, taps_x, taps_bc, heads, skip, gain, sums,
    dz_ref, dx_ref, acc_x, acc_bc, acc_dt, back, after_x, after_bc, d_scores,
):
    s_id, k = pl.program_id(0), pl.program_id(1)
    width = pz.shape[1]
    pairs = width // LANES
    bc_at, dt_at = width, width + 2 * N

    @pl.when(k == 0)
    def _():
        back[...] = jnp.zeros_like(back)
        after_x[...] = jnp.zeros_like(after_x)
        after_bc[...] = jnp.zeros_like(after_bc)

    @pl.when((k == 0) & (s_id == 0))
    def _():
        acc_x[...] = jnp.zeros_like(acc_x)
        acc_bc[...] = jnp.zeros_like(acc_bc)
        acc_dt[...] = jnp.zeros_like(acc_dt)

    keep = jnp.where(k < 3, 1.0, 0.0)
    lane = lane_ids((T, LANES))
    low = lane < P_SIZE
    row = lax.broadcasted_iota(jnp.int32, (T, T), 0)
    seen_t = lane >= row
    last = row == T - 1
    head_cols = heads[...]
    logits, steps, run = step_rows(px[:, dt_at : dt_at + LANES], head_cols)
    tail = jnp.exp(run[:, T - 1 : T] - run) * steps
    cols = columns(jnp.concatenate([run, steps, tail], axis=0))
    bc_cat = jnp.concatenate([halo[:, bc_at : bc_at + 2 * N] * keep, px[:, bc_at : bc_at + 2 * N]], axis=0)
    bc_parts = shifted(bc_cat)
    s_bc = conv(bc_parts, taps_bc[...])
    sig_bc = sigmoid(s_bc)
    bc = s_bc * sig_bc
    keys, reads = bc[:, :N].astype(bf16), bc[:, N:].astype(bf16)
    reads_t = jnp.transpose(bc[:, N:]).astype(bf16)
    scores_t = jnp.where(seen_t, dot_nt(keys, reads), 0.0)
    d_scores[...] = jnp.zeros_like(d_scores)
    d_reads = jnp.zeros((T, N), f32)
    d_keys = jnp.zeros((T, N), f32)
    head_sums = jnp.zeros((T, LANES), f32)
    row_scale = stats[:, 0:1]
    row_stat = stats[:, 1:2]
    for p in range(pairs):
        at = slice(p * LANES, (p + 1) * LANES)
        x_cat = jnp.concatenate([halo[:, at] * keep, px[:, at]], axis=0)
        x_parts = shifted(x_cat)
        s_x = conv(x_parts, taps_x[:, at])
        sig_x = sigmoid(s_x)
        xs = s_x * sig_x
        xr = xs.astype(bf16)
        z = pz[:, at]
        sig_z = sigmoid(z)
        silu_z = z * sig_z
        y = y_ref[:, at]
        y_all = y + skip[:, at] * xs
        g = y_all * silu_z
        dr = d_ref[:, at] * row_scale
        dg = gain[:, at] * dr - g * row_stat
        acc_x[5:6, at] += jnp.sum(dr * g, axis=0, keepdims=True)
        dz_ref[:, at] = (dg * y_all * (sig_z + silu_z * (1.0 - sig_z))).astype(bf16)
        dy = dg * silu_z
        dyr = dy.astype(bf16)
        acc_x[6:7, at] += jnp.sum(dy * xs, axis=0, keepdims=True)
        zero = jnp.zeros_like(xr)
        mixes_t = []
        wide = []
        total = d_scores[...]
        for i, h in enumerate((2 * p, 2 * p + 1)):
            cj = jnp.broadcast_to(cols[:, h : h + 1], (T, T))
            decay = jnp.exp(jnp.minimum(run[h : h + 1] - cj, 0.0)) * cols[:, HP + h : HP + h + 1]
            mixes_t.append((decay * scores_t).astype(bf16))
            x_one = jnp.where(low, xr, zero) if i == 0 else jnp.where(low, zero, xr)
            total = total + decay * dot_nt(x_one, dyr)
            wide.append(cj)
        d_scores[...] = total
        c_pair = jnp.where(low, wide[0], wide[1])
        at_w = 2 * HP + 2 * p
        w_pair = jnp.where(low, cols[:, at_w : at_w + 1], cols[:, at_w + 1 : at_w + 2])
        e_pair = jnp.exp(c_pair)
        dx_in = dot_nn(
            jnp.concatenate(mixes_t, axis=1),
            jnp.concatenate([jnp.where(low, dyr, zero), jnp.where(low, zero, dyr)], axis=0),
        )
        returning = back[:, at]
        returning_r = returning.astype(bf16)
        entering_r = s_ref[0, :, at]
        dx_out = w_pair * dot_nn(keys, returning_r)
        dye = (dy * e_pair).astype(bf16)
        d_reads = d_reads + dot_nt(dye, entering_r)
        d_keys = d_keys + dot_nt((xs * w_pair).astype(bf16), returning_r)
        e_last = e_pair[T - 1 : T]
        back[:, at] = e_last * returning + dot_nn(reads_t, dye)
        across = e_last * jnp.sum(returning * entering_r.astype(f32), axis=0, keepdims=True)
        xf, dyf = xr.astype(f32), dyr.astype(f32)
        one = dyf * y - xf * dx_in + jnp.where(last, across, 0.0)
        for i, part in enumerate((one, xf * dx_in, xf * dx_out)):
            high = part.astype(bf16)
            rest = (part - high.astype(f32)).astype(bf16)
            place = sums[(3 * p + i) * LANES : (3 * p + i + 1) * LANES]
            head_sums = head_sums + dot_nn(
                jnp.concatenate([high, rest], axis=1), jnp.concatenate([place, place], axis=0)
            )
        dxs = dx_in + dx_out + skip[:, at] * dy
        ds = dxs * (sig_x + xs * (1.0 - sig_x))
        for j in range(4):
            acc_x[j : j + 1, at] += jnp.sum(ds * x_parts[j], axis=0, keepdims=True)
        acc_x[4:5, at] += jnp.sum(ds, axis=0, keepdims=True)
        dx_ref[:, at] = conv_back(ds, after_x[:, at], taps_x[:, at]).astype(bf16)
        after_x[:, at] = ds[:8]
    rows = jnp.transpose(head_sums)
    one, two, three = rows[:HP], rows[HP : 2 * HP], rows[2 * HP : 3 * HP]
    lane_h = lane_ids((HP, T))
    d_decay = running_sum_back(one, lane_h) + running_sum(three, lane_h) - three
    sig_dt = sigmoid(logits)
    exact = jnp.exp(jnp.minimum(logits, 0.0)) / (1.0 + jnp.exp(-jnp.abs(logits)))
    ratio = jnp.where(logits < -15.0, 1.0, exact / jnp.maximum(steps, 1e-30))
    d_pre = (two + three) * ratio + head_cols[:, 1:2] * d_decay * sig_dt
    acc_dt[0:HP] += steps * d_decay
    acc_dt[HP : 2 * HP] += d_pre
    dx_ref[:, dt_at : dt_at + LANES] = columns(d_pre).astype(bf16)
    ds_t = jnp.where(seen_t, d_scores[...], 0.0)
    d_keys = d_keys + dot_nn(ds_t.astype(bf16), reads)
    d_reads = d_reads + dot_nn(jnp.transpose(ds_t).astype(bf16), keys)
    ds_bc = jnp.concatenate([d_keys, d_reads], axis=1) * (sig_bc + bc * (1.0 - sig_bc))
    for j in range(4):
        acc_bc[j : j + 1] += jnp.sum(ds_bc * bc_parts[j], axis=0, keepdims=True)
    acc_bc[4:5] += jnp.sum(ds_bc, axis=0, keepdims=True)
    dx_ref[:, bc_at : bc_at + 2 * N] = conv_back(ds_bc, after_bc[...], taps_bc[...]).astype(bf16)
    after_bc[...] = ds_bc[:8]


def whole_spec(array):
    return pl.BlockSpec(array.shape, lambda s, k, order: (0,) * array.ndim)


def scan_forward(order, pz, px, layer):
    rows, width = pz.shape
    steps = rows // T
    here = lambda s, k, order: (order[s * 4 + k], 0)
    before = lambda s, k, order: (order[s * 4 + jnp.maximum(k - 1, 0)] * (T // 8) + (T // 8 - 1), 0)
    small = (layer["taps_x"], layer["taps_bc"], layer["heads"], layer["skip"], layer["gain"])
    return pl.pallas_call(
        fwd_kernel,
        grid_spec=pltpu.PrefetchScalarGridSpec(
            num_scalar_prefetch=1,
            grid=(steps // 4, 4),
            in_specs=[
                pl.BlockSpec((T, width), here),
                pl.BlockSpec((T, px.shape[1]), here),
                pl.BlockSpec((8, px.shape[1]), before),
            ]
            + [whole_spec(m) for m in small],
            out_specs=[
                pl.BlockSpec((T, width), here),
                pl.BlockSpec((T, width), here),
                pl.BlockSpec((1, N, width), lambda s, k, order: (s * 4 + k, 0, 0)),
                pl.BlockSpec((1, 8, T), lambda s, k, order: (order[s * 4 + k], 0, 0)),
            ],
            scratch_shapes=[pltpu.VMEM((N, width), f32)],
        ),
        out_shape=[
            jax.ShapeDtypeStruct((rows, width), bf16),
            jax.ShapeDtypeStruct((rows, width), f32),
            jax.ShapeDtypeStruct((steps, N, width), bf16),
            jax.ShapeDtypeStruct((steps, 8, T), f32),
        ],
        compiler_params=pltpu.CompilerParams(vmem_limit_bytes=40 * 2**20),
        cost_estimate=pl.CostEstimate(flops=4 * 10**9, bytes_accessed=14 * 2**20, transcendentals=5 * 10**6),
        name="scan_forward",
    )(order, pz, px, px, *small)


def scan_backward(order, pz, px, y, states, d_out, stats, layer, sums):
    rows, width = pz.shape
    steps = rows // T
    here = lambda s, k, order: (order[s * 4 + 3 - k], 0)
    before = lambda s, k, order: (order[s * 4 + jnp.maximum(2 - k, 0)] * (T // 8) + (T // 8 - 1), 0)
    small = (layer["taps_x"], layer["taps_bc"], layer["heads"], layer["skip"], layer["gain"], sums)
    fixed = lambda s, k, order: (0, 0)
    return pl.pallas_call(
        bwd_kernel,
        grid_spec=pltpu.PrefetchScalarGridSpec(
            num_scalar_prefetch=1,
            grid=(steps // 4, 4),
            in_specs=[
                pl.BlockSpec((T, width), here),
                pl.BlockSpec((T, px.shape[1]), here),
                pl.BlockSpec((8, px.shape[1]), before),
                pl.BlockSpec((T, width), here),
                pl.BlockSpec((1, N, width), lambda s, k, order: (s * 4 + 3 - k, 0, 0)),
                pl.BlockSpec((T, width), here),
                pl.BlockSpec((T, stats.shape[1]), here),
            ]
            + [whole_spec(m) for m in small],
            out_specs=[
                pl.BlockSpec((T, width), here),
                pl.BlockSpec((T, px.shape[1]), here),
                pl.BlockSpec((8, width), fixed),
                pl.BlockSpec((8, 2 * N), fixed),
                pl.BlockSpec((2 * HP, T), fixed),
            ],
            scratch_shapes=[
                pltpu.VMEM((N, width), f32),
                pltpu.VMEM((8, width), f32),
                pltpu.VMEM((8, 2 * N), f32),
                pltpu.VMEM((T, T), f32),
            ],
        ),
        out_shape=[
            jax.ShapeDtypeStruct((rows, width), bf16),
            jax.ShapeDtypeStruct((rows, px.shape[1]), bf16),
            jax.ShapeDtypeStruct((8, width), f32),
            jax.ShapeDtypeStruct((8, 2 * N), f32),
            jax.ShapeDtypeStruct((2 * HP, T), f32),
        ],
        compiler_params=pltpu.CompilerParams(vmem_limit_bytes=40 * 2**20),
        cost_estimate=pl.CostEstimate(flops=8 * 10**9, bytes_accessed=24 * 2**20, transcendentals=10**7),
        name="scan_backward",
    )(order, pz, px, px, y, states, d_out, stats, *small)


def swap(value, axis):
    return lax.ppermute(value, axis, [(0, 1), (1, 0)])


AXES = (("section", "tensor"), ("tensor", "section"))


def spread(own, first, second):
    two = jnp.concatenate([own, swap(own, first)], axis=0)
    return jnp.concatenate([two, swap(two, second)], axis=0)


def spread_all(owns):
    return jnp.concatenate([spread(own, *axes) for own, axes in zip(owns, AXES)], axis=0)


def collect(parts, first, second):
    half = parts.shape[0] // 2
    two = parts[:half].astype(f32) + swap(parts[half:], second).astype(f32)
    quarter = half // 2
    return two[:quarter] + swap(two[quarter:].astype(parts.dtype), first).astype(f32)


def local(
    block_input,
    plan,
    lengths,
    norm_gain,
    gate_proj,
    value_proj,
    shared_proj,
    step_proj,
    conv_value,
    conv_shared,
    head_params,
    gate_gain,
    out_proj,
    cotangent,
):
    x = lax.axis_index("section")
    yy = lax.axis_index("tensor")
    streams = block_input.shape[1]
    model_width = block_input.shape[3]
    width = gate_proj.shape[2] // 2
    head_count = step_proj.shape[2] // 2
    rows_here = gate_proj.shape[1]

    def both(value):
        other = swap(value, "section")
        return jnp.where(x == 0, value, other), jnp.where(x == 0, other, value)

    def quarters(value):
        size = value.shape[-1] // 2
        axis = value.ndim - 1
        kept = lax.dynamic_slice_in_dim(value, x * size, size, axis)
        other = swap(lax.dynamic_slice_in_dim(value, (1 - x) * size, size, axis), "section")
        return jnp.where(x == 0, kept, other), jnp.where(x == 0, other, kept)

    shared_other = swap(shared_proj[0], "tensor")
    shared_full = jnp.where(
        yy == 0,
        jnp.concatenate([shared_proj[0], shared_other], axis=1),
        jnp.concatenate([shared_other, shared_proj[0]], axis=1),
    )
    step_padded = jnp.pad(
        step_proj[0].reshape(rows_here, 2, head_count), ((0, 0), (0, 0), (0, LANES - head_count))
    ).reshape(rows_here, 2 * LANES)
    value_two = quarters(value_proj[0])
    shared_two = both(shared_full)
    step_two = quarters(step_padded)
    gate_two = quarters(gate_proj[0])
    out_two = quarters(out_proj[0])
    weights = []
    for l in range(2):
        packed = jnp.concatenate([value_two[l], shared_two[l], step_two[l]], axis=1)
        weights.append(
            (
                lax.all_gather(packed, "dp", axis=0, tiled=True),
                lax.all_gather(gate_two[l], "dp", axis=0, tiled=True),
                lax.all_gather(out_two[l], "dp", axis=0, tiled=True),
            )
        )

    taps_x_two = quarters(jnp.pad(conv_value[0], ((0, 3), (0, 0))))
    shared_taps_other = swap(conv_shared[0], "tensor")
    taps_bc_full = jnp.where(
        yy == 0,
        jnp.concatenate([conv_shared[0], shared_taps_other], axis=1),
        jnp.concatenate([shared_taps_other, conv_shared[0]], axis=1),
    )
    taps_bc_two = both(jnp.pad(taps_bc_full, ((0, 3), (0, 0))))
    heads_two = quarters(head_params[0])
    gain_two = quarters(gate_gain)
    norm_two = both(norm_gain)
    layers = []
    for l in range(2):
        head_rows = heads_two[l]
        columns_of = jnp.stack([head_rows[0], -jnp.exp(head_rows[1])], axis=1)
        layers.append(
            dict(
                taps_x=taps_x_two[l],
                taps_bc=taps_bc_two[l],
                heads=jnp.pad(columns_of, ((0, HP - head_count), (0, LANES - 2))),
                skip=jnp.repeat(head_rows[2], P_SIZE)[None],
                gain=gain_two[l],
                norm=norm_two[l],
                decay=columns_of[:, 1],
            )
        )
    feature = lax.broadcasted_iota(jnp.int32, (3 * width, LANES), 0)
    target = lax.broadcasted_iota(jnp.int32, (3 * width, LANES), 1)
    pair, part, within = feature // (3 * LANES), (feature // LANES) % 3, feature % LANES
    sums = (target == part * HP + 2 * pair + within // P_SIZE).astype(bf16)

    chunk = jnp.arange(4, dtype=jnp.int32)
    x_bit, y_bit = (chunk & 1) ^ x, (chunk >> 1) ^ yy
    order = jnp.concatenate([2 * y_bit + x_bit, 4 + 2 * x_bit + y_bit]).astype(jnp.int32)

    def own_rows(value):
        half = value.shape[1] // 2
        return lax.dynamic_slice_in_dim(value, x * half, half, 1)

    first_rows = (2 * yy + x) * T
    positions = first_rows + lax.broadcasted_iota(jnp.int32, (T, 1), 0)
    valid = jnp.sum(jnp.where(plan[0][:, None] == jnp.arange(streams)[None, :], lengths[0][:, None], 0), axis=0)
    keep = (positions[None] < valid[:, None, None]).astype(f32)
    u = own_rows(block_input[0]).astype(f32)
    top = own_rows(cotangent[0]).astype(f32) * keep

    saved = []
    for l in range(2):
        w_in, w_gate, w_out = weights[l]
        layer = layers[l]
        rho = lax.rsqrt(jnp.mean(u * u, axis=2, keepdims=True) + eps)
        a_own = (u * rho * layer["norm"][None]).astype(bf16)
        a = spread_all([a_own[s] for s in range(streams)])
        px = dot_nn(a, w_in)
        pz = dot_nn(a, w_gate)
        og, y, states, squares = scan_forward(order, pz, px, layer)
        o_part = dot_nt(og, w_out).astype(bf16)
        sq = squares[:, 0, :].reshape(streams, 4 * T)
        size = 4 * T
        o = jnp.stack([collect(o_part[s * size : (s + 1) * size], *AXES[s]) for s in range(streams)])
        total = jnp.stack([collect(sq[s], *AXES[s]) for s in range(streams)])[:, :, None]
        r = lax.rsqrt(total / DI + eps)
        o = o * r
        saved.append((u, rho, a, pz, px, og, y, states, r, o))
        u = u + o
    final = u

    dv = top
    shards = [None, None]
    small_sums = [None, None]
    for l in (1, 0):
        w_in, w_gate, w_out = weights[l]
        layer = layers[l]
        u, rho, a, pz, px, og, y, states, r, o = saved[l]
        do_own = (dv * r).astype(bf16)
        kappa = r * r * jnp.sum(dv.astype(bf16).astype(f32) * o, axis=2, keepdims=True) / DI
        do = spread_all([do_own[s] for s in range(streams)])
        stat = spread_all([kappa[s, :, 0] for s in range(streams)])
        stats = jnp.stack([jnp.ones_like(stat), stat], axis=1)
        d_out = dot_nn(do, w_out)
        dz, dx, acc_x, acc_bc, acc_dt = scan_backward(order, pz, px, y, states, d_out, stats, layer, sums)
        da_part = (dot_nt(dz, w_gate) + dot_nt(dx, w_in)).astype(bf16)
        size = 4 * T
        da = jnp.stack([collect(da_part[s * size : (s + 1) * size], *AXES[s]) for s in range(streams)])
        grad_out = dot_tn(do, og).astype(bf16)
        grad_gate = dot_tn(a, dz).astype(bf16)
        grad_in = dot_tn(a, dx).astype(bf16)
        shards[l] = tuple(
            lax.psum_scatter(g, "dp", scatter_dimension=0, tiled=True) for g in (grad_out, grad_gate, grad_in)
        )
        scaled = da * layer["norm"][None]
        du = dv + rho * scaled - u * rho**3 * jnp.mean(scaled * u, axis=2, keepdims=True)
        grad_norm = jnp.sum(da * u * rho, axis=(0, 1))
        small_sums[l] = jnp.concatenate(
            [
                acc_x.reshape(-1),
                acc_bc.reshape(-1),
                jnp.sum(acc_dt, axis=1),
                grad_norm,
            ]
        )
        dv = du

    packed = jnp.stack(small_sums)
    packed = jnp.sum(lax.all_gather(packed, "dp", axis=0), axis=0)
    everyone = lax.all_gather(packed, ("section", "tensor"), axis=0)
    mine = lax.dynamic_index_in_dim(everyone, x, 1, keepdims=False)
    end_x, end_bc = 8 * width, 8 * width + 8 * 2 * N
    end_dt = end_bc + 2 * HP
    over_all = jnp.sum(mine, axis=0)
    halves = lax.dynamic_index_in_dim(mine.reshape(2, 2, -1), yy, 1, keepdims=False)
    by_x = halves[:, :end_x].reshape(2, 8, width).transpose(1, 0, 2).reshape(8, 2 * width)
    by_dt = halves[:, end_bc:end_dt].reshape(2, 2, HP)[:, :, :head_count].transpose(1, 0, 2).reshape(2, 2 * head_count)
    grad_conv_value = by_x[:5]
    grad_gate_gain = by_x[5]
    grad_skip = jnp.sum(by_x[6].reshape(2 * head_count, P_SIZE), axis=1)
    grad_heads = jnp.stack([by_dt[1], by_dt[0] * -jnp.exp(head_params[0, 1]), grad_skip])
    bc_all = over_all[end_x:end_bc].reshape(8, 2 * N)[:5]
    grad_conv_shared = lax.dynamic_slice_in_dim(bc_all, yy * N, N, 1)
    grad_norm = over_all[end_dt:]

    def home(per_layer):
        kept = jnp.where(x == 0, per_layer[0], per_layer[1])
        other = swap(jnp.where(x == 0, per_layer[1], per_layer[0]), "section")
        return jnp.concatenate(
            [jnp.where(x == 0, kept, other), jnp.where(x == 0, other, kept)], axis=1
        ).astype(f32)

    grad_out = home([shards[l][0] for l in range(2)])
    grad_gate = home([shards[l][1] for l in range(2)])
    grad_value = home([shards[l][2][:, :width] for l in range(2)])
    at_dt = width + 2 * N
    grad_step = home([shards[l][2][:, at_dt : at_dt + head_count] for l in range(2)])
    shared_sums = jnp.stack([shards[l][2][:, width:at_dt].astype(f32) for l in range(2)])
    shared_sums = lax.psum(shared_sums, ("section", "tensor"))
    grad_shared = lax.dynamic_slice_in_dim(
        lax.dynamic_index_in_dim(shared_sums, x, 0, keepdims=False), yy * N, N, 1
    )

    mine = jnp.where(x == 0, dv, final)
    other = swap(jnp.where(x == 0, final, dv).astype(bf16), "section").astype(f32)
    relay = jnp.concatenate([jnp.where(x == 0, mine, other), jnp.where(x == 0, other, mine)], axis=1)
    return (
        relay[None, None],
        grad_norm[None],
        grad_gate[None],
        grad_value[None],
        grad_shared[None],
        grad_step[None],
        grad_conv_value[None],
        grad_conv_shared[None],
        grad_heads[None],
        grad_gate_gain[None],
        grad_out[None],
    )


def solution(mesh):
    placed = (
        P("dp", None, "tensor", None),
        P("dp", None),
        P("dp", None),
        P("section", None),
        P("section", "dp", "tensor"),
        P("section", "dp", "tensor"),
        P("section", "dp", "tensor"),
        P("section", "dp", "tensor"),
        P("section", None, "tensor"),
        P("section", None, "tensor"),
        P("section", None, "tensor"),
        P("section", "tensor"),
        P("section", "dp", "tensor"),
        P("dp", None, "tensor", None),
    )
    return jax.shard_map(
        local,
        mesh=mesh,
        in_specs=placed,
        out_specs=(
            P("section", "dp", None, "tensor", None),
            P("section", None),
            P("section", "dp", "tensor"),
            P("section", "dp", "tensor"),
            P("section", "dp", "tensor"),
            P("section", "dp", "tensor"),
            P("section", None, "tensor"),
            P("section", None, "tensor"),
            P("section", None, "tensor"),
            P("section", "tensor"),
            P("section", "dp", "tensor"),
        ),
        check_vma=False,
    )
```

time: 2070 us -> 743 us (0.36)
  waiting for transfers between devices: 1010 us -> 298 us
  other arithmetic: 296 us -> 55.6 us
  matrix products: 326 us -> 105 us
  local copies, waits for them, and re-layouts: 277 us -> 70.9 us
  Pallas kernels: 0 us -> 95.3 us
  blocking collectives: 91.9 us -> 26.7 us
  starting transfers between devices: 13.4 us -> 71 us
    reduce_scatter x11 -> x6, waiting for transfers between devices: 667 us -> 66.3 us  [local(): lax.psum_scatter(g, 'dp', scatter_dimension=0, tiled=True)]
    dot_general x42 -> x18, matrix products: 326 us -> 105 us  [the longest x6 41.5 us: dot_nn(): lax.dot_general(a, b, (((1,), (0,)), ((), ())), preferred_element_type=f32)]
    all_gather x9 -> x6, waiting for transfers between devices: 175 us -> 9.59 us  [the longest x2 4.97 us: local(): lax.all_gather(packed, 'dp', axis=0, tiled=True)]
    pallas_call x0 -> x4, Pallas kernels: none -> 95.3 us  [the longest x2 65.8 us: scan_backward(): pl.pallas_call(bwd_kernel, grid_spec=pltpu.PrefetchScalarGridSpec(num_sca...]
    ppermute x4 -> x65, waiting for transfers between devices: 91.4 us -> 185 us  [swap(): return lax.ppermute(value, axis, [(0, 1), (1, 0)])]
    reduce_sum x31 -> x11, other arithmetic: 84 us -> 4.65 us  [the longest x1 1.31 us: local(): packed = jnp.sum(lax.all_gather(packed, 'dp', axis=0), axis=0)]
    mul x26 -> x1, other arithmetic: 65.2 us -> 0.67 us  [local(): by_dt[0] * -jnp.exp(head_params[0, 1])]
    another operation x39 -> x15, other arithmetic: 62.9 us -> 4.8 us  [the longest x4 2.51 us: local(): jnp.stack([collect(da_part[s * size:(s + 1) * size], *AXES[s]) for s in r...]
  transfers between devices with their start and end apart: 25 -> 78, of which waited for: 22 -> 37; matrix products, arithmetic and copies ran while one was open for 11% -> 24% of each run, Pallas kernels for 0% -> 8%
where the time goes in v1:
time: 743 us; the launch traced here: 738 us
  waiting for transfers between devices  298 us (40%)
  matrix products  105 us (14%)
  Pallas kernels  95.3 us (13%)
  starting transfers between devices  71 us (10%)
  local copies, waits for them, and re-layouts  70.9 us (10%)
  other arithmetic  55.6 us (7%)
  blocking collectives  26.7 us (4%)
  between operations  15.7 us (2%)
    ppermute x65, waiting for transfers between devices, swap(): return lax.ppermute(value, axis, [(0, 1), (1, 0)])  185 us
    ppermute x65, starting transfers between devices, swap(): return lax.ppermute(value, axis, [(0, 1), (1, 0)])  68.7 us
    reduce_scatter x6, waiting for transfers between devices, local(): lax.psum_scatter(g, 'dp', scatter_dimension=0, tiled=True)  66.3 us
    pallas_call x2, Pallas kernels, scan_backward(): pl.pallas_call(bwd_kernel, grid_spec=pltpu.PrefetchScalarGridSpec(num_sca...  65.8 us
    unnamed x235, local copies, waits for them, and re-layouts  45.5 us
    dot_general x6, matrix products, dot_nn(): lax.dot_general(a, b, (((1,), (0,)), ((), ())), preferred_element_type=f32)  41.5 us
    psum x1, waiting for transfers between devices, local(): shared_sums = lax.psum(shared_sums, ('section', 'tensor'))  37.3 us
    dot_general x6, matrix products, dot_tn(): lax.dot_general(a, b, (((0,), (0,)), ((), ())), preferred_element_type=f32)  37.1 us
  transfers between devices with their start and end apart: 78, of which 37 were waited for; matrix products, arithmetic and copies ran while one was open for 24% of the time, Pallas kernels for 8%

profile of v1, /device:TPU:0, one launch (start us, length us, event | category | flops | bytes accessed | tf_op | source)
XLA Modules:
  0.0 738.5 jit_solution(7276514835943368296)
XLA Ops:
  11.3 7.0 collective-permute-done.5
  26.8 6.5 collective-permute-done.8
  69.4 10.5 %collective-permute-done.2 = bf16[256,1536]{1,0:T(8,128)(2,1)} collective-permute-done((bf16[256,1536]{1,0:T(8,128)(2,1)}, bf16[256,1536]{1,0:T(8,128)(2,1)}, u32[]{:S(2)}, u32[]{:S(2)}) %collective-permute-start.2) | collective-permute-done | bytes 786464 | tf_op jit(solution)/shard_map/ppermute | solution.py:379
  84.5 7.0 fusion.79.pz
  96.4 7.3 fusion.80.px.halo
  103.7 14.8 %scan_forward.2 = (bf16[1024,768]{1,0:T(8,128)(2,1)S(1)}, f32[1024,768]{1,0:T(8,128)S(1)}, bf16[8,128,768]{2,1,0:T(8,128)(2,1)S(1)}, f32[8,8,128]{2,1,0:T(8,128)S(1)}) custom-call(s32[8]{0:T(128)S(1)} %pad_add_fusion.order, f32[1024,768]{1,0:T(8,128)S(1)} %copy-done.2, f32[1024,1152]{1,0:T(8,128)S(1)} %fusion.80.px.halo, f32[1024,1152]{1,0:T(8,128)S(1)} %fusion.80.px.halo, ...), custom_call_target="tpu_custom_call" | custom-call | flops 4000000000 | bytes 14680064 | tf_op jit(solution)/shard_map/scan_forward/pallas_call | solution.py:298
  137.7 16.6 %collective-permute-done.22 = f32[256]{0:T(256)S(1)} collective-permute-done((f32[256]{0:T(256)S(1)}, f32[256]{0:T(256)S(1)}, u32[]{:S(2)}, u32[]{:S(2)}) %collective-permute-start.22) | collective-permute-done | bytes 1056 | tf_op jit(solution)/shard_map/ppermute | solution.py:379
  187.1 12.7 %collective-permute-done.25 = bf16[256,1536]{1,0:T(8,128)(2,1)S(1)} collective-permute-done((bf16[256,1536]{1,0:T(8,128)(2,1)S(1)}, bf16[256,1536]{1,0:T(8,128)(2,1)S(1)}, u32[]{:S(2)}, u32[]{:S(2)}) %collective-permute-start.25) | collective-permute-done | bytes 786464 | tf_op jit(solution)/shard_map/ppermute | solution.py:379
  203.2 6.9 fusion.81.pz
  210.1 7.6 %fusion.82.px.halo = f32[1024,1152]{1,0:T(8,128)S(1)} fusion(bf16[1024,1536]{1,0:T(8,128)(2,1)} %constant_dynamic-update-slice_fusion.6, bf16[1536,1152]{1,0:T(8,128)(2,1)} %all-gather.19.cloned.1.call-done), kind=kOutput, calls=%fused_computation.314 | convolution fusion | flops 3623878656 | bytes 11403264 | tf_op jit(solution)/shard_map/dot_general | solution.py:20
  217.7 14.7 %scan_forward.3 = (bf16[1024,768]{1,0:T(8,128)(2,1)S(1)}, f32[1024,768]{1,0:T(8,128)S(1)}, bf16[8,128,768]{2,1,0:T(8,128)(2,1)S(1)}, f32[8,8,128]{2,1,0:T(8,128)S(1)}) custom-call(s32[8]{0:T(128)S(1)} %pad_add_fusion.order, f32[1024,768]{1,0:T(8,128)S(1)} %copy-done.6, f32[1024,1152]{1,0:T(8,128)S(1)} %fusion.82.px.halo, f32[1024,1152]{1,0:T(8,128)S(1)} %fusion.82.px.halo, ...), custom_call_target="tpu_custom_call" | custom-call | flops 4000000000 | bytes 14680064 | tf_op jit(solution)/shard_map/scan_forward/pallas_call | solution.py:298
  253.4 10.4 %collective-permute-done.30 = f32[256]{0:T(256)S(1)} collective-permute-done((f32[256]{0:T(256)S(1)}, f32[256]{0:T(256)S(1)}, u32[]{:S(2)}, u32[]{:S(2)}) %collective-permute-start.30) | collective-permute-done | bytes 1056 | tf_op jit(solution)/shard_map/ppermute | solution.py:379
  299.3 7.5 %collective-permute-done.33 = bf16[256,1536]{1,0:T(8,128)(2,1)} collective-permute-done((bf16[256,1536]{1,0:T(8,128)(2,1)}, bf16[256,1536]{1,0:T(8,128)(2,1)}, u32[]{:S(2)}, u32[]{:S(2)}) %collective-permute-start.33) | collective-permute-done | bytes 786464 | tf_op jit(solution)/shard_map/ppermute | solution.py:379
  311.4 6.3 fusion.83.d_ref
  317.7 32.9 %scan_backward.2 = (bf16[1024,768]{1,0:T(8,128)(2,1)S(1)}, bf16[1024,1152]{1,0:T(8,128)(2,1)S(1)}, f32[8,768]{1,0:T(8,128)S(1)}, f32[8,256]{1,0:T(8,128)S(1)}, f32[32,128]{1,0:T(8,128)S(1)}) custom-call(s32[8]{0:T(128)S(1)} %pad_add_fusion.order, f32[1024,768]{1,0:T(8,128)S(1)} %copy-done.7, f32[1024,1152]{1,0:T(8,128)} %copy-done.1, ...), custom_call_target="tpu_custom_call" | custom-call | flops 8000000000 | bytes 25165824 | tf_op jit(solution)/shard_map/scan_backward/pallas_call | solution.py:336
  361.6 11.4 %collective-permute-done.44 = bf16[256,1536]{1,0:T(8,128)(2,1)S(1)} collective-permute-done((bf16[256,1536]{1,0:T(8,128)(2,1)}, bf16[256,1536]{1,0:T(8,128)(2,1)S(1)}, u32[]{:S(2)}, u32[]{:S(2)}) %collective-permute-start.44) | collective-permute-done | bytes 786464 | tf_op jit(solution)/shard_map/ppermute | solution.py:379
  378.7 6.0 convolution_convert_fusion.6
  388.0 8.2 %collective-permute-done.45 = bf16[128,1536]{1,0:T(8,128)(2,1)S(1)} collective-permute-done((bf16[128,1536]{1,0:T(8,128)(2,1)S(1)}, bf16[128,1536]{1,0:T(8,128)(2,1)S(1)}, u32[]{:S(2)}, u32[]{:S(2)}) %collective-permute-start.45) | collective-permute-done | bytes 393248 | tf_op jit(solution)/shard_map/ppermute | solution.py:379
  423.2 6.2 collective-permute-done.49
  435.1 6.4 fusion.85.d_ref
  441.5 32.9 %scan_backward.3 = (bf16[1024,768]{1,0:T(8,128)(2,1)S(1)}, bf16[1024,1152]{1,0:T(8,128)(2,1)S(1)}, f32[8,768]{1,0:T(8,128)S(1)}, f32[8,256]{1,0:T(8,128)S(1)}, f32[32,128]{1,0:T(8,128)S(1)}) custom-call(s32[8]{0:T(128)S(1)} %pad_add_fusion.order, f32[1024,768]{1,0:T(8,128)S(1)} %copy-done.3, f32[1024,1152]{1,0:T(8,128)} %copy-done, f32[1024,1152]{1,0:T(8,128)} %copy-done, ...), custom_call_target="tpu_custom_call" | custom-call | flops 8000000000 | bytes 25165824 | tf_op jit(solution)/shard_map/scan_backward/pallas_call | solution.py:336
  481.2 6.5 convolution_convert_fusion.4
  487.8 6.0 convolution_convert_fusion.5
  493.8 8.8 %convolution_convert_fusion = bf16[1536,1152]{1,0:T(8,128)(2,1)} fusion(bf16[1024,1536]{1,0:T(8,128)(2,1)} %constant_dynamic-update-slice_fusion.6, bf16[1024,1152]{1,0:T(8,128)(2,1)} %copy-done.15), kind=kOutput, calls=%fused_computation | convolution fusion | flops 3625648128 | bytes 9043968 | tf_op jit(solution)/shard_map/dot_general | solution.py:28
  503.2 7.1 fusion.86
  517.7 13.5 %collective-permute-done.56 = bf16[256,1536]{1,0:T(8,128)(2,1)S(1)} collective-permute-done((bf16[256,1536]{1,0:T(8,128)(2,1)S(1)}, bf16[256,1536]{1,0:T(8,128)(2,1)S(1)}, u32[]{:S(2)}, u32[]{:S(2)}) %collective-permute-start.56) | collective-permute-done | bytes 786464 | tf_op jit(solution)/shard_map/ppermute | solution.py:379
  551.4 17.3 %all-gather.2 = f32[8,2,9760]{2,1,0:T(2,128)} all-gather(f32[1,2,9760]{2,1,0:T(2,128)S(1)} %maximum_bitcast_fusion.1), channel_id=2, replica_groups=mesh['section'=2,'dp'=8,'tensor'=2] {'dp'}, dimensions={0}, use_global_device_ids=true | all-gather | bytes 702720 | tf_op jit(solution)/shard_map/all_gather | solution.py:565
  570.0 9.4 %all-gather.3 = f32[4,2,9760]{2,1,0:T(2,128)S(1)} all-gather(f32[1,2,9760]{2,1,0:T(2,128)S(1)} %bitcast.239), channel_id=3, replica_groups=mesh['section'=2,'dp'=8,'tensor'=2] {'section','tensor'}, dimensions={0}, use_global_device_ids=true | all-gather | bytes 390400 | tf_op jit(solution)/shard_map/all_gather | solution.py:566
  590.3 14.0 %collective-permute-done.60 = bf16[2,128,1536]{2,1,0:T(8,128)(2,1)S(1)} collective-permute-done((bf16[2,128,1536]{2,1,0:T(8,128)(2,1)}, bf16[2,128,1536]{2,1,0:T(8,128)(2,1)S(1)}, u32[]{:S(2)}, u32[]{:S(2)}) %collective-permute-start.60) | collective-permute-done | bytes 786464 | tf_op jit(solution)/shard_map/ppermute | solution.py:379
  612.3 25.1 %reduce-scatter.13.cloned.1.call-done = bf16[192,1152]{1,0:T(8,128)(2,1)} async-done(((bf16[1536,1152]{1,0:T(8,128)(2,1)}), bf16[192,1152]{1,0:T(8,128)(2,1)}) %reduce-scatter.13.cloned.1.call-update) | async-done | bytes 442384 | tf_op jit(solution)/shard_map/reduce_scatter | solution.py:549
  640.7 41.3 %reduce-scatter.11.cloned.1.call-done = bf16[192,1152]{1,0:T(8,128)(2,1)} async-done(((bf16[1536,1152]{1,0:T(8,128)(2,1)}), bf16[192,1152]{1,0:T(8,128)(2,1)}) %reduce-scatter.11.cloned.1.call-update) | async-done | bytes 442384 | tf_op jit(solution)/shard_map/reduce_scatter | solution.py:549
  692.8 37.3 %all-reduce.9.cloned.1.call-done = f32[2,192,256]{2,1,0:T(8,128)} async-done(((f32[2,192,256]{2,1,0:T(8,128)}), f32[2,192,256]{2,1,0:T(8,128)}) %all-reduce.9.cloned.1.call-update) | async-done | bytes 393232 | tf_op jit(solution)/shard_map/psum | solution.py:595
  (580 shorter events, 296.9 us)
Async XLA Ops:
  7.2 77.3 %all-gather.11.cloned.1.call-start = ((), (), s32[]{:S(2)}) async-start(), calls=%async_computation.6 | async-start | bytes 2654208 | tf_op jit(solution)/shard_map/all_gather | solution.py:456
  20.2 76.2 %all-gather.13.cloned.1.call-start = ((), (), s32[]{:S(2)}) async-start(), calls=%async_computation.7 | async-start | bytes 3981312 | tf_op jit(solution)/shard_map/all_gather | solution.py:455
  35.0 93.1 %all-gather.15.cloned.1.call-start = ((), (), s32[]{:S(2)}) async-start(), calls=%async_computation.8 | async-start | bytes 2654208 | tf_op jit(solution)/shard_map/all_gather | solution.py:457
  42.9 160.4 %all-gather.17.cloned.1.call-start = ((), (), s32[]{:S(2)}) async-start(), calls=%async_computation.9 | async-start | bytes 2654208 | tf_op jit(solution)/shard_map/all_gather | solution.py:456
  44.3 165.8 %all-gather.19.cloned.1.call-start = ((), (), s32[]{:S(2)}) async-start(), calls=%async_computation.10 | async-start | bytes 3981312 | tf_op jit(solution)/shard_map/all_gather | solution.py:455
  44.4 18.6 %collective-permute-start.10 = (f32[8,768]{1,0:T(8,128)S(1)}, f32[8,768]{1,0:T(8,128)S(1)}, u32[]{:S(2)}, u32[]{:S(2)}) collective-permute-start(f32[8,768]{1,0:T(8,128)S(1)} %pad_dynamic-slice_fusion), channel_id=1, source_target_pairs={{0,16},{16,0},{1,17},{17,1},{2,18},{18,2},{3,19},{19,3},{4,20},{20... | collective-permute-start | bytes 73736 | tf_op jit(solution)/shard_map/ppermute | solution.py:379
  61.7 18.3 %collective-permute-start.2 = (bf16[256,1536]{1,0:T(8,128)(2,1)}, bf16[256,1536]{1,0:T(8,128)(2,1)}, u32[]{:S(2)}, u32[]{:S(2)}) collective-permute-start(bf16[256,1536]{1,0:T(8,128)(2,1)} %pad_maximum_fusion.2), channel_id=1, source_target_pairs={{0,1},{1,0},{2,3},{3,2},{4,5},{5,4},{6,7},{7,6},{8,9},{9,8},{10,11... | collective-permute-start | bytes 2359304 | tf_op jit(solution)/shard_map/ppermute | solution.py:379
  63.8 174.8 %all-gather.21.cloned.1.call-start = ((), (), s32[]{:S(2)}) async-start(), calls=%async_computation.11 | async-start | bytes 2654208 | tf_op jit(solution)/shard_map/all_gather | solution.py:457
  68.1 15.5 %collective-permute-start.4 = (bf16[256,1536]{1,0:T(8,128)(2,1)S(1)}, bf16[256,1536]{1,0:T(8,128)(2,1)S(1)}, u32[]{:S(2)}, u32[]{:S(2)}) collective-permute-start(bf16[256,1536]{1,0:T(8,128)(2,1)S(1)} %pad_maximum_fusion.3), channel_id=1, source_target_pairs={{0,16},{16,0},{1,17},{17,1},{2,18},{18,2},{3,19},{19,3},{4,20},{20... | collective-permute-start | bytes 2359304 | tf_op jit(solution)/shard_map/ppermute | solution.py:379
  132.9 23.5 %collective-permute-start.16 = (bf16[256,1536]{1,0:T(8,128)(2,1)S(1)}, bf16[256,1536]{1,0:T(8,128)(2,1)S(1)}, u32[]{:S(2)}, u32[]{:S(2)}) collective-permute-start(bf16[256,1536]{1,0:T(8,128)(2,1)S(1)} %get-tuple-element.124), channel_id=1, source_target_pairs={{0,1},{1,0},{2,3},{3,2},{4,5},{5,4},{6,7},{7,6},{8,9},{9,8},{10,11... | collective-permute-start | bytes 2359304 | tf_op jit(solution)/shard_map/ppermute | solution.py:379
  134.8 21.5 %collective-permute-start.18 = (bf16[256,1536]{1,0:T(8,128)(2,1)S(1)}, bf16[256,1536]{1,0:T(8,128)(2,1)S(1)}, u32[]{:S(2)}, u32[]{:S(2)}) collective-permute-start(bf16[256,1536]{1,0:T(8,128)(2,1)S(1)} %get-tuple-element.125), channel_id=1, source_target_pairs={{0,16},{16,0},{1,17},{17,1},{2,18},{18,2},{3,19},{19,3},{4,20},{20... | collective-permute-start | bytes 2359304 | tf_op jit(solution)/shard_map/ppermute | solution.py:379
  136.3 18.0 %collective-permute-start.22 = (f32[256]{0:T(256)S(1)}, f32[256]{0:T(256)S(1)}, u32[]{:S(2)}, u32[]{:S(2)}) collective-permute-start(f32[256]{0:T(256)S(1)} %bitcast.264), channel_id=1, source_target_pairs={{0,16},{16,0},{1,17},{17,1},{2,18},{18,2},{3,19},{19,3},{4,20},{20... | collective-permute-start | bytes 3080 | tf_op jit(solution)/shard_map/ppermute | solution.py:379
  136.9 17.7 %collective-permute-start.20 = (f32[256]{0:T(256)S(1)}, f32[256]{0:T(256)S(1)}, u32[]{:S(2)}, u32[]{:S(2)}) collective-permute-start(f32[256]{0:T(256)S(1)} %bitcast.262), channel_id=1, source_target_pairs={{0,1},{1,0},{2,3},{3,2},{4,5},{5,4},{6,7},{7,6},{8,9},{9,8},{10,11... | collective-permute-start | bytes 3080 | tf_op jit(solution)/shard_map/ppermute | solution.py:379
  174.1 433.8 %reduce-scatter.9.cloned.1.call-start = ((), (), s32[]{:S(2)}) async-start(), calls=%async_computation.13 | async-start | bytes 2654208 | tf_op jit(solution)/shard_map/reduce_scatter | solution.py:549
  181.3 18.4 %collective-permute-start.25 = (bf16[256,1536]{1,0:T(8,128)(2,1)S(1)}, bf16[256,1536]{1,0:T(8,128)(2,1)S(1)}, u32[]{:S(2)}, u32[]{:S(2)}) collective-permute-start(bf16[256,1536]{1,0:T(8,128)(2,1)S(1)} %pad_maximum_fusion.4), channel_id=1, source_target_pairs={{0,1},{1,0},{2,3},{3,2},{4,5},{5,4},{6,7},{7,6},{8,9},{9,8},{10,11... | collective-permute-start | bytes 2359304 | tf_op jit(solution)/shard_map/ppermute | solution.py:379
  185.3 17.0 %collective-permute-start.27 = (bf16[256,1536]{1,0:T(8,128)(2,1)S(1)}, bf16[256,1536]{1,0:T(8,128)(2,1)S(1)}, u32[]{:S(2)}, u32[]{:S(2)}) collective-permute-start(bf16[256,1536]{1,0:T(8,128)(2,1)S(1)} %pad_maximum_fusion.5), channel_id=1, source_target_pairs={{0,16},{16,0},{1,17},{17,1},{2,18},{18,2},{3,19},{19,3},{4,20},{20... | collective-permute-start | bytes 2359304 | tf_op jit(solution)/shard_map/ppermute | solution.py:379
  245.6 20.3 %collective-permute-start.36 = (bf16[256,1536]{1,0:T(8,128)(2,1)}, bf16[256,1536]{1,0:T(8,128)(2,1)S(1)}, u32[]{:S(2)}, u32[]{:S(2)}) collective-permute-start(bf16[256,1536]{1,0:T(8,128)(2,1)} %get-tuple-element.120), channel_id=1, source_target_pairs={{0,1},{1,0},{2,3},{3,2},{4,5},{5,4},{6,7},{7,6},{8,9},{9,8},{10,11... | collective-permute-start | bytes 2359304 | tf_op jit(solution)/shard_map/ppermute | solution.py:379
  246.7 19.2 %collective-permute-start.38 = (bf16[256,1536]{1,0:T(8,128)(2,1)}, bf16[256,1536]{1,0:T(8,128)(2,1)}, u32[]{:S(2)}, u32[]{:S(2)}) collective-permute-start(bf16[256,1536]{1,0:T(8,128)(2,1)} %get-tuple-element.121), channel_id=1, source_target_pairs={{0,16},{16,0},{1,17},{17,1},{2,18},{18,2},{3,19},{19,3},{4,20},{20... | collective-permute-start | bytes 2359304 | tf_op jit(solution)/shard_map/ppermute | solution.py:379
  280.7 15.6 %collective-permute-start.34 = (bf16[128,1536]{1,0:T(8,128)(2,1)}, bf16[128,1536]{1,0:T(8,128)(2,1)S(1)}, u32[]{:S(2)}, u32[]{:S(2)}) collective-permute-start(bf16[128,1536]{1,0:T(8,128)(2,1)} %get-tuple-element.144), channel_id=1, source_target_pairs={{0,1},{1,0},{2,3},{3,2},{4,5},{5,4},{6,7},{7,6},{8,9},{9,8},{10,11... | collective-permute-start | bytes 1179656 | tf_op jit(solution)/shard_map/ppermute | solution.py:379
  384.8 223.2 %reduce-scatter.7.cloned.1.call-start = ((), (), s32[]{:S(2)}) async-start(), calls=%async_computation.12 | async-start | bytes 2654208 | tf_op jit(solution)/shard_map/reduce_scatter | solution.py:549
  401.2 14.3 %collective-permute-start.48 = (bf16[128,1536]{1,0:T(8,128)(2,1)S(1)}, bf16[128,1536]{1,0:T(8,128)(2,1)S(1)}, u32[]{:S(2)}, u32[]{:S(2)}) collective-permute-start(bf16[128,1536]{1,0:T(8,128)(2,1)S(1)} %get-tuple-element.143), channel_id=1, source_target_pairs={{0,16},{16,0},{1,17},{17,1},{2,18},{18,2},{3,19},{19,3},{4,20},{20... | collective-permute-start | bytes 1179656 | tf_op jit(solution)/shard_map/ppermute | solution.py:379
  401.6 19.5 %collective-permute-start.50 = (bf16[128,1536]{1,0:T(8,128)(2,1)}, bf16[128,1536]{1,0:T(8,128)(2,1)S(1)}, u32[]{:S(2)}, u32[]{:S(2)}) collective-permute-start(bf16[128,1536]{1,0:T(8,128)(2,1)} %get-tuple-element.142), channel_id=1, source_target_pairs={{0,1},{1,0},{2,3},{3,2},{4,5},{5,4},{6,7},{7,6},{8,9},{9,8},{10,11... | collective-permute-start | bytes 1179656 | tf_op jit(solution)/shard_map/ppermute | solution.py:379
  480.9 128.8 %reduce-scatter.17.cloned.1.call-start = ((), (), s32[]{:S(2)}) async-start(), calls=%async_computation.18 | async-start | bytes 2654208 | tf_op jit(solution)/shard_map/reduce_scatter | solution.py:549
  487.7 122.0 %reduce-scatter.15.cloned.1.call-start = ((), (), s32[]{:S(2)}) async-start(), calls=%async_computation.17 | async-start | bytes 2654208 | tf_op jit(solution)/shard_map/reduce_scatter | solution.py:549
  493.8 143.6 %reduce-scatter.13.cloned.1.call-start = ((), (), s32[]{:S(2)}) async-start(), calls=%async_computation.15 | async-start | bytes 3981312 | tf_op jit(solution)/shard_map/reduce_scatter | solution.py:549
  502.6 179.4 %reduce-scatter.11.cloned.1.call-start = ((), (), s32[]{:S(2)}) async-start(), calls=%async_computation.14 | async-start | bytes 3981312 | tf_op jit(solution)/shard_map/reduce_scatter | solution.py:549
  515.0 16.2 %collective-permute-start.56 = (bf16[256,1536]{1,0:T(8,128)(2,1)S(1)}, bf16[256,1536]{1,0:T(8,128)(2,1)S(1)}, u32[]{:S(2)}, u32[]{:S(2)}) collective-permute-start(bf16[256,1536]{1,0:T(8,128)(2,1)S(1)} %get-tuple-element.112), channel_id=1, source_target_pairs={{0,1},{1,0},{2,3},{3,2},{4,5},{5,4},{6,7},{7,6},{8,9},{9,8},{10,11... | collective-permute-start | bytes 2359304 | tf_op jit(solution)/shard_map/ppermute | solution.py:379
  515.5 15.7 %collective-permute-start.58 = (bf16[256,1536]{1,0:T(8,128)(2,1)S(1)}, bf16[256,1536]{1,0:T(8,128)(2,1)}, u32[]{:S(2)}, u32[]{:S(2)}) collective-permute-start(bf16[256,1536]{1,0:T(8,128)(2,1)S(1)} %get-tuple-element.113), channel_id=1, source_target_pairs={{0,16},{16,0},{1,17},{17,1},{2,18},{18,2},{3,19},{19,3},{4,20},{20... | collective-permute-start | bytes 2359304 | tf_op jit(solution)/shard_map/ppermute | solution.py:379
  542.2 187.9 %all-reduce.9.cloned.1.call-start = ((), (), s32[]{:S(2)}) async-start(), calls=%async_computation.16 | async-start | bytes 786432 | tf_op jit(solution)/shard_map/psum | solution.py:595
  585.4 18.8 %collective-permute-start.60 = (bf16[2,128,1536]{2,1,0:T(8,128)(2,1)}, bf16[2,128,1536]{2,1,0:T(8,128)(2,1)S(1)}, u32[]{:S(2)}, u32[]{:S(2)}) collective-permute-start(bf16[2,128,1536]{2,1,0:T(8,128)(2,1)} %get-tuple-element.101), channel_id=1, source_target_pairs={{0,16},{16,0},{1,17},{17,1},{2,18},{18,2},{3,19},{19,3},{4,20},{20... | collective-permute-start | bytes 2359304 | tf_op jit(solution)/shard_map/ppermute | solution.py:379
  609.0 29.2 %collective-permute-start.61 = (bf16[192,768]{1,0:T(8,128)(2,1)S(1)}, bf16[192,768]{1,0:T(8,128)(2,1)S(1)}, u32[]{:S(2)}, u32[]{:S(2)}) collective-permute-start(bf16[192,768]{1,0:T(8,128)(2,1)S(1)} %broadcast_select_fusion.5), channel_id=1, source_target_pairs={{0,16},{16,0},{1,17},{17,1},{2,18},{18,2},{3,19},{19,3},{4,20},{20... | collective-permute-start | bytes 884744 | tf_op jit(solution)/shard_map/ppermute | solution.py:379
  610.8 27.6 %collective-permute-start.64 = (bf16[192,768]{1,0:T(8,128)(2,1)S(1)}, bf16[192,768]{1,0:T(8,128)(2,1)S(1)}, u32[]{:S(2)}, u32[]{:S(2)}) collective-permute-start(bf16[192,768]{1,0:T(8,128)(2,1)S(1)} %broadcast_select_fusion.1), channel_id=1, source_target_pairs={{0,16},{16,0},{1,17},{17,1},{2,18},{18,2},{3,19},{19,3},{4,20},{20... | collective-permute-start | bytes 884744 | tf_op jit(solution)/shard_map/ppermute | solution.py:379
  (143 other events, 1177.0 us)
Sparse Core Ops, SparseCore 0:
  20.4 33.1 all-gather.10
  55.7 40.6 all-gather.12
  98.0 30.0 all-gather.14
  129.7 31.2 all-gather.16
  163.0 40.5 all-gather.18
  205.1 30.4 all-gather.20
  384.9 34.3 reduce-scatter.8
  481.0 34.0 reduce-scatter.6
  517.4 35.6 reduce-scatter.16
  555.3 36.2 reduce-scatter.14
  593.8 43.4 reduce-scatter.12
  639.7 42.2 reduce-scatter.10
  687.8 42.2 all-reduce.8

commit v2 on v1

v2 whole, which is shorter than its diff:
```python
import functools

import jax
import jax.numpy as jnp
import numpy as np
from jax import lax
from jax.experimental import pallas as pl
from jax.experimental.pallas import tpu as pltpu
from jax.sharding import PartitionSpec as P

DI = 3072
P_SIZE = 64
N = 128
T = 128
LANES = 128
HP = 16
eps = 1e-05
bf16 = jnp.bfloat16
f32 = jnp.float32


def dot_nn(a, b):
    return lax.dot_general(a, b, (((1,), (0,)), ((), ())), preferred_element_type=f32)


def dot_nt(a, b):
    return lax.dot_general(a, b, (((1,), (1,)), ((), ())), preferred_element_type=f32)


def dot_tn(a, b):
    return lax.dot_general(a, b, (((0,), (0,)), ((), ())), preferred_element_type=f32)


def sigmoid(v):
    return 0.5 + 0.5 * jnp.tanh(0.5 * v)


def shifted(cat):
    return (
        pltpu.roll(cat, 3, 0)[8:],
        pltpu.roll(cat, 2, 0)[8:],
        pltpu.roll(cat, 1, 0)[8:],
        cat[8:],
    )


def conv(parts, taps):
    total = taps[4:5]
    for j in range(4):
        total = total + taps[j : j + 1] * parts[j]
    return total


def conv_back(ds, after, taps):
    cat = jnp.concatenate([ds, after], axis=0)
    rows = cat.shape[0]
    total = taps[3:4] * ds
    for j in range(3):
        total = total + taps[j : j + 1] * pltpu.roll(cat, rows - (3 - j), 0)[: ds.shape[0]]
    return total


def lane_ids(shape):
    return lax.broadcasted_iota(jnp.int32, shape, len(shape) - 1)


def running_sum(v, lane):
    step = 1
    while step < LANES:
        v = v + jnp.where(lane >= step, pltpu.roll(v, step, 1), 0.0)
        step *= 2
    return v


def running_sum_back(v, lane):
    step = 1
    while step < LANES:
        v = v + jnp.where(lane < LANES - step, pltpu.roll(v, LANES - step, 1), 0.0)
        step *= 2
    return v


def parts_of(v):
    high = v.astype(bf16)
    rest = v - high.astype(f32)
    middle = rest.astype(bf16)
    return high, middle, (rest - middle.astype(f32)).astype(bf16)


def prepare_steps(pre_dt, heads, rows_ref, cols_ref):
    chunks = pre_dt.shape[0] // T
    logits = jnp.concatenate(
        [jnp.transpose(pre_dt[c * T : (c + 1) * T])[:HP] + heads[:, 0:1] for c in range(chunks)], axis=0
    )
    small = jnp.exp(-jnp.abs(logits))
    log_part = jnp.where(small < 1e-3, small * (1.0 - small * (0.5 - small / 3.0)), jnp.log(1.0 + small))
    steps = jnp.maximum(logits, 0.0) + log_part
    decays = jnp.concatenate([heads[:, 1:2]] * chunks, axis=0)
    run = running_sum(steps * decays, lane_ids(steps.shape))
    for c in range(chunks):
        at = slice(c * HP, (c + 1) * HP)
        rows_ref[c, 0:HP] = logits[at]
        rows_ref[c, HP : 2 * HP] = steps[at]
        rows_ref[c, 2 * HP : 3 * HP] = run[at]
        split = [part.astype(f32) for part in parts_of(run[at]) + parts_of(steps[at])]
        split.append(jnp.zeros((LANES - 6 * HP, T), f32))
        cols_ref[c] = jnp.transpose(jnp.concatenate(split, axis=0)).astype(bf16)


def eights(v):
    return jnp.sum(v.reshape(v.shape[0] // 8, 8, v.shape[1]), axis=0)


def fwd_kernel(
    order, px, halo, pre_dt, taps_x, taps_bc, heads, skip, gain, spread_run, spread_steps,
    og_ref, y_ref, s_ref, sq_ref, rows_ref, cols_ref, state,
):
    s_id, k = pl.program_id(0), pl.program_id(1)
    width = y_ref.shape[1]
    pairs = width // LANES
    bc_at, z_at = width, width + 2 * N + LANES

    @pl.when((s_id == 0) & (k == 0))
    def _():
        prepare_steps(pre_dt[...], heads[...], rows_ref, cols_ref)

    @pl.when(k == 0)
    def _():
        state[...] = jnp.zeros_like(state)

    block = order[s_id * 4 + k]
    keep = jnp.where(k > 0, 1.0, 0.0)
    lane = lane_ids((T, LANES))
    low = lane < P_SIZE
    row = lax.broadcasted_iota(jnp.int32, (T, T), 0)
    run = rows_ref[block, 2 * HP : 3 * HP]
    cols = cols_ref[block]
    runs_wide = dot_nn(cols, spread_run[...])
    steps_wide = dot_nn(cols, spread_steps[...])
    bc_cat = jnp.concatenate([halo[:, bc_at : bc_at + 2 * N] * keep, px[:, bc_at : bc_at + 2 * N]], axis=0)
    s_bc = conv(shifted(bc_cat), taps_bc[...])
    bc = s_bc * sigmoid(s_bc)
    keys = bc[:, :N]
    keys_t = jnp.transpose(keys).astype(bf16)
    reads = bc[:, N:].astype(bf16)
    scores = jnp.where(row >= lane, dot_nt(reads, keys.astype(bf16)), 0.0)
    squares = jnp.zeros((T, LANES), f32)
    for p in range(pairs):
        at = slice(p * LANES, (p + 1) * LANES)
        x_cat = jnp.concatenate([halo[:, at] * keep, px[:, at]], axis=0)
        s_x = conv(shifted(x_cat), taps_x[:, at])
        xs = s_x * sigmoid(s_x)
        xd = xs * steps_wide[:, at]
        xr = xd.astype(bf16)
        mixes = []
        wide = []
        for h in (2 * p, 2 * p + 1):
            ci = runs_wide[:, h * LANES : (h + 1) * LANES]
            mixes.append((jnp.exp(jnp.minimum(ci - run[h : h + 1], 0.0)) * scores).astype(bf16))
            wide.append(ci)
        c_pair = jnp.where(low, wide[0], wide[1])
        e_pair = jnp.exp(c_pair)
        zero = jnp.zeros_like(xr)
        y = dot_nn(
            jnp.concatenate(mixes, axis=1),
            jnp.concatenate([jnp.where(low, xr, zero), jnp.where(low, zero, xr)], axis=0),
        )
        entering = state[:, at]
        entering_r = entering.astype(bf16)
        s_ref[0, :, at] = entering_r
        y = y + e_pair * dot_nn(reads, entering_r)
        left = (xd * jnp.exp(c_pair[T - 1 : T] - c_pair)).astype(bf16)
        state[:, at] = e_pair[T - 1 : T] * entering + dot_nn(keys_t, left)
        y_ref[:, at] = y
        z = px[:, z_at + p * LANES : z_at + (p + 1) * LANES]
        g = (y + skip[:, at] * xs) * (z * sigmoid(z))
        squares = squares + g * g
        og_ref[:, at] = (g * gain[:, at]).astype(bf16)
    sq_ref[0] = jnp.broadcast_to(jnp.sum(jnp.transpose(squares), axis=0, keepdims=True), (8, T))


def bwd_kernel(
    order, px, halo, y_ref, s_ref, d_ref, stats, rows_ref, cols_ref,
    taps_x, taps_bc, heads, skip, gain, spread_run, spread_steps, sums,
    pre_ref, acc_x, acc_bc, acc_dt,
    back, after_x, after_bc, d_scores, head_sums_ref, part_x, part_bc,
):
    s_id, k = pl.program_id(0), pl.program_id(1)
    width = y_ref.shape[1]
    pairs = width // LANES
    bc_at, dt_at, z_at = width, width + 2 * N, width + 2 * N + LANES

    @pl.when(k == 0)
    def _():
        back[...] = jnp.zeros_like(back)
        after_x[...] = jnp.zeros_like(after_x)
        after_bc[...] = jnp.zeros_like(after_bc)

    @pl.when((k == 0) & (s_id == 0))
    def _():
        part_x[...] = jnp.zeros_like(part_x)
        part_bc[...] = jnp.zeros_like(part_bc)
        acc_dt[...] = jnp.zeros_like(acc_dt)

    block = order[s_id * 4 + 3 - k]
    place = block - s_id * 4
    dx_ref = pre_ref.at[pl.ds(pl.multiple_of(place * T, T), T)]
    keep = jnp.where(k < 3, 1.0, 0.0)
    lane = lane_ids((T, LANES))
    low = lane < P_SIZE
    row = lax.broadcasted_iota(jnp.int32, (T, T), 0)
    seen_t = lane >= row
    last = row == T - 1
    run = rows_ref[block, 2 * HP : 3 * HP]
    cols = cols_ref[block]
    runs_wide = dot_nn(cols, spread_run[...])
    steps_wide = dot_nn(cols, spread_steps[...])
    bc_cat = jnp.concatenate([halo[:, bc_at : bc_at + 2 * N] * keep, px[:, bc_at : bc_at + 2 * N]], axis=0)
    bc_parts = shifted(bc_cat)
    s_bc = conv(bc_parts, taps_bc[...])
    sig_bc = sigmoid(s_bc)
    bc = s_bc * sig_bc
    keys, reads = bc[:, :N].astype(bf16), bc[:, N:].astype(bf16)
    reads_t = jnp.transpose(bc[:, N:]).astype(bf16)
    scores_t = jnp.where(seen_t, dot_nt(keys, reads), 0.0)
    d_scores[...] = jnp.zeros_like(d_scores)
    d_reads = jnp.zeros((T, N), f32)
    d_keys = jnp.zeros((T, N), f32)
    head_sums = jnp.zeros((T, LANES), f32)
    stat_cols = jnp.transpose(stats[0])
    row_scale = jnp.broadcast_to(stat_cols[:, 0:1], (T, LANES))
    row_stat = jnp.broadcast_to(stat_cols[:, 1:2], (T, LANES))
    for p in range(pairs):
        at = slice(p * LANES, (p + 1) * LANES)
        x_cat = jnp.concatenate([halo[:, at] * keep, px[:, at]], axis=0)
        x_parts = shifted(x_cat)
        s_x = conv(x_parts, taps_x[:, at])
        sig_x = sigmoid(s_x)
        xs = s_x * sig_x
        steps_pair = steps_wide[:, at]
        xd = xs * steps_pair
        xr = xd.astype(bf16)
        z = px[:, z_at + p * LANES : z_at + (p + 1) * LANES]
        sig_z = sigmoid(z)
        silu_z = z * sig_z
        y = y_ref[:, at]
        y_all = y + skip[:, at] * xs
        g = y_all * silu_z
        dr = d_ref[:, at] * row_scale
        dg = gain[:, at] * dr - g * row_stat
        part_x[40:48, at] += eights(dr * g)
        dx_ref[:, z_at + p * LANES : z_at + (p + 1) * LANES] = (
            dg * y_all * (sig_z + silu_z * (1.0 - sig_z))
        ).astype(bf16)
        dy = dg * silu_z
        dyr = dy.astype(bf16)
        part_x[48:56, at] += eights(dy * xs)
        zero = jnp.zeros_like(xr)
        mixes_t = []
        wide = []
        total = d_scores[...]
        for i, h in enumerate((2 * p, 2 * p + 1)):
            cj = runs_wide[:, h * LANES : (h + 1) * LANES]
            decay = jnp.exp(jnp.minimum(run[h : h + 1] - cj, 0.0))
            mixes_t.append((decay * scores_t).astype(bf16))
            x_one = jnp.where(low, xr, zero) if i == 0 else jnp.where(low, zero, xr)
            total = total + decay * dot_nt(x_one, dyr)
            wide.append(cj)
        d_scores[...] = total
        c_pair = jnp.where(low, wide[0], wide[1])
        e_pair = jnp.exp(c_pair)
        e_left = jnp.exp(c_pair[T - 1 : T] - c_pair)
        dx_in = dot_nn(
            jnp.concatenate(mixes_t, axis=1),
            jnp.concatenate([jnp.where(low, dyr, zero), jnp.where(low, zero, dyr)], axis=0),
        )
        returning = back[:, at]
        returning_r = returning.astype(bf16)
        entering_r = s_ref[0, :, at]
        dx_out = e_left * dot_nn(keys, returning_r)
        dye = (dy * e_pair).astype(bf16)
        d_reads = d_reads + dot_nt(dye, entering_r)
        d_keys = d_keys + dot_nt((xd * e_left).astype(bf16), returning_r)
        e_last = e_pair[T - 1 : T]
        back[:, at] = e_last * returning + dot_nn(reads_t, dye)
        across = e_last * jnp.sum(returning * entering_r.astype(f32), axis=0, keepdims=True)
        xf, dyf = xr.astype(f32), dyr.astype(f32)
        two = xf * dx_in
        three = xd * dx_out
        one = dyf * y - two + jnp.where(last, across, 0.0)
        high = one.astype(bf16)
        rest = (one - high.astype(f32)).astype(bf16)
        head_sums = head_sums + dot_nn(
            jnp.concatenate([high, rest, (two + three).astype(bf16), three.astype(bf16)], axis=1),
            sums[4 * p * LANES : 4 * (p + 1) * LANES],
        )
        dxs = steps_pair * (dx_in + dx_out) + skip[:, at] * dy
        ds = dxs * (sig_x + xs * (1.0 - sig_x))
        for j in range(4):
            part_x[8 * j : 8 * j + 8, at] += eights(ds * x_parts[j])
        part_x[32:40, at] += eights(ds)
        dx_ref[:, at] = conv_back(ds, after_x[:, at], taps_x[:, at]).astype(bf16)
        after_x[:, at] = ds[:8]
    head_sums_ref[pl.ds(pl.multiple_of(place * T, T), T)] = head_sums
    ds_t = jnp.where(seen_t, d_scores[...], 0.0)
    d_keys = d_keys + dot_nn(ds_t.astype(bf16), reads)
    d_reads = d_reads + dot_nn(jnp.transpose(ds_t).astype(bf16), keys)
    ds_bc = jnp.concatenate([d_keys, d_reads], axis=1) * (sig_bc + bc * (1.0 - sig_bc))
    for j in range(4):
        part_bc[8 * j : 8 * j + 8] += eights(ds_bc * bc_parts[j])
    part_bc[32:40] += eights(ds_bc)
    dx_ref[:, bc_at : bc_at + 2 * N] = conv_back(ds_bc, after_bc[...], taps_bc[...]).astype(bf16)
    after_bc[...] = ds_bc[:8]

    @pl.when(k == 3)
    def _():
        head_cols = heads[...]
        turned = [jnp.transpose(head_sums_ref[c * T : (c + 1) * T]) for c in range(4)]
        one, both, three = (
            jnp.concatenate([t[i * HP : (i + 1) * HP] for t in turned], axis=0) for i in range(3)
        )
        logits = jnp.concatenate([rows_ref[s_id * 4 + c, 0:HP] for c in range(4)], axis=0)
        steps = jnp.concatenate([rows_ref[s_id * 4 + c, HP : 2 * HP] for c in range(4)], axis=0)
        decay_rate = jnp.concatenate([head_cols[:, 1:2]] * 4, axis=0)
        lane_h = lane_ids(one.shape)
        d_decay = running_sum_back(one, lane_h) + running_sum(three, lane_h) - three
        exact = jnp.exp(jnp.minimum(logits, 0.0)) / (1.0 + jnp.exp(-jnp.abs(logits)))
        ratio = jnp.where(logits < -15.0, 1.0, exact / jnp.maximum(steps, 1e-30))
        d_pre = both * ratio + decay_rate * d_decay * exact
        d_rate = steps * d_decay
        for c in range(4):
            at = slice(c * HP, (c + 1) * HP)
            acc_dt[0:HP] += d_rate[at]
            acc_dt[HP : 2 * HP] += d_pre[at]
            padded = jnp.concatenate([d_pre[at], jnp.zeros((LANES - HP, T), f32)], axis=0)
            pre_ref[c * T : (c + 1) * T, dt_at : dt_at + LANES] = jnp.transpose(padded).astype(bf16)

    @pl.when((k == 3) & (s_id == pl.num_programs(0) - 1))
    def _():
        acc_x[...] = jnp.zeros_like(acc_x)
        acc_bc[...] = jnp.zeros_like(acc_bc)
        for j in range(7):
            acc_x[j : j + 1] = jnp.sum(part_x[8 * j : 8 * j + 8], axis=0, keepdims=True)
        for j in range(5):
            acc_bc[j : j + 1] = jnp.sum(part_bc[8 * j : 8 * j + 8], axis=0, keepdims=True)


def hbm(*arrays):
    return [pltpu.with_memory_space_constraint(array, pltpu.HBM) for array in arrays]


def whole_spec(array):
    return pl.BlockSpec(array.shape, lambda s, k, order: (0,) * array.ndim)


def scan_forward(order, px, layer, fixed_arrays):
    rows, width = px.shape[0], layer["skip"].shape[1]
    steps = rows // T
    here = lambda s, k, order: (order[s * 4 + k], 0)
    before = lambda s, k, order: (order[s * 4 + jnp.maximum(k - 1, 0)] * (T // 8) + (T // 8 - 1), 0)
    small = (layer["taps_x"], layer["taps_bc"], layer["heads"], layer["skip"], layer["gain"]) + fixed_arrays[:2]
    whole = lambda s, k, order: (0, 0, 0)
    return pl.pallas_call(
        fwd_kernel,
        grid_spec=pltpu.PrefetchScalarGridSpec(
            num_scalar_prefetch=1,
            grid=(steps // 4, 4),
            in_specs=[
                pl.BlockSpec((T, px.shape[1]), here),
                pl.BlockSpec((8, width + 2 * N), before),
                pl.BlockSpec((rows, LANES), lambda s, k, order: (0, (width + 2 * N) // LANES)),
            ]
            + [whole_spec(m) for m in small],
            out_specs=[
                pl.BlockSpec((T, width), here),
                pl.BlockSpec((T, width), here),
                pl.BlockSpec((1, N, width), lambda s, k, order: (s * 4 + k, 0, 0)),
                pl.BlockSpec((1, 8, T), lambda s, k, order: (order[s * 4 + k], 0, 0)),
                pl.BlockSpec((steps, 3 * HP, T), whole),
                pl.BlockSpec((steps, T, LANES), whole),
            ],
            scratch_shapes=[pltpu.VMEM((N, width), f32)],
        ),
        out_shape=[
            pltpu.HBM((rows, width), bf16),
            pltpu.HBM((rows, width), f32),
            pltpu.HBM((steps, N, width), bf16),
            jax.ShapeDtypeStruct((steps, 8, T), f32),
            pltpu.HBM((steps, 3 * HP, T), f32),
            pltpu.HBM((steps, T, LANES), bf16),
        ],
        compiler_params=pltpu.CompilerParams(vmem_limit_bytes=40 * 2**20),
        cost_estimate=pl.CostEstimate(flops=12 * 10**9, bytes_accessed=14 * 2**20, transcendentals=5 * 10**6),
        name="scan_forward",
    )(order, *hbm(px, px, px), *small[:5], *hbm(*small[5:]))


def scan_backward(order, px, y, states, d_out, stats, row_steps, col_steps, layer, fixed_arrays):
    rows, width = y.shape
    steps = rows // T
    here = lambda s, k, order: (order[s * 4 + 3 - k], 0)
    before = lambda s, k, order: (order[s * 4 + jnp.maximum(2 - k, 0)] * (T // 8) + (T // 8 - 1), 0)
    small = (row_steps, col_steps, layer["taps_x"], layer["taps_bc"], layer["heads"], layer["skip"], layer["gain"])
    small = small + fixed_arrays
    fixed = lambda s, k, order: (0, 0)
    return pl.pallas_call(
        bwd_kernel,
        grid_spec=pltpu.PrefetchScalarGridSpec(
            num_scalar_prefetch=1,
            grid=(steps // 4, 4),
            in_specs=[
                pl.BlockSpec((T, px.shape[1]), here),
                pl.BlockSpec((8, width + 2 * N), before),
                pl.BlockSpec((T, width), here),
                pl.BlockSpec((1, N, width), lambda s, k, order: (s * 4 + 3 - k, 0, 0)),
                pl.BlockSpec((T, width), here),
                pl.BlockSpec((1, 8, T), lambda s, k, order: (order[s * 4 + 3 - k], 0, 0)),
            ]
            + [whole_spec(m) for m in small],
            out_specs=[
                pl.BlockSpec((4 * T, px.shape[1]), lambda s, k, order: (s, 0)),
                pl.BlockSpec((8, width), fixed),
                pl.BlockSpec((8, 2 * N), fixed),
                pl.BlockSpec((2 * HP, T), fixed),
            ],
            scratch_shapes=[
                pltpu.VMEM((N, width), f32),
                pltpu.VMEM((8, width), f32),
                pltpu.VMEM((8, 2 * N), f32),
                pltpu.VMEM((T, T), f32),
                pltpu.VMEM((4 * T, LANES), f32),
                pltpu.VMEM((56, width), f32),
                pltpu.VMEM((40, 2 * N), f32),
            ],
        ),
        out_shape=[
            pltpu.HBM((rows, px.shape[1]), bf16),
            jax.ShapeDtypeStruct((8, width), f32),
            jax.ShapeDtypeStruct((8, 2 * N), f32),
            jax.ShapeDtypeStruct((2 * HP, T), f32),
        ],
        compiler_params=pltpu.CompilerParams(vmem_limit_bytes=40 * 2**20),
        cost_estimate=pl.CostEstimate(flops=24 * 10**9, bytes_accessed=24 * 2**20, transcendentals=10**7),
        name="scan_backward",
    )(order, *hbm(px, px, y, states, d_out), stats, *hbm(*small[:2]), *small[2:7], *hbm(*small[7:]))


def dots_kernel(do, w_out, og, d_ref, dots_ref):
    d_ref[...] = dot_nn(do[...], w_out[...])
    for c in range(do.shape[0] // T):
        at = slice(c * T, (c + 1) * T)
        total = jnp.zeros((T, LANES), f32)
        for p in range(0, og.shape[1], LANES):
            total = total + d_ref[at, p : p + LANES] * og[at, p : p + LANES].astype(f32)
        dots_ref[c] = jnp.broadcast_to(jnp.sum(jnp.transpose(total), axis=0, keepdims=True), (8, T))


def rows_and_dots(do, w_out, og):
    rows, width = og.shape
    size = rows // 2
    return pl.pallas_call(
        dots_kernel,
        grid=(2,),
        in_specs=[
            pl.BlockSpec((size, do.shape[1]), lambda i: (i, 0)),
            pl.BlockSpec(w_out.shape, lambda i: (0, 0), pipeline_mode=pl.Buffered(1)),
            pl.BlockSpec((size, width), lambda i: (i, 0)),
        ],
        out_specs=[
            pl.BlockSpec((size, width), lambda i: (i, 0)),
            pl.BlockSpec((size // T, 8, T), lambda i: (i, 0, 0)),
        ],
        out_shape=[pltpu.HBM((rows, width), f32), jax.ShapeDtypeStruct((rows // T, 8, T), f32)],
        compiler_params=pltpu.CompilerParams(vmem_limit_bytes=40 * 2**20),
        cost_estimate=pl.CostEstimate(flops=4 * 10**9, bytes_accessed=10 * 2**20, transcendentals=0),
        name="rows_and_dots",
    )(*hbm(do, w_out, og))


def rows_kernel(rows, w, *outs):
    product = dot_nt(rows[...], w[...]).astype(bf16)
    size = product.shape[0] // len(outs)
    for i, out in enumerate(outs):
        out[...] = product[i * size : (i + 1) * size]


def rows_product(rows, w):
    count, size = rows.shape[0], rows.shape[0] // 4
    wide = w.shape[0] // 3
    return pl.pallas_call(
        rows_kernel,
        grid=(3,),
        in_specs=[
            pl.BlockSpec(rows.shape, lambda i: (0, 0), pipeline_mode=pl.Buffered(1)),
            pl.BlockSpec((wide, w.shape[1]), lambda i: (i, 0)),
        ],
        out_specs=[pl.BlockSpec((size, wide), lambda i: (0, i))] * 4,
        out_shape=[jax.ShapeDtypeStruct((size, w.shape[0]), bf16)] * 4,
        compiler_params=pltpu.CompilerParams(vmem_limit_bytes=40 * 2**20),
        cost_estimate=pl.CostEstimate(
            flops=4 * count * w.shape[0] * w.shape[1], bytes_accessed=2 * (rows.size + w.size), transcendentals=0
        ),
        name="rows_product",
    )(*hbm(rows, w))


def fixed_tables(width):
    heads = width // P_SIZE
    column, lane = np.indices((LANES, heads * LANES))
    spread_run = (column < 3 * HP) & (column % HP == lane // LANES)
    column, lane = np.indices((LANES, width))
    spread_steps = (column >= 3 * HP) & (column < 6 * HP) & (column % HP == lane // P_SIZE)
    feature, target = np.indices((4 * width, LANES))
    part, head = (feature // LANES) % 4, 2 * (feature // (4 * LANES)) + (feature % LANES) // P_SIZE
    sums = target == np.array([0, 0, 1, 2])[part] * HP + head
    return tuple(jnp.asarray(m, bf16) for m in (spread_run, spread_steps, sums))


tied = lax.optimization_barrier


def swap(value, axis):
    return lax.ppermute(value, axis, [(0, 1), (1, 0)])


AXES = (("section", "tensor"), ("tensor", "section"))


def spread_first(value):
    return [swap(value[s], axes[0]) for s, axes in enumerate(AXES)]


def join_first(value, received):
    return [jnp.concatenate([value[s], received[s]], axis=0) for s in range(len(AXES))]


def spread_second(twos):
    return [swap(two, axes[1]) for two, axes in zip(twos, AXES)]


def join_second(twos, received):
    return jnp.concatenate([part for pair in zip(twos, received) for part in pair], axis=0)


def spread_all(*values):
    received = tied([spread_first(value) for value in values])
    twos = [join_first(value, r) for value, r in zip(values, received)]
    received = tied([spread_second(pair) for pair in twos])
    return [join_second(pair, r) for pair, r in zip(twos, received)]


def local(
    block_input,
    plan,
    lengths,
    norm_gain,
    gate_proj,
    value_proj,
    shared_proj,
    step_proj,
    conv_value,
    conv_shared,
    head_params,
    gate_gain,
    out_proj,
    cotangent,
):
    x = lax.axis_index("section")
    yy = lax.axis_index("tensor")
    streams = block_input.shape[1]
    model_width = block_input.shape[3]
    width = gate_proj.shape[2] // 2
    head_count = step_proj.shape[2] // 2
    rows_here = gate_proj.shape[1]

    def both(value):
        other = swap(value, "section")
        return jnp.where(x == 0, value, other), jnp.where(x == 0, other, value)

    def quarters(value):
        size = value.shape[-1] // 2
        axis = value.ndim - 1
        kept = lax.dynamic_slice_in_dim(value, x * size, size, axis)
        other = swap(lax.dynamic_slice_in_dim(value, (1 - x) * size, size, axis), "section")
        return jnp.where(x == 0, kept, other), jnp.where(x == 0, other, kept)

    shared_other = swap(shared_proj[0], "tensor")
    shared_full = jnp.where(
        yy == 0,
        jnp.concatenate([shared_proj[0], shared_other], axis=1),
        jnp.concatenate([shared_other, shared_proj[0]], axis=1),
    )

    def quarter_of(value, which):
        return lax.dynamic_slice_in_dim(value, which * (value.shape[1] // 2), value.shape[1] // 2, 1)

    def packed_in(which):
        steps = jnp.pad(quarter_of(step_proj[0], which), ((0, 0), (0, LANES - head_count)))
        return jnp.concatenate([steps, quarter_of(value_proj[0], which), quarter_of(gate_proj[0], which)], axis=1)

    in_kept, in_other = packed_in(x), swap(packed_in(1 - x), "section")
    shared_section = swap(shared_full, "section")
    out_kept, out_other = quarter_of(out_proj[0], x), swap(quarter_of(out_proj[0], 1 - x), "section")
    weights = []
    for l in range(2):
        shared_l = jnp.where(x == l, shared_full, shared_section)
        rest = jnp.where(x == l, in_kept, in_other)
        packed = jnp.concatenate(
            [rest[:, LANES : LANES + width], shared_l, rest[:, :LANES], rest[:, LANES + width :]], axis=1
        )
        weights.append(
            (
                lax.all_gather(packed, "dp", axis=0, tiled=True),
                lax.all_gather(jnp.where(x == l, out_kept, out_other), "dp", axis=0, tiled=True),
            )
        )

    taps_x_two = quarters(jnp.pad(conv_value[0], ((0, 3), (0, 0))))
    shared_taps_other = swap(conv_shared[0], "tensor")
    taps_bc_full = jnp.where(
        yy == 0,
        jnp.concatenate([conv_shared[0], shared_taps_other], axis=1),
        jnp.concatenate([shared_taps_other, conv_shared[0]], axis=1),
    )
    taps_bc_two = both(jnp.pad(taps_bc_full, ((0, 3), (0, 0))))
    heads_two = quarters(head_params[0])
    gain_two = quarters(gate_gain)
    norm_two = both(norm_gain)
    layers = []
    for l in range(2):
        head_rows = heads_two[l]
        columns_of = jnp.stack([head_rows[0], -jnp.exp(head_rows[1])], axis=1)
        layers.append(
            dict(
                taps_x=taps_x_two[l],
                taps_bc=taps_bc_two[l],
                heads=jnp.pad(columns_of, ((0, HP - head_count), (0, LANES - 2))),
                skip=jnp.repeat(head_rows[2], P_SIZE)[None],
                gain=gain_two[l],
                norm=norm_two[l],
                decay=columns_of[:, 1],
            )
        )
    tables = fixed_tables(width)

    chunk = jnp.arange(4, dtype=jnp.int32)
    x_bit, y_bit = (chunk & 1) ^ x, (chunk >> 1) ^ yy
    order = jnp.concatenate([2 * y_bit + x_bit, 4 + 2 * x_bit + y_bit]).astype(jnp.int32)

    def own_rows(value):
        half = value.shape[1] // 2
        return lax.dynamic_slice_in_dim(value, x * half, half, 1)

    first_rows = (2 * yy + x) * T
    positions = first_rows + lax.broadcasted_iota(jnp.int32, (T, 1), 0)
    valid = jnp.sum(jnp.where(plan[0][:, None] == jnp.arange(streams)[None, :], lengths[0][:, None], 0), axis=0)
    keep = (positions[None] < valid[:, None, None]).astype(f32)
    u = own_rows(block_input[0]).astype(f32)
    top = own_rows(cotangent[0]).astype(f32) * keep

    size = 4 * T

    def send_half(parts):
        return [swap(parts[2 * s + 1], AXES[s][1]) for s in range(streams)]

    def add_half(parts, received):
        return [parts[2 * s].astype(f32) + received[s].astype(f32) for s in range(streams)]

    def send_quarter(twos, kind):
        return [swap(two[size // 4 :].astype(kind), AXES[s][0]) for s, two in enumerate(twos)]

    def add_quarter(twos, received):
        return jnp.stack([two[: size // 4] + other.astype(f32) for two, other in zip(twos, received)])

    saved = []
    for l in range(2):
        w_in, w_out = weights[l]
        layer = layers[l]
        rho = lax.rsqrt(jnp.mean(u * u, axis=2, keepdims=True) + eps)
        a_own = (u * rho * layer["norm"][None]).astype(bf16)
        (a,) = spread_all(a_own)
        if l == 0:
            top_rounded, a = tied((top.astype(bf16), a))
            top_received = spread_first(top_rounded)
        pre = dot_nn(a, w_in)
        if l == 0:
            pre, top_received = tied((pre, top_received))
            top_twos = join_first(top_rounded, top_received)
            top_received = spread_second(top_twos)
        og, y, states, squares, row_steps, col_steps = scan_forward(order, pre, layer, tables)
        if l == 1:
            og, do_top = tied((og, do_top))
        sq = squares[:, 0, :]
        saved.append((u, rho, a, pre, og, y, states, sq, row_steps, col_steps))
        if l == 0:
            o_part, sq_part = rows_product(og, w_out), list(sq.reshape(4, size // 2))
            o_part, top_received = tied((o_part, top_received))
            do_top = join_second(top_twos, top_received)
            received = send_half(o_part)
            twos = add_half(o_part, received)
            sq_twos = add_half(sq_part, send_half(sq_part))
            o = add_quarter(twos, send_quarter(twos, bf16))
            total = add_quarter(sq_twos, send_quarter(sq_twos, f32))[:, :, None]
            r_first = lax.rsqrt(total / DI + eps)
            o_first = o * r_first
            u = u + o_first

    def summed_rows(rows_sums):
        count = rows_sums.shape[0]
        total = rows_sums.reshape(count, streams, 2, 2, T)
        for flips, pairs in (((1, 0), (2, 3, 0, 1)), ((0, 1), (1, 0, 3, 2)), ((1, 1), (3, 2, 1, 0))):
            other = lax.ppermute(rows_sums, ("section", "tensor"), list(enumerate(pairs)))
            other = other.reshape(count, streams, 2, 2, T)
            turned = []
            for s in range(streams):
                piece = other[:, s]
                for axis in (0, 1):
                    if flips[0 if AXES[s][axis] == "section" else 1]:
                        piece = jnp.flip(piece, axis=2 - axis)
                turned.append(piece)
            total = total + jnp.stack(turned, axis=1)
        return total.reshape(count, -1)

    def rows_of_stats(scale, stat):
        pair = jnp.stack([scale.reshape(-1, T), stat.reshape(-1, T)], axis=1)
        return jnp.pad(pair, ((0, 0), (0, 6), (0, 0)))

    u, rho, a, pre, og, y, states, sq, row_steps, col_steps = saved[1]
    d_out, dots = rows_and_dots(do_top, weights[1][1], og)
    square_sums, dots = tied((summed_rows(sq.reshape(1, -1)), dots[:, 0, :].reshape(-1)))
    r_last = lax.rsqrt(square_sums[0] / DI + eps)
    scaled_og = (og.astype(f32) * r_last[:, None]).astype(bf16)
    grad_out_last = dot_tn(do_top, scaled_og).astype(bf16)
    dot_sums, grad_out_last = tied((summed_rows(dots[None]), grad_out_last))
    stats_last = rows_of_stats(r_last, r_last**3 * dot_sums[0] / DI)

    shards = [None, None]

    def pack(acc_x, acc_bc, acc_dt, da_part, a, layer):
        norm = sum(
            jnp.sum(part.astype(f32) * a[i * part.shape[0] : (i + 1) * part.shape[0]].astype(f32), axis=0)
            for i, part in enumerate(da_part)
        ) / layer["norm"][0]
        return jnp.concatenate([acc_x.reshape(-1), acc_bc.reshape(-1), jnp.sum(acc_dt, axis=1), norm])

    def sum_steps():
        devices = lax.axis_size("dp")
        same = lambda value: value
        if devices & (devices - 1):
            return [lambda value: jnp.sum(lax.all_gather(value, "dp", axis=0), axis=0), same, same]

        def add_other(value, step):
            return value + lax.ppermute(value, "dp", [(i, i ^ step) for i in range(devices)])

        steps = [functools.partial(add_other, step=1 << i) for i in range(devices.bit_length() - 1)]
        return steps + [same] * max(0, 3 - len(steps))

    def input_gradient(l, dv, da):
        u, rho = saved[l][0], saved[l][1]
        scaled = da * layers[l]["norm"][None]
        return dv + rho * scaled - u * rho**3 * jnp.mean(scaled * u, axis=2, keepdims=True)

    shard_out = lax.psum_scatter(grad_out_last, "dp", scatter_dimension=0, tiled=True)
    d_pre, acc_x, acc_bc, acc_dt = scan_backward(
        order, pre, y, states, d_out, stats_last, row_steps, col_steps, layers[1], tables
    )
    da_part = rows_product(d_pre, weights[1][0])
    d_pre, da_part = tied((d_pre, da_part))
    grad_in = dot_tn(a, d_pre).astype(bf16)
    small_last = pack(acc_x, acc_bc, acc_dt, da_part, a, layers[1])
    received, grad_after, small_last, shard_out, og = tied(
        (send_half(da_part), grad_in, small_last, shard_out, og)
    )
    o_part = rows_product(og, weights[1][1])
    small_last = small_last + 0.0 * grad_after[0, 0].astype(f32)
    twos = add_half(da_part, received)
    da = add_quarter(twos, send_quarter(twos, bf16))
    shards[1] = (shard_out, lax.psum_scatter(grad_in, "dp", scatter_dimension=0, tiled=True))
    dv = input_gradient(1, top, da)

    do_own = (dv * r_first).astype(bf16)
    kappa = r_first[:, :, 0] ** 2 * jnp.sum(dv * o_first, axis=2) / DI
    do, stat = spread_all(do_own, kappa)
    do, o_part = tied((do, o_part))
    u, rho, a, pre, og, y, states, sq, row_steps, col_steps = saved[0]
    w_in, w_out = weights[0]
    stats = rows_of_stats(jnp.ones_like(stat), stat)
    d_out = dot_nn(do, w_out)
    do, d_out = tied((do, d_out))
    grad_out = dot_tn(do, og).astype(bf16)
    grad_out, shards[1] = tied((grad_out, shards[1]))
    d_out, grad_out = tied((d_out, grad_out))
    shard_out = lax.psum_scatter(grad_out, "dp", scatter_dimension=0, tiled=True)
    d_pre, acc_x, acc_bc, acc_dt = scan_backward(
        order, pre, y, states, d_out, stats, row_steps, col_steps, layers[0], tables
    )
    d_pre, o_received = tied((d_pre, send_half(o_part)))
    o_twos = add_half(o_part, o_received)
    grad_in = dot_tn(a, d_pre).astype(bf16)
    d_pre, grad_in = tied((d_pre, grad_in))
    da_part = rows_product(d_pre, w_in)
    da_part, o_received, shard_out = tied((da_part, send_quarter(o_twos, bf16), shard_out))
    r_own = jnp.stack([r_last[s * size : s * size + T] for s in range(streams)])
    final = saved[1][0] + add_quarter(o_twos, o_received) * r_own[:, :, None]
    small = jnp.stack([pack(acc_x, acc_bc, acc_dt, da_part, a, layers[0]), small_last])
    received, small = tied((send_half(da_part), small))
    twos = add_half(da_part, received)
    steps = sum_steps()
    received, small = tied((send_quarter(twos, bf16), steps[0](small)))
    da = add_quarter(twos, received)
    dv = input_gradient(0, dv, da)
    shard_in = lax.psum_scatter(grad_in, "dp", scatter_dimension=0, tiled=True)
    ends_other = swap(jnp.where(x == 0, final, dv).astype(bf16), "section")
    for step in steps[1:]:
        small = step(small)

    partners = ((2, 3, 0, 1), (1, 0, 3, 2), (3, 2, 1, 0))

    def mine_and_partners(first, last):
        return jnp.where(x == 0, first, last), jnp.where(x == 0, last, first)

    kept, sent = mine_and_partners(small[0], small[1])
    other = swap(sent, "section")
    of_section = jnp.stack(mine_and_partners(kept, other))
    other = swap(of_section, "tensor")

    out_kept, out_sent = mine_and_partners(shard_out, shards[1][0])
    out_other = swap(out_sent, "section")
    mine = jnp.stack([jnp.where(yy == 0, of_section, other), jnp.where(yy == 0, other, of_section)], axis=1)
    mine = mine.reshape(4, -1)
    end_x, end_bc = 8 * width, 8 * width + 8 * 2 * N
    end_dt = end_bc + 2 * HP
    over_all = jnp.sum(mine, axis=0)
    halves = lax.dynamic_index_in_dim(mine.reshape(2, 2, -1), yy, 1, keepdims=False)
    by_x = halves[:, :end_x].reshape(2, 8, width).transpose(1, 0, 2).reshape(8, 2 * width)
    by_dt = halves[:, end_bc:end_dt].reshape(2, 2, HP)[:, :, :head_count].transpose(1, 0, 2).reshape(2, 2 * head_count)
    grad_conv_value = by_x[:5]
    grad_gate_gain = by_x[5]
    grad_skip = jnp.sum(by_x[6].reshape(2 * head_count, P_SIZE), axis=1)
    grad_heads = jnp.stack([by_dt[1], by_dt[0] * -jnp.exp(head_params[0, 1]), grad_skip])
    bc_all = over_all[end_x:end_bc].reshape(8, 2 * N)[:5]
    grad_conv_shared = lax.dynamic_slice_in_dim(bc_all, yy * N, N, 1)
    grad_norm = over_all[end_dt:]

    mine = jnp.where(x == 0, dv, final)
    other = ends_other.astype(f32)
    relay = jnp.concatenate([jnp.where(x == 0, mine, other), jnp.where(x == 0, other, mine)], axis=1)
    grad_out = jnp.concatenate(mine_and_partners(out_kept, out_other), axis=1).astype(f32)

    done = (relay, grad_out, grad_norm, grad_conv_value, grad_conv_shared, grad_heads, grad_gate_gain)
    shard_in, done = tied((shard_in, done))
    relay, grad_out, grad_norm, grad_conv_value, grad_conv_shared, grad_heads, grad_gate_gain = done
    in_kept, in_sent = mine_and_partners(shard_in, shards[1][1])
    bc_at, dt_at, z_at = width, width + 2 * N, width + 2 * N + LANES

    def half_of(value, which):
        return lax.dynamic_slice_in_dim(value, bc_at + which * N, N, 1)

    in_other = swap(in_sent, "section")
    bc_tensor = swap(half_of(in_kept, 1 - yy), "tensor")
    bc_diagonal = lax.ppermute(half_of(in_sent, 1 - yy), ("section", "tensor"), list(enumerate(partners[2])))
    in_other, bc_tensor, bc_diagonal = tied((in_other, bc_tensor, bc_diagonal))

    def both_halves(first, last):
        return jnp.concatenate(mine_and_partners(in_kept[:, first:last], in_other[:, first:last]), axis=1).astype(f32)

    grad_value = both_halves(0, width)
    grad_gate = both_halves(z_at, z_at + width)
    grad_step = both_halves(dt_at, dt_at + head_count)
    grad_shared = sum(
        part.astype(f32) for part in (half_of(in_kept, yy), half_of(in_other, yy), bc_tensor, bc_diagonal)
    )

    return (
        relay[None, None],
        grad_norm[None],
        grad_gate[None],
        grad_value[None],
        grad_shared[None],
        grad_step[None],
        grad_conv_value[None],
        grad_conv_shared[None],
        grad_heads[None],
        grad_gate_gain[None],
        grad_out[None],
    )


def solution(mesh):
    placed = (
        P("dp", None, "tensor", None),
        P("dp", None),
        P("dp", None),
        P("section", None),
        P("section", "dp", "tensor"),
        P("section", "dp", "tensor"),
        P("section", "dp", "tensor"),
        P("section", "dp", "tensor"),
        P("section", None, "tensor"),
        P("section", None, "tensor"),
        P("section", None, "tensor"),
        P("section", "tensor"),
        P("section", "dp", "tensor"),
        P("dp", None, "tensor", None),
    )
    return jax.shard_map(
        local,
        mesh=mesh,
        in_specs=placed,
        out_specs=(
            P("section", "dp", None, "tensor", None),
            P("section", None),
            P("section", "dp", "tensor"),
            P("section", "dp", "tensor"),
            P("section", "dp", "tensor"),
            P("section", "dp", "tensor"),
            P("section", None, "tensor"),
            P("section", None, "tensor"),
            P("section", None, "tensor"),
            P("section", "tensor"),
            P("section", "dp", "tensor"),
        ),
        check_vma=False,
    )
```

time: 743 us -> 524 us (0.71)
  waiting for transfers between devices: 298 us -> 171 us
  matrix products: 105 us -> 57 us
  local copies, waits for them, and re-layouts: 70.9 us -> 32.1 us
  blocking collectives: 26.7 us -> 0 us
  Pallas kernels: 95.3 us -> 121 us
  other arithmetic: 55.6 us -> 41.5 us
  starting transfers between devices: 71 us -> 78.9 us
    reduce_scatter x6 -> x4, waiting for transfers between devices: 66.3 us -> 0.03 us  [the longest x1 0.02 us: local(): lax.psum_scatter(grad_out, 'dp', scatter_dimension=0, tiled=True)]
    ppermute x65 -> x56, waiting for transfers between devices: 185 us -> 144 us  [swap(): return lax.ppermute(value, axis, [(0, 1), (1, 0)])]
    pallas_call x0 -> x5, Pallas kernels: none -> 38.3 us  [the longest x4 31.6 us: rows_product(): pl.pallas_call(rows_kernel, grid=(3,), in_specs=[pl.BlockSpec(rows.shape,...]
    psum x1 -> x0, waiting for transfers between devices: 37.3 us -> none  [local(): shared_sums = lax.psum(shared_sums, ('section', 'tensor'))]
    unnamed x235 -> x141, local copies, waits for them, and re-layouts: 45.5 us -> 17.8 us
    dot_general x6 -> x0, matrix products: 26.7 us -> none  [dot_nt(): lax.dot_general(a, b, (((1,), (1,)), ((), ())), preferred_element_type=f32)]
    all_gather x2 -> x0, blocking collectives: 26.7 us -> none  [the longest x1 17.3 us: local(): packed = jnp.sum(lax.all_gather(packed, 'dp', axis=0), axis=0)]
    ppermute x0 -> x10, waiting for transfers between devices: none -> 17.6 us  [the longest x3 11 us: add_other(): lax.ppermute(value, 'dp', [(i, i ^ step) for i in range(devices)])]
  transfers between devices with their start and end apart: 78 -> 74, of which waited for: 37 -> 37; matrix products, arithmetic and copies ran while one was open for 24% -> 21% of each run, Pallas kernels for 8% -> 23%
where the time goes in v2:
time: 524 us; the launch traced here: 518 us
  waiting for transfers between devices  171 us (33%)
  Pallas kernels  121 us (23%)
  starting transfers between devices  78.9 us (15%)
  matrix products  57 us (11%)
  other arithmetic  41.5 us (8%)
  local copies, waits for them, and re-layouts  32.1 us (6%)
  between operations  16.6 us (3%)
    ppermute x56, waiting for transfers between devices, swap(): return lax.ppermute(value, axis, [(0, 1), (1, 0)])  144 us
    ppermute x56, starting transfers between devices, swap(): return lax.ppermute(value, axis, [(0, 1), (1, 0)])  63.7 us
    pallas_call x2, Pallas kernels, scan_backward(): pl.pallas_call(bwd_kernel, grid_spec=pltpu.PrefetchScalarGridSpec(num_sca...  54.1 us
    pallas_call x4, Pallas kernels, rows_product(): pl.pallas_call(rows_kernel, grid=(3,), in_specs=[pl.BlockSpec(rows.shape,...  31.6 us
    dot_general x4, matrix products, dot_tn(): lax.dot_general(a, b, (((0,), (0,)), ((), ())), preferred_element_type=f32)  28.7 us
    pallas_call x2, Pallas kernels, scan_forward(): pl.pallas_call(fwd_kernel, grid_spec=pltpu.PrefetchScalarGridSpec(num_sca...  28.5 us
    dot_general x3, matrix products, dot_nn(): lax.dot_general(a, b, (((1,), (0,)), ((), ())), preferred_element_type=f32)  28.3 us
    unnamed x141, local copies, waits for them, and re-layouts  17.8 us
  transfers between devices with their start and end apart: 74, of which 37 were waited for; matrix products, arithmetic and copies ran while one was open for 21% of the time, Pallas kernels for 23%

profile of v2, /device:TPU:0, one launch (start us, length us, event | category | flops | bytes accessed | tf_op | source)
XLA Modules:
  0.0 518.2 jit_solution(11635593969072474930)
XLA Ops:
  17.0 12.1 %collective-permute-done.7 = bf16[192,256]{1,0:T(8,128)(2,1)S(1)} collective-permute-done((bf16[192,256]{1,0:T(8,128)(2,1)S(1)}, bf16[192,256]{1,0:T(8,128)(2,1)S(1)}, u32[]{:S(2)}, u32[]{:S(2)}) %collective-permute-start.7) | collective-permute-done | bytes 98336 | tf_op jit(solution)/shard_map/ppermute | solution.py:523
  32.3 6.5 %collective-permute-done.15 = bf16[192,768]{1,0:T(8,128)(2,1)S(1)} collective-permute-done((bf16[192,768]{1,0:T(8,128)(2,1)S(1)}, bf16[192,768]{1,0:T(8,128)(2,1)S(1)}, u32[]{:S(2)}, u32[]{:S(2)}) %collective-permute-start.15) | collective-permute-done | bytes 294944 | tf_op jit(solution)/shard_map/ppermute | solution.py:523
  52.9 4.5 collective-permute-done.2
  65.1 10.3 %collective-permute-done.4 = bf16[256,1536]{1,0:T(8,128)(2,1)} collective-permute-done((bf16[256,1536]{1,0:T(8,128)(2,1)}, bf16[256,1536]{1,0:T(8,128)(2,1)}, u32[]{:S(2)}, u32[]{:S(2)}) %collective-permute-start.4) | collective-permute-done | bytes 786464 | tf_op jit(solution)/shard_map/ppermute | solution.py:523
  83.7 9.8 %all-gather.5.cloned.1.call-done.w = bf16[1536,1920]{1,0:T(8,128)(2,1)} async-done(((bf16[192,1920]{1,0:T(8,128)(2,1)}), bf16[1536,1920]{1,0:T(8,128)(2,1)}) %all-gather.5.cloned.1.call-update) | async-done | bytes 5898256 | tf_op jit(solution)/shard_map/all_gather | solution.py:613
  93.5 12.1 %fusion.54.px.halo.pre_dt = f32[1024,1920]{1,0:T(8,128)} fusion(bf16[1024,1536]{1,0:T(8,128)(2,1)} %constant_dynamic-update-slice_fusion, bf16[1536,1920]{1,0:T(8,128)(2,1)} %all-gather.5.cloned.1.call-done.w), kind=kOutput, calls=%fused_computation.289 | convolution fusion | flops 6039797760 | bytes 16908288 | tf_op jit(solution)/shard_map/dot_general | solution.py:23
  110.5 14.3 %scan_forward.2 = (bf16[1024,768]{1,0:T(8,128)(2,1)}, f32[1024,768]{1,0:T(8,128)}, bf16[8,128,768]{2,1,0:T(8,128)(2,1)}, f32[8,8,128]{2,1,0:T(8,128)S(1)}, f32[8...) custom-call(s32[8]{0:T(128)S(1)} %pad_add_fusion.order, f32[1024,1920]{1,0:T(8,128)} %fusion.54.px.halo.pre_dt, ...), custom_call_target="tpu_custom_call" | custom-call | flops 12000000000 | bytes 14680064 | tf_op jit(solution)/shard_map/scan_forward/pallas_call | solution.py:363
  125.9 5.1 rows_product.4
  137.9 15.0 %collective-permute-done.18 = bf16[256,1536]{1,0:T(8,128)(2,1)S(1)} collective-permute-done((bf16[256,1536]{1,0:T(8,128)(2,1)S(1)}, bf16[256,1536]{1,0:T(8,128)(2,1)S(1)}, u32[]{:S(2)}, u32[]{:S(2)}) %collective-permute-start.18) | collective-permute-done | bytes 786464 | tf_op jit(solution)/shard_map/ppermute | solution.py:523
  155.1 7.6 %collective-permute-done.19 = bf16[128,1536]{1,0:T(8,128)(2,1)S(1)} collective-permute-done((bf16[128,1536]{1,0:T(8,128)(2,1)S(1)}, bf16[128,1536]{1,0:T(8,128)(2,1)S(1)}, u32[]{:S(2)}, u32[]{:S(2)}) %collective-permute-start.19) | collective-permute-done | bytes 393248 | tf_op jit(solution)/shard_map/ppermute | solution.py:523
  167.4 6.2 %collective-permute-done.27 = bf16[128,1536]{1,0:T(8,128)(2,1)S(1)} collective-permute-done((bf16[128,1536]{1,0:T(8,128)(2,1)S(1)}, bf16[128,1536]{1,0:T(8,128)(2,1)S(1)}, u32[]{:S(2)}, u32[]{:S(2)}) %collective-permute-start.27) | collective-permute-done | bytes 393248 | tf_op jit(solution)/shard_map/ppermute | solution.py:523
  180.0 11.2 %collective-permute-done.29 = bf16[256,1536]{1,0:T(8,128)(2,1)S(1)} collective-permute-done((bf16[256,1536]{1,0:T(8,128)(2,1)S(1)}, bf16[256,1536]{1,0:T(8,128)(2,1)S(1)}, u32[]{:S(2)}, u32[]{:S(2)}) %collective-permute-start.29) | collective-permute-done | bytes 786464 | tf_op jit(solution)/shard_map/ppermute | solution.py:523
  196.0 11.8 %fusion.55.px.halo.pre_dt = f32[1024,1920]{1,0:T(8,128)} fusion(bf16[1024,1536]{1,0:T(8,128)(2,1)} %constant_dynamic-update-slice_fusion.6, bf16[1536,1920]{1,0:T(8,128)(2,1)} %all-gather.9.cloned.1.call-done.w), kind=kOutput, calls=%fused_computation.290 | convolution fusion | flops 6039797760 | bytes 16908288 | tf_op jit(solution)/shard_map/dot_general | solution.py:23
  207.9 14.2 %scan_forward.3 = (bf16[1024,768]{1,0:T(8,128)(2,1)}, f32[1024,768]{1,0:T(8,128)}, bf16[8,128,768]{2,1,0:T(8,128)(2,1)}, f32[8,8,128]{2,1,0:T(8,128)S(1)}, f32[8...) custom-call(s32[8]{0:T(128)S(1)} %pad_add_fusion.order, f32[1024,1920]{1,0:T(8,128)} %fusion.55.px.halo.pre_dt, ...), custom_call_target="tpu_custom_call" | custom-call | flops 12000000000 | bytes 14680064 | tf_op jit(solution)/shard_map/scan_forward/pallas_call | solution.py:363
  225.6 6.6 %rows_and_dots.1 = (f32[1024,768]{1,0:T(8,128)}, f32[8,8,128]{2,1,0:T(8,128)S(1)}) custom-call(bf16[1024,1536]{1,0:T(8,128)(2,1)} %copy-done.35, bf16[1536,768]{1,0:T(8,128)(2,1)} %all-gather.11.cloned.1.call-done.w_out.w, bf16[1024,768]{1,0:T(8,128)(2,1)} %get-tuple-element.196.og.rows), custom_call_target="tpu_custom_call" | custom-call | flops 4000000000 | bytes 10485760 | tf_op jit(solution)/shard_map/rows_and_dots/pallas_call | solution.py:461
  232.5 5.8 %convolution_convert_fusion.3 = bf16[1536,768]{1,0:T(8,128)(2,1)} fusion(bf16[1024,1536]{1,0:T(8,128)(2,1)S(1)} %copy-done.36, bf16[1024,768]{1,0:T(8,128)(2,1)} %get-tuple-element.196.og.rows, f32[1024]{0:T(1024)S(1)} %bitcast.277), kind=kOutput, calls=%fused_computation.3 | convolution fusion | flops 2419458048 | bytes 7081984 | tf_op jit(solution)/shard_map/dot_general | solution.py:31
  244.6 26.9 %scan_backward.2 = (bf16[1024,1920]{1,0:T(8,128)(2,1)}, f32[8,768]{1,0:T(8,128)S(1)}, f32[8,256]{1,0:T(8,128)S(1)}, f32[32,128]{1,0:T(8,128)S(1)}) custom-call(s32[8]{0:T(128)S(1)} %pad_add_fusion.order, f32[1024,1920]{1,0:T(8,128)} %fusion.55.px.halo.pre_dt, f32[1024,1920]{1,0:T(8,128)} %fusion.55.px.halo.pre_dt, f32[1024,768]{1,0:T(8,128)} %get-tuple-element.159.y_ref, ...), custom_call_target="tpu_custom_call" | custom-call | flops 24000000000 | bytes 25165824 | tf_op jit(solution)/shard_map/scan_backward/pallas_call | solution.py:406
  271.5 10.2 %rows_product.5 = (bf16[256,1536]{1,0:T(8,128)(2,1)S(1)}, bf16[256,1536]{1,0:T(8,128)(2,1)S(1)}, bf16[256,1536]{1,0:T(8,128)(2,1)S(1)}, bf16[256,1536]{1,0:T(8,128)(2,1)S(1)}) custom-call(bf16[1024,1920]{1,0:T(8,128)(2,1)} %get-tuple-element.182.rows, bf16[1536,1920]{1,0:T(8,128)(2,1)} %all-gather.9.cloned.1.call-done.w), custom_call_target="tpu_custom_call" | custom-call | flops 12079595520 | bytes 9830400 | tf_op jit(solution)/shard_map/rows_product/pallas_call | solution.py:490
  281.7 10.4 %convolution_convert_fusion.1 = bf16[1536,1920]{1,0:T(8,128)(2,1)} fusion(bf16[1024,1536]{1,0:T(8,128)(2,1)} %constant_dynamic-update-slice_fusion.6, bf16[1024,1920]{1,0:T(8,128)(2,1)S(1)} %copy-done.53), kind=kOutput, calls=%fused_computation.1 | convolution fusion | flops 6042746880 | bytes 12976128 | tf_op jit(solution)/shard_map/dot_general | solution.py:31
  298.5 7.4 %collective-permute-done.36 = bf16[256,1536]{1,0:T(8,128)(2,1)} collective-permute-done((bf16[256,1536]{1,0:T(8,128)(2,1)S(1)}, bf16[256,1536]{1,0:T(8,128)(2,1)}, u32[]{:S(2)}, u32[]{:S(2)}) %collective-permute-start.36) | collective-permute-done | bytes 786464 | tf_op jit(solution)/shard_map/ppermute | solution.py:523
  315.3 6.1 %rows_product.6 = (bf16[256,1536]{1,0:T(8,128)(2,1)S(1)}, bf16[256,1536]{1,0:T(8,128)(2,1)}, bf16[256,1536]{1,0:T(8,128)(2,1)S(1)}, bf16[256,1536]{1,0:T(8,128)(2,1)S(1)}) custom-call(bf16[1024,768]{1,0:T(8,128)(2,1)} %get-tuple-element.196.og.rows, bf16[1536,768]{1,0:T(8,128)(2,1)} %all-gather.11.cloned.1.call-done.w_out.w), custom_call_target="tpu_custom_call" | custom-call | flops 4831838208 | bytes 3932160 | tf_op jit(solution)/shard_map/rows_product/pallas_call | solution.py:490
  331.7 9.3 %collective-permute-done.41 = bf16[128,1536]{1,0:T(8,128)(2,1)S(1)} collective-permute-done((bf16[128,1536]{1,0:T(8,128)(2,1)S(1)}, bf16[128,1536]{1,0:T(8,128)(2,1)S(1)}, u32[]{:S(2)}, u32[]{:S(2)}) %collective-permute-start.41) | collective-permute-done | bytes 393248 | tf_op jit(solution)/shard_map/ppermute | solution.py:523
  346.9 10.0 %collective-permute-done.47 = f32[256]{0:T(256)S(1)} collective-permute-done((f32[256]{0:T(256)S(1)}, f32[256]{0:T(256)S(1)}, u32[]{:S(2)}, u32[]{:S(2)}) %collective-permute-start.47) | collective-permute-done | bytes 1056 | tf_op jit(solution)/shard_map/ppermute | solution.py:523
  360.6 4.3 fusion.56.d_ref
  370.6 27.2 %scan_backward.3 = (bf16[1024,1920]{1,0:T(8,128)(2,1)}, f32[8,768]{1,0:T(8,128)S(1)}, f32[8,256]{1,0:T(8,128)S(1)}, f32[32,128]{1,0:T(8,128)S(1)}) custom-call(s32[8]{0:T(128)S(1)} %pad_add_fusion.order, f32[1024,1920]{1,0:T(8,128)} %fusion.54.px.halo.pre_dt, f32[1024,1920]{1,0:T(8,128)} %fusion.54.px.halo.pre_dt, f32[1024,768]{1,0:T(8,128)} %get-tuple-element.141.y_ref, ...), custom_call_target="tpu_custom_call" | custom-call | flops 24000000000 | bytes 25165824 | tf_op jit(solution)/shard_map/scan_backward/pallas_call | solution.py:406
  405.8 8.5 %convolution_convert_fusion = bf16[1536,1920]{1,0:T(8,128)(2,1)} fusion(bf16[1024,1536]{1,0:T(8,128)(2,1)S(1)} %copy-done.15, bf16[1024,1920]{1,0:T(8,128)(2,1)S(1)} %copy-done.52), kind=kOutput, calls=%fused_computation | convolution fusion | flops 6042746880 | bytes 12976128 | tf_op jit(solution)/shard_map/dot_general | solution.py:31
  414.4 10.2 %rows_product.7 = (bf16[256,1536]{1,0:T(8,128)(2,1)S(1)}, bf16[256,1536]{1,0:T(8,128)(2,1)S(1)}, bf16[256,1536]{1,0:T(8,128)(2,1)S(1)}, bf16[256,1536]{1,0:T(8,128)(2,1)S(1)}) custom-call(bf16[1024,1920]{1,0:T(8,128)(2,1)} %get-tuple-element.216.rows, bf16[1536,1920]{1,0:T(8,128)(2,1)} %all-gather.5.cloned.1.call-done.w), custom_call_target="tpu_custom_call" | custom-call | flops 12079595520 | bytes 9830400 | tf_op jit(solution)/shard_map/rows_product/pallas_call | solution.py:490
  434.5 5.1 collective-permute-done.52
  453.5 5.1 collective-permute-done.59
  461.9 5.8 %collective-permute-done.60 = f32[2,9760]{1,0:T(2,128)S(1)} collective-permute-done((f32[2,9760]{1,0:T(2,128)S(1)}, f32[2,9760]{1,0:T(2,128)S(1)}, u32[]{:S(2)}, u32[]{:S(2)}) %collective-permute-start.60) | collective-permute-done | bytes 78112 | tf_op jit(solution)/shard_map/ppermute | solution.py:753
  479.0 12.0 %collective-permute-done.57 = bf16[2,128,1536]{2,1,0:T(8,128)(2,1)} collective-permute-done((bf16[2,128,1536]{2,1,0:T(8,128)(2,1)}, bf16[2,128,1536]{2,1,0:T(8,128)(2,1)}, u32[]{:S(2)}, u32[]{:S(2)}) %collective-permute-start.57) | collective-permute-done | bytes 786464 | tf_op jit(solution)/shard_map/ppermute | solution.py:523
  502.3 4.2 collective-permute-done.65
  (491 shorter events, 185.8 us)
Async XLA Ops:
  7.2 86.3 %all-gather.5.cloned.1.call-start = ((), (), s32[]{:S(2)}) async-start(), calls=%async_computation.4 | async-start | bytes 6635520 | tf_op jit(solution)/shard_map/all_gather | solution.py:613
  9.6 19.5 %collective-permute-start.5 = (bf16[192,1664]{1,0:T(8,128)(2,1)S(1)}, bf16[192,1664]{1,0:T(8,128)(2,1)S(1)}, u32[]{:S(2)}, u32[]{:S(2)}) collective-permute-start(bf16[192,1664]{1,0:T(8,128)(2,1)S(1)} %fusion.28), channel_id=1, source_target_pairs={{0,16},{16,0},{1,17},{17,1},{2,18},{18,2},{3,19},{19,3},{4,20},{20... | collective-permute-start | bytes 1916936 | tf_op jit(solution)/shard_map/ppermute | solution.py:523
  30.3 95.6 %all-gather.7.cloned.1.call-start = ((), (), s32[]{:S(2)}) async-start(), calls=%async_computation.5 | async-start | bytes 2654208 | tf_op jit(solution)/shard_map/all_gather | solution.py:614
  39.7 156.3 %all-gather.9.cloned.1.call-start = ((), (), s32[]{:S(2)}) async-start(), calls=%async_computation.6 | async-start | bytes 6635520 | tf_op jit(solution)/shard_map/all_gather | solution.py:613
  40.9 184.7 %all-gather.11.cloned.1.call-start = ((), (), s32[]{:S(2)}) async-start(), calls=%async_computation.7 | async-start | bytes 2654208 | tf_op jit(solution)/shard_map/all_gather | solution.py:614
  46.1 18.1 %collective-permute-start.10 = (f32[8,768]{1,0:T(8,128)S(1)}, f32[8,768]{1,0:T(8,128)S(1)}, u32[]{:S(2)}, u32[]{:S(2)}) collective-permute-start(f32[8,768]{1,0:T(8,128)S(1)} %pad_dynamic-slice_fusion.2), channel_id=1, source_target_pairs={{0,16},{16,0},{1,17},{17,1},{2,18},{18,2},{3,19},{19,3},{4,20},{20... | collective-permute-start | bytes 73736 | tf_op jit(solution)/shard_map/ppermute | solution.py:523
  59.4 15.9 %collective-permute-start.4 = (bf16[256,1536]{1,0:T(8,128)(2,1)}, bf16[256,1536]{1,0:T(8,128)(2,1)}, u32[]{:S(2)}, u32[]{:S(2)}) collective-permute-start(bf16[256,1536]{1,0:T(8,128)(2,1)} %pad_maximum_fusion.2), channel_id=1, source_target_pairs={{0,16},{16,0},{1,17},{17,1},{2,18},{18,2},{3,19},{19,3},{4,20},{20... | collective-permute-start | bytes 2359304 | tf_op jit(solution)/shard_map/ppermute | solution.py:523
  61.9 14.4 %collective-permute-start.3 = (bf16[256,1536]{1,0:T(8,128)(2,1)}, bf16[256,1536]{1,0:T(8,128)(2,1)S(1)}, u32[]{:S(2)}, u32[]{:S(2)}) collective-permute-start(bf16[256,1536]{1,0:T(8,128)(2,1)} %pad_maximum_fusion.1), channel_id=1, source_target_pairs={{0,1},{1,0},{2,3},{3,2},{4,5},{5,4},{6,7},{7,6},{8,9},{9,8},{10,11... | collective-permute-start | bytes 2359304 | tf_op jit(solution)/shard_map/ppermute | solution.py:523
  64.3 243.9 %reduce-scatter.5.cloned.1.call-start = ((), (), s32[]{:S(2)}) async-start(), calls=%async_computation.8 | async-start | bytes 2654208 | tf_op jit(solution)/shard_map/reduce_scatter | solution.py:763
  81.7 23.9 %collective-permute-start.9 = (bf16[128,1536]{1,0:T(8,128)(2,1)S(1)}, bf16[128,1536]{1,0:T(8,128)(2,1)S(1)}, u32[]{:S(2)}, u32[]{:S(2)}) collective-permute-start(bf16[128,1536]{1,0:T(8,128)(2,1)S(1)} %get-tuple-element.329), channel_id=1, source_target_pairs={{0,1},{1,0},{2,3},{3,2},{4,5},{5,4},{6,7},{7,6},{8,9},{9,8},{10,11... | collective-permute-start | bytes 1179656 | tf_op jit(solution)/shard_map/ppermute | solution.py:523
  83.2 22.4 %collective-permute-start.8 = (bf16[128,1536]{1,0:T(8,128)(2,1)S(1)}, bf16[128,1536]{1,0:T(8,128)(2,1)S(1)}, u32[]{:S(2)}, u32[]{:S(2)}) collective-permute-start(bf16[128,1536]{1,0:T(8,128)(2,1)S(1)} %get-tuple-element.330), channel_id=1, source_target_pairs={{0,16},{16,0},{1,17},{17,1},{2,18},{18,2},{3,19},{19,3},{4,20},{20... | collective-permute-start | bytes 1179656 | tf_op jit(solution)/shard_map/ppermute | solution.py:523
  107.5 26.7 %collective-permute-start.17 = (bf16[256,1536]{1,0:T(8,128)(2,1)}, bf16[256,1536]{1,0:T(8,128)(2,1)S(1)}, u32[]{:S(2)}, u32[]{:S(2)}) collective-permute-start(bf16[256,1536]{1,0:T(8,128)(2,1)} %pad_maximum_fusion.4), channel_id=1, source_target_pairs={{0,16},{16,0},{1,17},{17,1},{2,18},{18,2},{3,19},{19,3},{4,20},{20... | collective-permute-start | bytes 2359304 | tf_op jit(solution)/shard_map/ppermute | solution.py:523
  109.0 25.2 %collective-permute-start.16 = (bf16[256,1536]{1,0:T(8,128)(2,1)}, bf16[256,1536]{1,0:T(8,128)(2,1)S(1)}, u32[]{:S(2)}, u32[]{:S(2)}) collective-permute-start(bf16[256,1536]{1,0:T(8,128)(2,1)} %pad_maximum_fusion.3), channel_id=1, source_target_pairs={{0,1},{1,0},{2,3},{3,2},{4,5},{5,4},{6,7},{7,6},{8,9},{9,8},{10,11... | collective-permute-start | bytes 2359304 | tf_op jit(solution)/shard_map/ppermute | solution.py:523
  134.2 18.7 %collective-permute-start.18 = (bf16[256,1536]{1,0:T(8,128)(2,1)S(1)}, bf16[256,1536]{1,0:T(8,128)(2,1)S(1)}, u32[]{:S(2)}, u32[]{:S(2)}) collective-permute-start(bf16[256,1536]{1,0:T(8,128)(2,1)S(1)} %get-tuple-element.151), channel_id=1, source_target_pairs={{0,1},{1,0},{2,3},{3,2},{4,5},{5,4},{6,7},{7,6},{8,9},{9,8},{10,11... | collective-permute-start | bytes 2359304 | tf_op jit(solution)/shard_map/ppermute | solution.py:523
  136.3 17.9 %collective-permute-start.20 = (bf16[256,1536]{1,0:T(8,128)(2,1)S(1)}, bf16[256,1536]{1,0:T(8,128)(2,1)S(1)}, u32[]{:S(2)}, u32[]{:S(2)}) collective-permute-start(bf16[256,1536]{1,0:T(8,128)(2,1)S(1)} %get-tuple-element.153), channel_id=1, source_target_pairs={{0,16},{16,0},{1,17},{17,1},{2,18},{18,2},{3,19},{19,3},{4,20},{20... | collective-permute-start | bytes 2359304 | tf_op jit(solution)/shard_map/ppermute | solution.py:523
  174.7 16.5 %collective-permute-start.29 = (bf16[256,1536]{1,0:T(8,128)(2,1)S(1)}, bf16[256,1536]{1,0:T(8,128)(2,1)S(1)}, u32[]{:S(2)}, u32[]{:S(2)}) collective-permute-start(bf16[256,1536]{1,0:T(8,128)(2,1)S(1)} %pad_maximum_fusion.6), channel_id=1, source_target_pairs={{0,16},{16,0},{1,17},{17,1},{2,18},{18,2},{3,19},{19,3},{4,20},{20... | collective-permute-start | bytes 2359304 | tf_op jit(solution)/shard_map/ppermute | solution.py:523
  176.5 15.9 %collective-permute-start.28 = (bf16[256,1536]{1,0:T(8,128)(2,1)S(1)}, bf16[256,1536]{1,0:T(8,128)(2,1)S(1)}, u32[]{:S(2)}, u32[]{:S(2)}) collective-permute-start(bf16[256,1536]{1,0:T(8,128)(2,1)S(1)} %pad_maximum_fusion.5), channel_id=1, source_target_pairs={{0,1},{1,0},{2,3},{3,2},{4,5},{5,4},{6,7},{7,6},{8,9},{9,8},{10,11... | collective-permute-start | bytes 2359304 | tf_op jit(solution)/shard_map/ppermute | solution.py:523
  244.5 126.0 %reduce-scatter.7.cloned.1.call-start = ((), (), s32[]{:S(2)}) async-start(), calls=%async_computation.9 | async-start | bytes 6635520 | tf_op jit(solution)/shard_map/reduce_scatter | solution.py:778
  292.1 132.5 %reduce-scatter.11.cloned.1.call-start = ((), (), s32[]{:S(2)}) async-start(), calls=%async_computation.11 | async-start | bytes 2654208 | tf_op jit(solution)/shard_map/reduce_scatter | solution.py:793
  294.5 13.7 %collective-permute-start.37 = (bf16[256,1536]{1,0:T(8,128)(2,1)S(1)}, bf16[256,1536]{1,0:T(8,128)(2,1)}, u32[]{:S(2)}, u32[]{:S(2)}) collective-permute-start(bf16[256,1536]{1,0:T(8,128)(2,1)S(1)} %get-tuple-element.181), channel_id=1, source_target_pairs={{0,16},{16,0},{1,17},{17,1},{2,18},{18,2},{3,19},{19,3},{4,20},{20... | collective-permute-start | bytes 2359304 | tf_op jit(solution)/shard_map/ppermute | solution.py:523
  342.5 16.3 %collective-permute-start.45 = (bf16[256,1536]{1,0:T(8,128)(2,1)S(1)}, bf16[256,1536]{1,0:T(8,128)(2,1)S(1)}, u32[]{:S(2)}, u32[]{:S(2)}) collective-permute-start(bf16[256,1536]{1,0:T(8,128)(2,1)S(1)} %pad_maximum_fusion.8), channel_id=1, source_target_pairs={{0,16},{16,0},{1,17},{17,1},{2,18},{18,2},{3,19},{19,3},{4,20},{20... | collective-permute-start | bytes 2359304 | tf_op jit(solution)/shard_map/ppermute | solution.py:523
  343.5 15.4 %collective-permute-start.44 = (bf16[256,1536]{1,0:T(8,128)(2,1)S(1)}, bf16[256,1536]{1,0:T(8,128)(2,1)S(1)}, u32[]{:S(2)}, u32[]{:S(2)}) collective-permute-start(bf16[256,1536]{1,0:T(8,128)(2,1)S(1)} %pad_maximum_fusion.7), channel_id=1, source_target_pairs={{0,1},{1,0},{2,3},{3,2},{4,5},{5,4},{6,7},{7,6},{8,9},{9,8},{10,11... | collective-permute-start | bytes 2359304 | tf_op jit(solution)/shard_map/ppermute | solution.py:523
  345.3 13.5 %collective-permute-start.46 = (f32[256]{0:T(256)S(1)}, f32[256]{0:T(256)S(1)}, u32[]{:S(2)}, u32[]{:S(2)}) collective-permute-start(f32[256]{0:T(256)S(1)} %pad_maximum_fusion.22), channel_id=1, source_target_pairs={{0,1},{1,0},{2,3},{3,2},{4,5},{5,4},{6,7},{7,6},{8,9},{9,8},{10,11... | collective-permute-start | bytes 3080 | tf_op jit(solution)/shard_map/ppermute | solution.py:523
  364.9 34.8 %collective-permute-start.48 = (bf16[256,1536]{1,0:T(8,128)(2,1)}, bf16[256,1536]{1,0:T(8,128)(2,1)}, u32[]{:S(2)}, u32[]{:S(2)}) collective-permute-start(bf16[256,1536]{1,0:T(8,128)(2,1)} %get-tuple-element.212), channel_id=1, source_target_pairs={{0,1},{1,0},{2,3},{3,2},{4,5},{5,4},{6,7},{7,6},{8,9},{9,8},{10,11... | collective-permute-start | bytes 2359304 | tf_op jit(solution)/shard_map/ppermute | solution.py:523
  365.3 34.3 %collective-permute-start.49 = (bf16[256,1536]{1,0:T(8,128)(2,1)S(1)}, bf16[256,1536]{1,0:T(8,128)(2,1)S(1)}, u32[]{:S(2)}, u32[]{:S(2)}) collective-permute-start(bf16[256,1536]{1,0:T(8,128)(2,1)S(1)} %get-tuple-element.213), channel_id=1, source_target_pairs={{0,16},{16,0},{1,17},{17,1},{2,18},{18,2},{3,19},{19,3},{4,20},{20... | collective-permute-start | bytes 2359304 | tf_op jit(solution)/shard_map/ppermute | solution.py:523
  370.6 123.9 %reduce-scatter.9.cloned.1.call-start = ((), (), s32[]{:S(2)}) async-start(), calls=%async_computation.10 | async-start | bytes 6635520 | tf_op jit(solution)/shard_map/reduce_scatter | solution.py:812
  402.0 22.6 %collective-permute-start.50 = (bf16[128,1536]{1,0:T(8,128)(2,1)}, bf16[128,1536]{1,0:T(8,128)(2,1)}, u32[]{:S(2)}, u32[]{:S(2)}) collective-permute-start(bf16[128,1536]{1,0:T(8,128)(2,1)} %slice.546), channel_id=1, source_target_pairs={{0,16},{16,0},{1,17},{17,1},{2,18},{18,2},{3,19},{19,3},{4,20},{20... | collective-permute-start | bytes 1179656 | tf_op jit(solution)/shard_map/ppermute | solution.py:523
  404.2 20.4 %collective-permute-start.51 = (bf16[128,1536]{1,0:T(8,128)(2,1)S(1)}, bf16[128,1536]{1,0:T(8,128)(2,1)}, u32[]{:S(2)}, u32[]{:S(2)}) collective-permute-start(bf16[128,1536]{1,0:T(8,128)(2,1)S(1)} %slice.545), channel_id=1, source_target_pairs={{0,1},{1,0},{2,3},{3,2},{4,5},{5,4},{6,7},{7,6},{8,9},{9,8},{10,11... | collective-permute-start | bytes 1179656 | tf_op jit(solution)/shard_map/ppermute | solution.py:523
  424.7 14.9 %collective-permute-start.52 = (bf16[256,1536]{1,0:T(8,128)(2,1)S(1)}, bf16[256,1536]{1,0:T(8,128)(2,1)}, u32[]{:S(2)}, u32[]{:S(2)}) collective-permute-start(bf16[256,1536]{1,0:T(8,128)(2,1)S(1)} %get-tuple-element.227), channel_id=1, source_target_pairs={{0,1},{1,0},{2,3},{3,2},{4,5},{5,4},{6,7},{7,6},{8,9},{9,8},{10,11... | collective-permute-start | bytes 2359304 | tf_op jit(solution)/shard_map/ppermute | solution.py:523
  425.2 14.4 %collective-permute-start.53 = (bf16[256,1536]{1,0:T(8,128)(2,1)S(1)}, bf16[256,1536]{1,0:T(8,128)(2,1)}, u32[]{:S(2)}, u32[]{:S(2)}) collective-permute-start(bf16[256,1536]{1,0:T(8,128)(2,1)S(1)} %get-tuple-element.228), channel_id=1, source_target_pairs={{0,16},{16,0},{1,17},{17,1},{2,18},{18,2},{3,19},{19,3},{4,20},{20... | collective-permute-start | bytes 2359304 | tf_op jit(solution)/shard_map/ppermute | solution.py:523
  430.1 14.8 %collective-permute-start.58 = (bf16[192,768]{1,0:T(8,128)(2,1)S(1)}, bf16[192,768]{1,0:T(8,128)(2,1)S(1)}, u32[]{:S(2)}, u32[]{:S(2)}) collective-permute-start(bf16[192,768]{1,0:T(8,128)(2,1)S(1)} %broadcast_select_fusion.7), channel_id=1, source_target_pairs={{0,16},{16,0},{1,17},{17,1},{2,18},{18,2},{3,19},{19,3},{4,20},{20... | collective-permute-start | bytes 884744 | tf_op jit(solution)/shard_map/ppermute | solution.py:523
  476.3 14.6 %collective-permute-start.57 = (bf16[2,128,1536]{2,1,0:T(8,128)(2,1)}, bf16[2,128,1536]{2,1,0:T(8,128)(2,1)}, u32[]{:S(2)}, u32[]{:S(2)}) collective-permute-start(bf16[2,128,1536]{2,1,0:T(8,128)(2,1)} %get-tuple-element.302), channel_id=1, source_target_pairs={{0,16},{16,0},{1,17},{17,1},{2,18},{18,2},{3,19},{19,3},{4,20},{20... | collective-permute-start | bytes 2359304 | tf_op jit(solution)/shard_map/ppermute | solution.py:523
  (96 other events, 634.0 us)
Sparse Core Ops, SparseCore 0:
  30.5 62.9 all-gather.4
  95.1 30.2 all-gather.6
  127.1 60.6 all-gather.8
  189.3 30.2 all-gather.10
  244.6 34.9 reduce-scatter.4
  292.3 64.8 reduce-scatter.6
  370.7 34.9 reduce-scatter.10
  414.5 68.0 reduce-scatter.8

commit v3 on v2

--- a/solution.py
+++ b/solution.py
@@ -51,12 +51,16 @@
     return total
 
 
-def conv_back(ds, after, taps):
+def shifted_back(ds, after):
     cat = jnp.concatenate([ds, after], axis=0)
     rows = cat.shape[0]
-    total = taps[3:4] * ds
+    return [pltpu.roll(cat, rows - (3 - j), 0)[: ds.shape[0]] for j in range(3)] + [ds]
+
+
+def conv_back(later, taps):
+    total = taps[3:4] * later[3]
     for j in range(3):
-        total = total + taps[j : j + 1] * pltpu.roll(cat, rows - (3 - j), 0)[: ds.shape[0]]
+        total = total + taps[j : j + 1] * later[j]
     return total
 
 
@@ -113,7 +117,7 @@
 
 def fwd_kernel(
     order, px, halo, pre_dt, taps_x, taps_bc, heads, skip, gain, spread_run, spread_steps,
-    og_ref, y_ref, s_ref, sq_ref, rows_ref, cols_ref, state,
+    og_ref, y_ref, conv_ref, s_ref, sq_ref, rows_ref, cols_ref, state,
 ):
     s_id, k = pl.program_id(0), pl.program_id(1)
     width = y_ref.shape[1]
@@ -149,6 +153,7 @@
         at = slice(p * LANES, (p + 1) * LANES)
         x_cat = jnp.concatenate([halo[:, at] * keep, px[:, at]], axis=0)
         s_x = conv(shifted(x_cat), taps_x[:, at])
+        conv_ref[:, at] = s_x
         xs = s_x * sigmoid(s_x)
         xd = xs * steps_wide[:, at]
         xr = xd.astype(bf16)
@@ -180,7 +185,7 @@
 
 
 def bwd_kernel(
-    order, px, halo, y_ref, s_ref, d_ref, stats, rows_ref, cols_ref,
+    order, px, halo, conv_ref, y_ref, s_ref, d_ref, stats, rows_ref, cols_ref,
     taps_x, taps_bc, heads, skip, gain, spread_run, spread_steps, sums,
     pre_ref, acc_x, acc_bc, acc_dt,
     back, after_x, after_bc, d_scores, head_sums_ref, part_x, part_bc,
@@ -232,9 +237,7 @@
     row_stat = jnp.broadcast_to(stat_cols[:, 1:2], (T, LANES))
     for p in range(pairs):
         at = slice(p * LANES, (p + 1) * LANES)
-        x_cat = jnp.concatenate([halo[:, at] * keep, px[:, at]], axis=0)
-        x_parts = shifted(x_cat)
-        s_x = conv(x_parts, taps_x[:, at])
+        s_x = conv_ref[:, at]
         sig_x = sigmoid(s_x)
         xs = s_x * sig_x
         steps_pair = steps_wide[:, at]
@@ -296,10 +299,12 @@
         )
         dxs = steps_pair * (dx_in + dx_out) + skip[:, at] * dy
         ds = dxs * (sig_x + xs * (1.0 - sig_x))
+        later = shifted_back(ds, after_x[:, at])
+        pre_x = px[:, at]
         for j in range(4):
-            part_x[8 * j : 8 * j + 8, at] += eights(ds * x_parts[j])
+            part_x[8 * j : 8 * j + 8, at] += eights(later[j] * pre_x)
         part_x[32:40, at] += eights(ds)
-        dx_ref[:, at] = conv_back(ds, after_x[:, at], taps_x[:, at]).astype(bf16)
+        dx_ref[:, at] = conv_back(later, taps_x[:, at]).astype(bf16)
         after_x[:, at] = ds[:8]
     head_sums_ref[pl.ds(pl.multiple_of(place * T, T), T)] = head_sums
     ds_t = jnp.where(seen_t, d_scores[...], 0.0)
@@ -309,7 +314,7 @@
     for j in range(4):
         part_bc[8 * j : 8 * j + 8] += eights(ds_bc * bc_parts[j])
     part_bc[32:40] += eights(ds_bc)
-    dx_ref[:, bc_at : bc_at + 2 * N] = conv_back(ds_bc, after_bc[...], taps_bc[...]).astype(bf16)
+    dx_ref[:, bc_at : bc_at + 2 * N] = conv_back(shifted_back(ds_bc, after_bc[...]), taps_bc[...]).astype(bf16)
     after_bc[...] = ds_bc[:8]
 
     @pl.when(k == 3)
@@ -374,6 +379,7 @@
             out_specs=[
                 pl.BlockSpec((T, width), here),
                 pl.BlockSpec((T, width), here),
+                pl.BlockSpec((T, width), here),
                 pl.BlockSpec((1, N, width), lambda s, k, order: (s * 4 + k, 0, 0)),
                 pl.BlockSpec((1, 8, T), lambda s, k, order: (order[s * 4 + k], 0, 0)),
                 pl.BlockSpec((steps, 3 * HP, T), whole),
@@ -384,6 +390,7 @@
         out_shape=[
             pltpu.HBM((rows, width), bf16),
             pltpu.HBM((rows, width), f32),
+            pltpu.HBM((rows, width), f32),
             pltpu.HBM((steps, N, width), bf16),
             jax.ShapeDtypeStruct((steps, 8, T), f32),
             pltpu.HBM((steps, 3 * HP, T), f32),
@@ -395,7 +402,7 @@
     )(order, *hbm(px, px, px), *small[:5], *hbm(*small[5:]))
 
 
-def scan_backward(order, px, y, states, d_out, stats, row_steps, col_steps, layer, fixed_arrays):
+def scan_backward(order, px, conv_x, y, states, d_out, stats, row_steps, col_steps, layer, fixed_arrays):
     rows, width = y.shape
     steps = rows // T
     here = lambda s, k, order: (order[s * 4 + 3 - k], 0)
@@ -411,6 +418,7 @@
             in_specs=[
                 pl.BlockSpec((T, px.shape[1]), here),
                 pl.BlockSpec((8, width + 2 * N), before),
+                pl.BlockSpec((T, width), here),
                 pl.BlockSpec((T, width), here),
                 pl.BlockSpec((1, N, width), lambda s, k, order: (s * 4 + 3 - k, 0, 0)),
                 pl.BlockSpec((T, width), here),
@@ -442,7 +450,7 @@
         compiler_params=pltpu.CompilerParams(vmem_limit_bytes=40 * 2**20),
         cost_estimate=pl.CostEstimate(flops=24 * 10**9, bytes_accessed=24 * 2**20, transcendentals=10**7),
         name="scan_backward",
-    )(order, *hbm(px, px, y, states, d_out), stats, *hbm(*small[:2]), *small[2:7], *hbm(*small[7:]))
+    )(order, *hbm(px, px, conv_x, y, states, d_out), stats, *hbm(*small[:2]), *small[2:7], *hbm(*small[7:]))
 
 
 def dots_kernel(do, w_out, og, d_ref, dots_ref):
@@ -687,18 +695,17 @@
             pre, top_received = tied((pre, top_received))
             top_twos = join_first(top_rounded, top_received)
             top_received = spread_second(top_twos)
-        og, y, states, squares, row_steps, col_steps = scan_forward(order, pre, layer, tables)
+        og, y, conv_x, states, squares, row_steps, col_steps = scan_forward(order, pre, layer, tables)
         if l == 1:
             og, do_top = tied((og, do_top))
         sq = squares[:, 0, :]
-        saved.append((u, rho, a, pre, og, y, states, sq, row_steps, col_steps))
+        saved.append((u, rho, a, pre, og, y, conv_x, states, sq, row_steps, col_steps))
         if l == 0:
             o_part, sq_part = rows_product(og, w_out), list(sq.reshape(4, size // 2))
             o_part, top_received = tied((o_part, top_received))
             do_top = join_second(top_twos, top_received)
-            received = send_half(o_part)
-            twos = add_half(o_part, received)
-            sq_twos = add_half(sq_part, send_half(sq_part))
+            received, sq_received = tied((send_half(o_part), send_half(sq_part)))
+            twos, sq_twos = add_half(o_part, received), add_half(sq_part, sq_received)
             o = add_quarter(twos, send_quarter(twos, bf16))
             total = add_quarter(sq_twos, send_quarter(sq_twos, f32))[:, :, None]
             r_first = lax.rsqrt(total / DI + eps)
@@ -725,7 +732,7 @@
         pair = jnp.stack([scale.reshape(-1, T), stat.reshape(-1, T)], axis=1)
         return jnp.pad(pair, ((0, 0), (0, 6), (0, 0)))
 
-    u, rho, a, pre, og, y, states, sq, row_steps, col_steps = saved[1]
+    u, rho, a, pre, og, y, conv_x, states, sq, row_steps, col_steps = saved[1]
     d_out, dots = rows_and_dots(do_top, weights[1][1], og)
     square_sums, dots = tied((summed_rows(sq.reshape(1, -1)), dots[:, 0, :].reshape(-1)))
     r_last = lax.rsqrt(square_sums[0] / DI + eps)
@@ -745,15 +752,20 @@
 
     def sum_steps():
         devices = lax.axis_size("dp")
-        same = lambda value: value
         if devices & (devices - 1):
-            return [lambda value: jnp.sum(lax.all_gather(value, "dp", axis=0), axis=0), same, same]
-
-        def add_other(value, step):
-            return value + lax.ppermute(value, "dp", [(i, i ^ step) for i in range(devices)])
-
-        steps = [functools.partial(add_other, step=1 << i) for i in range(devices.bit_length() - 1)]
-        return steps + [same] * max(0, 3 - len(steps))
+            return [lambda value: jnp.sum(lax.all_gather(value, "dp", axis=0), axis=0), lambda value: value]
+
+        def add_others(value, masks):
+            return value + sum(
+                lax.ppermute(value, "dp", [(i, i ^ mask) for i in range(devices)]) for mask in masks
+            )
+
+        steps, bit = [], 1
+        while bit < devices:
+            four = bit > 1 and 2 * bit < devices
+            steps.append(functools.partial(add_others, masks=(bit, 2 * bit, 3 * bit) if four else (bit,)))
+            bit *= 4 if four else 2
+        return steps + [lambda value: value] * max(0, 2 - len(steps))
 
     def input_gradient(l, dv, da):
         u, rho = saved[l][0], saved[l][1]
@@ -762,7 +774,7 @@
 
     shard_out = lax.psum_scatter(grad_out_last, "dp", scatter_dimension=0, tiled=True)
     d_pre, acc_x, acc_bc, acc_dt = scan_backward(
-        order, pre, y, states, d_out, stats_last, row_steps, col_steps, layers[1], tables
+        order, pre, conv_x, y, states, d_out, stats_last, row_steps, col_steps, layers[1], tables
     )
     da_part = rows_product(d_pre, weights[1][0])
     d_pre, da_part = tied((d_pre, da_part))
@@ -782,7 +794,7 @@
     kappa = r_first[:, :, 0] ** 2 * jnp.sum(dv * o_first, axis=2) / DI
     do, stat = spread_all(do_own, kappa)
     do, o_part = tied((do, o_part))
-    u, rho, a, pre, og, y, states, sq, row_steps, col_steps = saved[0]
+    u, rho, a, pre, og, y, conv_x, states, sq, row_steps, col_steps = saved[0]
     w_in, w_out = weights[0]
     stats = rows_of_stats(jnp.ones_like(stat), stat)
     d_out = dot_nn(do, w_out)
@@ -792,12 +804,12 @@
     d_out, grad_out = tied((d_out, grad_out))
     shard_out = lax.psum_scatter(grad_out, "dp", scatter_dimension=0, tiled=True)
     d_pre, acc_x, acc_bc, acc_dt = scan_backward(
-        order, pre, y, states, d_out, stats, row_steps, col_steps, layers[0], tables
+        order, pre, conv_x, y, states, d_out, stats, row_steps, col_steps, layers[0], tables
     )
     d_pre, o_received = tied((d_pre, send_half(o_part)))
+    grad_in = dot_tn(a, d_pre).astype(bf16)
+    d_pre, grad_after, o_received = tied((d_pre, grad_in, o_received))
     o_twos = add_half(o_part, o_received)
-    grad_in = dot_tn(a, d_pre).astype(bf16)
-    d_pre, grad_in = tied((d_pre, grad_in))
     da_part = rows_product(d_pre, w_in)
     da_part, o_received, shard_out = tied((da_part, send_quarter(o_twos, bf16), shard_out))
     r_own = jnp.stack([r_last[s * size : s * size + T] for s in range(streams)])
@@ -807,12 +819,12 @@
     twos = add_half(da_part, received)
     steps = sum_steps()
     received, small = tied((send_quarter(twos, bf16), steps[0](small)))
+    for step in steps[1:]:
+        small = step(small)
     da = add_quarter(twos, received)
     dv = input_gradient(0, dv, da)
     shard_in = lax.psum_scatter(grad_in, "dp", scatter_dimension=0, tiled=True)
     ends_other = swap(jnp.where(x == 0, final, dv).astype(bf16), "section")
-    for step in steps[1:]:
-        small = step(small)
 
     partners = ((2, 3, 0, 1), (1, 0, 3, 2), (3, 2, 1, 0))
 
@@ -820,13 +832,18 @@
         return jnp.where(x == 0, first, last), jnp.where(x == 0, last, first)
 
     kept, sent = mine_and_partners(small[0], small[1])
-    other = swap(sent, "section")
-    of_section = jnp.stack(mine_and_partners(kept, other))
-    other = swap(of_section, "tensor")
+    from_section = swap(sent, "section")
+    from_tensor = swap(kept, "tensor")
+    from_diagonal = lax.ppermute(sent, ("section", "tensor"), list(enumerate(partners[2])))
 
     out_kept, out_sent = mine_and_partners(shard_out, shards[1][0])
     out_other = swap(out_sent, "section")
-    mine = jnp.stack([jnp.where(yy == 0, of_section, other), jnp.where(yy == 0, other, of_section)], axis=1)
+    ends_other, from_section, from_tensor, from_diagonal = tied(
+        (ends_other, from_section, from_tensor, from_diagonal)
+    )
+    own_row = jnp.stack(mine_and_partners(kept, from_section))
+    other_row = jnp.stack(mine_and_partners(from_tensor, from_diagonal))
+    mine = jnp.stack([jnp.where(yy == 0, own_row, other_row), jnp.where(yy == 0, other_row, own_row)], axis=1)
     mine = mine.reshape(4, -1)
     end_x, end_bc = 8 * width, 8 * width + 8 * 2 * N
     end_dt = end_bc + 2 * HP
@@ -847,9 +864,7 @@
     relay = jnp.concatenate([jnp.where(x == 0, mine, other), jnp.where(x == 0, other, mine)], axis=1)
     grad_out = jnp.concatenate(mine_and_partners(out_kept, out_other), axis=1).astype(f32)
 
-    done = (relay, grad_out, grad_norm, grad_conv_value, grad_conv_shared, grad_heads, grad_gate_gain)
-    shard_in, done = tied((shard_in, done))
-    relay, grad_out, grad_norm, grad_conv_value, grad_conv_shared, grad_heads, grad_gate_gain = done
+    shard_in, relay, grad_out = tied((shard_in, relay, grad_out))
     in_kept, in_sent = mine_and_partners(shard_in, shards[1][1])
     bc_at, dt_at, z_at = width, width + 2 * N, width + 2 * N + LANES
 

time: 524 us -> 507 us (0.968)
  waiting for transfers between devices: 171 us -> 151 us
    ppermute x56, waiting for transfers between devices: 144 us -> 128 us  [swap(): return lax.ppermute(value, axis, [(0, 1), (1, 0)])]
    all_gather x2, waiting for transfers between devices: 9.77 us -> 4.4 us  [local(): lax.all_gather(packed, 'dp', axis=0, tiled=True)]
    ppermute x3 -> x5, waiting for transfers between devices: 11 us -> 9.06 us  [the longest x4 6.48 us: add_others(): lax.ppermute(value, 'dp', [(i, i ^ mask) for i in range(devices)])]
  transfers between devices with their start and end apart: 74 -> 76, of which waited for: 37 -> 36; matrix products, arithmetic and copies ran while one was open for 21% -> 23% of each run, Pallas kernels for 23% -> 24%
where the time goes in v3:
time: 507 us; the launch traced here: 500 us
  waiting for transfers between devices  151 us (30%)
  Pallas kernels  118 us (23%)
  starting transfers between devices  77.1 us (15%)
  matrix products  57.4 us (11%)
  other arithmetic  45.4 us (9%)
  local copies, waits for them, and re-layouts  34 us (7%)
  between operations  16.7 us (3%)
    ppermute x56, waiting for transfers between devices, swap(): return lax.ppermute(value, axis, [(0, 1), (1, 0)])  128 us
    ppermute x56, starting transfers between devices, swap(): return lax.ppermute(value, axis, [(0, 1), (1, 0)])  62 us
    pallas_call x2, Pallas kernels, scan_backward(): pl.pallas_call(bwd_kernel, grid_spec=pltpu.PrefetchScalarGridSpec(num_sca...  51 us
    pallas_call x4, Pallas kernels, rows_product(): pl.pallas_call(rows_kernel, grid=(3,), in_specs=[pl.BlockSpec(rows.shape,...  30.8 us
    pallas_call x2, Pallas kernels, scan_forward(): pl.pallas_call(fwd_kernel, grid_spec=pltpu.PrefetchScalarGridSpec(num_sca...  29.8 us
    dot_general x4, matrix products, dot_tn(): lax.dot_general(a, b, (((0,), (0,)), ((), ())), preferred_element_type=f32)  29.2 us
    dot_general x3, matrix products, dot_nn(): lax.dot_general(a, b, (((1,), (0,)), ((), ())), preferred_element_type=f32)  28.1 us
    unnamed x141, local copies, waits for them, and re-layouts  20.2 us
  transfers between devices with their start and end apart: 76, of which 36 were waited for; matrix products, arithmetic and copies ran while one was open for 23% of the time, Pallas kernels for 24%

profile of v3, /device:TPU:0, one launch (start us, length us, event | category | flops | bytes accessed | tf_op | source)
XLA Modules:
  0.0 500.2 jit_solution(2591966521944144427)
XLA Ops:
  17.0 12.1 %collective-permute-done.7 = bf16[192,256]{1,0:T(8,128)(2,1)S(1)} collective-permute-done((bf16[192,256]{1,0:T(8,128)(2,1)S(1)}, bf16[192,256]{1,0:T(8,128)(2,1)S(1)}, u32[]{:S(2)}, u32[]{:S(2)}) %collective-permute-start.7) | collective-permute-done | bytes 98336 | tf_op jit(solution)/shard_map/ppermute | solution.py:531
  32.3 6.5 %collective-permute-done.15 = bf16[192,768]{1,0:T(8,128)(2,1)S(1)} collective-permute-done((bf16[192,768]{1,0:T(8,128)(2,1)S(1)}, bf16[192,768]{1,0:T(8,128)(2,1)S(1)}, u32[]{:S(2)}, u32[]{:S(2)}) %collective-permute-start.15) | collective-permute-done | bytes 294944 | tf_op jit(solution)/shard_map/ppermute | solution.py:531
  53.6 4.8 collective-permute-done.2
  68.9 7.7 %collective-permute-done.4 = bf16[256,1536]{1,0:T(8,128)(2,1)} collective-permute-done((bf16[256,1536]{1,0:T(8,128)(2,1)}, bf16[256,1536]{1,0:T(8,128)(2,1)}, u32[]{:S(2)}, u32[]{:S(2)}) %collective-permute-start.4) | collective-permute-done | bytes 786464 | tf_op jit(solution)/shard_map/ppermute | solution.py:531
  89.2 4.4 all-gather.5.cloned.1.call-done.w
  93.5 11.9 %fusion.51.px.halo.pre_dt = f32[1024,1920]{1,0:T(8,128)} fusion(bf16[1024,1536]{1,0:T(8,128)(2,1)} %constant_dynamic-update-slice_fusion, bf16[1536,1920]{1,0:T(8,128)(2,1)} %all-gather.5.cloned.1.call-done.w), kind=kOutput, calls=%fused_computation.290 | convolution fusion | flops 6039797760 | bytes 16908288 | tf_op jit(solution)/shard_map/dot_general | solution.py:23
  112.3 14.9 %scan_forward.2 = (bf16[1024,768]{1,0:T(8,128)(2,1)}, f32[1024,768]{1,0:T(8,128)}, f32[1024,768]{1,0:T(8,128)}, bf16[8,128,768]{2,1,0:T(8,128)(2,1)}, f32[8,8,12...) custom-call(s32[8]{0:T(128)S(1)} %pad_add_fusion.order, f32[1024,1920]{1,0:T(8,128)} %fusion.51.px.halo.pre_dt, ...), custom_call_target="tpu_custom_call" | custom-call | flops 12000000000 | bytes 14680064 | tf_op jit(solution)/shard_map/scan_forward/pallas_call | solution.py:368
  127.3 5.0 rows_product.4
  137.7 14.1 %collective-permute-done.21 = f32[256]{0:T(256)S(1)} collective-permute-done((f32[256]{0:T(256)S(1)}, f32[256]{0:T(256)S(1)}, u32[]{:S(2)}, u32[]{:S(2)}) %collective-permute-start.21) | collective-permute-done | bytes 1056 | tf_op jit(solution)/shard_map/ppermute | solution.py:531
  157.0 6.6 %collective-permute-done.22 = bf16[128,1536]{1,0:T(8,128)(2,1)S(1)} collective-permute-done((bf16[128,1536]{1,0:T(8,128)(2,1)S(1)}, bf16[128,1536]{1,0:T(8,128)(2,1)S(1)}, u32[]{:S(2)}, u32[]{:S(2)}) %collective-permute-start.22) | collective-permute-done | bytes 393248 | tf_op jit(solution)/shard_map/ppermute | solution.py:531
  169.4 5.6 %collective-permute-done.27 = bf16[128,1536]{1,0:T(8,128)(2,1)S(1)} collective-permute-done((bf16[128,1536]{1,0:T(8,128)(2,1)S(1)}, bf16[128,1536]{1,0:T(8,128)(2,1)S(1)}, u32[]{:S(2)}, u32[]{:S(2)}) %collective-permute-start.27) | collective-permute-done | bytes 393248 | tf_op jit(solution)/shard_map/ppermute | solution.py:531
  179.8 13.1 %collective-permute-done.29 = bf16[256,1536]{1,0:T(8,128)(2,1)S(1)} collective-permute-done((bf16[256,1536]{1,0:T(8,128)(2,1)S(1)}, bf16[256,1536]{1,0:T(8,128)(2,1)S(1)}, u32[]{:S(2)}, u32[]{:S(2)}) %collective-permute-start.29) | collective-permute-done | bytes 786464 | tf_op jit(solution)/shard_map/ppermute | solution.py:531
  194.3 11.9 %fusion.52.px.halo.pre_dt = f32[1024,1920]{1,0:T(8,128)} fusion(bf16[1024,1536]{1,0:T(8,128)(2,1)S(1)} %constant_dynamic-update-slice_fusion.6, bf16[1536,1920]{1,0:T(8,128)(2,1)} %all-gather.9.cloned.1.call-done.w), kind=kOutput, calls=%fused_computation.291 | convolution fusion | flops 6039797760 | bytes 16908288 | tf_op jit(solution)/shard_map/dot_general | solution.py:23
  206.2 14.9 %scan_forward.3 = (bf16[1024,768]{1,0:T(8,128)(2,1)}, f32[1024,768]{1,0:T(8,128)}, f32[1024,768]{1,0:T(8,128)}, bf16[8,128,768]{2,1,0:T(8,128)(2,1)}, f32[8,8,12...) custom-call(s32[8]{0:T(128)S(1)} %pad_add_fusion.order, f32[1024,1920]{1,0:T(8,128)} %fusion.52.px.halo.pre_dt, ...), custom_call_target="tpu_custom_call" | custom-call | flops 12000000000 | bytes 14680064 | tf_op jit(solution)/shard_map/scan_forward/pallas_call | solution.py:368
  224.6 6.8 %rows_and_dots.1 = (f32[1024,768]{1,0:T(8,128)}, f32[8,8,128]{2,1,0:T(8,128)S(1)}) custom-call(bf16[1024,1536]{1,0:T(8,128)(2,1)} %copy-done.35, bf16[1536,768]{1,0:T(8,128)(2,1)} %all-gather.11.cloned.1.call-done.w_out.w, bf16[1024,768]{1,0:T(8,128)(2,1)} %get-tuple-element.208.og.rows), custom_call_target="tpu_custom_call" | custom-call | flops 4000000000 | bytes 10485760 | tf_op jit(solution)/shard_map/rows_and_dots/pallas_call | solution.py:469
  231.7 5.6 %convolution_convert_fusion.3 = bf16[1536,768]{1,0:T(8,128)(2,1)} fusion(bf16[1024,1536]{1,0:T(8,128)(2,1)S(1)} %copy-done.36, bf16[1024,768]{1,0:T(8,128)(2,1)} %get-tuple-element.208.og.rows, f32[1024]{0:T(1024)S(1)} %bitcast.272), kind=kOutput, calls=%fused_computation.3 | convolution fusion | flops 2419458048 | bytes 7081984 | tf_op jit(solution)/shard_map/dot_general | solution.py:31
  244.2 25.4 %scan_backward.2 = (bf16[1024,1920]{1,0:T(8,128)(2,1)}, f32[8,768]{1,0:T(8,128)S(1)}, f32[8,256]{1,0:T(8,128)S(1)}, f32[32,128]{1,0:T(8,128)S(1)}) custom-call(s32[8]{0:T(128)S(1)} %pad_add_fusion.order, f32[1024,1920]{1,0:T(8,128)} %fusion.52.px.halo.pre_dt, f32[1024,1920]{1,0:T(8,128)} %fusion.52.px.halo.pre_dt, f32[1024,768]{1,0:T(8,128)} %get-tuple-element.170.conv_ref, ...), custom_call_target="tpu_custom_call" | custom-call | flops 24000000000 | bytes 25165824 | tf_op jit(solution)/shard_map/scan_backward/pallas_call | solution.py:413
  269.6 10.2 %rows_product.5 = (bf16[256,1536]{1,0:T(8,128)(2,1)S(1)}, bf16[256,1536]{1,0:T(8,128)(2,1)S(1)}, bf16[256,1536]{1,0:T(8,128)(2,1)S(1)}, bf16[256,1536]{1,0:T(8,128)(2,1)S(1)}) custom-call(bf16[1024,1920]{1,0:T(8,128)(2,1)} %get-tuple-element.194.rows, bf16[1536,1920]{1,0:T(8,128)(2,1)} %all-gather.9.cloned.1.call-done.w), custom_call_target="tpu_custom_call" | custom-call | flops 12079595520 | bytes 9830400 | tf_op jit(solution)/shard_map/rows_product/pallas_call | solution.py:498
  279.8 8.4 %convolution_convert_fusion.1 = bf16[1536,1920]{1,0:T(8,128)(2,1)} fusion(bf16[1024,1536]{1,0:T(8,128)(2,1)S(1)} %copy-done.38, bf16[1024,1920]{1,0:T(8,128)(2,1)S(1)} %copy-done.53), kind=kOutput, calls=%fused_computation.1 | convolution fusion | flops 6042746880 | bytes 12976128 | tf_op jit(solution)/shard_map/dot_general | solution.py:31
  293.3 8.8 %collective-permute-done.36 = bf16[256,1536]{1,0:T(8,128)(2,1)} collective-permute-done((bf16[256,1536]{1,0:T(8,128)(2,1)S(1)}, bf16[256,1536]{1,0:T(8,128)(2,1)}, u32[]{:S(2)}, u32[]{:S(2)}) %collective-permute-start.36) | collective-permute-done | bytes 786464 | tf_op jit(solution)/shard_map/ppermute | solution.py:531
  310.1 5.4 %rows_product.6 = (bf16[256,1536]{1,0:T(8,128)(2,1)S(1)}, bf16[256,1536]{1,0:T(8,128)(2,1)S(1)}, bf16[256,1536]{1,0:T(8,128)(2,1)S(1)}, bf16[256,1536]{1,0:T(8,128)(2,1)S(1)}) custom-call(bf16[1024,768]{1,0:T(8,128)(2,1)} %get-tuple-element.208.og.rows, bf16[1536,768]{1,0:T(8,128)(2,1)} %all-gather.11.cloned.1.call-done.w_out.w), custom_call_target="tpu_custom_call" | custom-call | flops 4831838208 | bytes 3932160 | tf_op jit(solution)/shard_map/rows_product/pallas_call | solution.py:498
  324.7 10.2 %collective-permute-done.41 = bf16[128,1536]{1,0:T(8,128)(2,1)S(1)} collective-permute-done((bf16[128,1536]{1,0:T(8,128)(2,1)S(1)}, bf16[128,1536]{1,0:T(8,128)(2,1)S(1)}, u32[]{:S(2)}, u32[]{:S(2)}) %collective-permute-start.41) | collective-permute-done | bytes 393248 | tf_op jit(solution)/shard_map/ppermute | solution.py:531
  341.1 7.7 %collective-permute-done.47 = f32[256]{0:T(256)S(1)} collective-permute-done((f32[256]{0:T(256)S(1)}, f32[256]{0:T(256)S(1)}, u32[]{:S(2)}, u32[]{:S(2)}) %collective-permute-start.47) | collective-permute-done | bytes 1056 | tf_op jit(solution)/shard_map/ppermute | solution.py:531
  350.8 4.3 fusion.53.d_ref
  355.1 4.0 convolution_convert_fusion.2
  361.6 25.7 %scan_backward.3 = (bf16[1024,1920]{1,0:T(8,128)(2,1)}, f32[8,768]{1,0:T(8,128)S(1)}, f32[8,256]{1,0:T(8,128)S(1)}, f32[32,128]{1,0:T(8,128)S(1)}) custom-call(s32[8]{0:T(128)S(1)} %pad_add_fusion.order, f32[1024,1920]{1,0:T(8,128)} %fusion.51.px.halo.pre_dt, f32[1024,1920]{1,0:T(8,128)} %fusion.51.px.halo.pre_dt, f32[1024,768]{1,0:T(8,128)} %get-tuple-element.147.conv_ref, ...), custom_call_target="tpu_custom_call" | custom-call | flops 24000000000 | bytes 25165824 | tf_op jit(solution)/shard_map/scan_backward/pallas_call | solution.py:413
  388.5 11.2 %convolution_convert_fusion = bf16[1536,1920]{1,0:T(8,128)(2,1)} fusion(bf16[1024,1536]{1,0:T(8,128)(2,1)} %constant_dynamic-update-slice_fusion, bf16[1024,1920]{1,0:T(8,128)(2,1)} %get-tuple-element.229.rows), kind=kOutput, calls=%fused_computation | convolution fusion | flops 6042746880 | bytes 12976128 | tf_op jit(solution)/shard_map/dot_general | solution.py:31
  405.8 10.2 %rows_product.7 = (bf16[256,1536]{1,0:T(8,128)(2,1)S(1)}, bf16[256,1536]{1,0:T(8,128)(2,1)S(1)}, bf16[256,1536]{1,0:T(8,128)(2,1)S(1)}, bf16[256,1536]{1,0:T(8,128)(2,1)S(1)}) custom-call(bf16[1024,1920]{1,0:T(8,128)(2,1)} %get-tuple-element.229.rows, bf16[1536,1920]{1,0:T(8,128)(2,1)} %all-gather.5.cloned.1.call-done.w), custom_call_target="tpu_custom_call" | custom-call | flops 12079595520 | bytes 9830400 | tf_op jit(solution)/shard_map/rows_product/pallas_call | solution.py:498
  426.2 3.3 collective-permute-done.52
  429.5 4.7 collective-permute-done.53
  454.8 4.8 collective-permute-done.59
  482.1 7.1 %collective-permute-done.67 = bf16[192,128]{1,0:T(8,128)(2,1)S(1)} collective-permute-done((bf16[192,128]{1,0:T(8,128)(2,1)S(1)}, bf16[192,128]{1,0:T(8,128)(2,1)S(1)}, u32[]{:S(2)}, u32[]{:S(2)}) %collective-permute-start.67) | collective-permute-done | bytes 49184 | tf_op jit(solution)/shard_map/ppermute | solution.py:876
  (494 shorter events, 186.2 us)
Async XLA Ops:
  7.2 86.4 %all-gather.5.cloned.1.call-start = ((), (), s32[]{:S(2)}) async-start(), calls=%async_computation.4 | async-start | bytes 6635520 | tf_op jit(solution)/shard_map/all_gather | solution.py:621
  9.5 19.5 %collective-permute-start.5 = (bf16[192,1664]{1,0:T(8,128)(2,1)S(1)}, bf16[192,1664]{1,0:T(8,128)(2,1)S(1)}, u32[]{:S(2)}, u32[]{:S(2)}) collective-permute-start(bf16[192,1664]{1,0:T(8,128)(2,1)S(1)} %fusion.28), channel_id=1, source_target_pairs={{0,16},{16,0},{1,17},{17,1},{2,18},{18,2},{3,19},{19,3},{4,20},{20... | collective-permute-start | bytes 1916936 | tf_op jit(solution)/shard_map/ppermute | solution.py:531
  30.4 96.9 %all-gather.7.cloned.1.call-start = ((), (), s32[]{:S(2)}) async-start(), calls=%async_computation.5 | async-start | bytes 2654208 | tf_op jit(solution)/shard_map/all_gather | solution.py:622
  39.7 154.6 %all-gather.9.cloned.1.call-start = ((), (), s32[]{:S(2)}) async-start(), calls=%async_computation.6 | async-start | bytes 6635520 | tf_op jit(solution)/shard_map/all_gather | solution.py:621
  40.9 183.7 %all-gather.11.cloned.1.call-start = ((), (), s32[]{:S(2)}) async-start(), calls=%async_computation.7 | async-start | bytes 2654208 | tf_op jit(solution)/shard_map/all_gather | solution.py:622
  46.1 20.7 %collective-permute-start.10 = (f32[8,768]{1,0:T(8,128)S(1)}, f32[8,768]{1,0:T(8,128)S(1)}, u32[]{:S(2)}, u32[]{:S(2)}) collective-permute-start(f32[8,768]{1,0:T(8,128)S(1)} %pad_dynamic-slice_fusion.2), channel_id=1, source_target_pairs={{0,16},{16,0},{1,17},{17,1},{2,18},{18,2},{3,19},{19,3},{4,20},{20... | collective-permute-start | bytes 73736 | tf_op jit(solution)/shard_map/ppermute | solution.py:531
  52.9 13.9 %collective-permute-start.12 = (f32[8,256]{1,0:T(8,128)S(1)}, f32[8,256]{1,0:T(8,128)S(1)}, u32[]{:S(2)}, u32[]{:S(2)}) collective-permute-start(f32[8,256]{1,0:T(8,128)S(1)} %pad.33), channel_id=1, source_target_pairs={{0,16},{16,0},{1,17},{17,1},{2,18},{18,2},{3,19},{19,3},{4,20},{20... | collective-permute-start | bytes 24584 | tf_op jit(solution)/shard_map/ppermute | solution.py:531
  61.0 15.6 %collective-permute-start.4 = (bf16[256,1536]{1,0:T(8,128)(2,1)}, bf16[256,1536]{1,0:T(8,128)(2,1)}, u32[]{:S(2)}, u32[]{:S(2)}) collective-permute-start(bf16[256,1536]{1,0:T(8,128)(2,1)} %pad_maximum_fusion.2), channel_id=1, source_target_pairs={{0,16},{16,0},{1,17},{17,1},{2,18},{18,2},{3,19},{19,3},{4,20},{20... | collective-permute-start | bytes 2359304 | tf_op jit(solution)/shard_map/ppermute | solution.py:531
  64.5 15.0 %collective-permute-start.3 = (bf16[256,1536]{1,0:T(8,128)(2,1)}, bf16[256,1536]{1,0:T(8,128)(2,1)}, u32[]{:S(2)}, u32[]{:S(2)}) collective-permute-start(bf16[256,1536]{1,0:T(8,128)(2,1)} %pad_maximum_fusion.1), channel_id=1, source_target_pairs={{0,1},{1,0},{2,3},{3,2},{4,5},{5,4},{6,7},{7,6},{8,9},{9,8},{10,11... | collective-permute-start | bytes 2359304 | tf_op jit(solution)/shard_map/ppermute | solution.py:531
  66.9 236.8 %reduce-scatter.5.cloned.1.call-start = ((), (), s32[]{:S(2)}) async-start(), calls=%async_computation.8 | async-start | bytes 2654208 | tf_op jit(solution)/shard_map/reduce_scatter | solution.py:775
  87.1 18.4 %collective-permute-start.9 = (bf16[128,1536]{1,0:T(8,128)(2,1)}, bf16[128,1536]{1,0:T(8,128)(2,1)S(1)}, u32[]{:S(2)}, u32[]{:S(2)}) collective-permute-start(bf16[128,1536]{1,0:T(8,128)(2,1)} %get-tuple-element.343), channel_id=1, source_target_pairs={{0,1},{1,0},{2,3},{3,2},{4,5},{5,4},{6,7},{7,6},{8,9},{9,8},{10,11... | collective-permute-start | bytes 1179656 | tf_op jit(solution)/shard_map/ppermute | solution.py:531
  88.6 16.9 %collective-permute-start.8 = (bf16[128,1536]{1,0:T(8,128)(2,1)}, bf16[128,1536]{1,0:T(8,128)(2,1)S(1)}, u32[]{:S(2)}, u32[]{:S(2)}) collective-permute-start(bf16[128,1536]{1,0:T(8,128)(2,1)} %get-tuple-element.344), channel_id=1, source_target_pairs={{0,16},{16,0},{1,17},{17,1},{2,18},{18,2},{3,19},{19,3},{4,20},{20... | collective-permute-start | bytes 1179656 | tf_op jit(solution)/shard_map/ppermute | solution.py:531
  109.3 22.9 %collective-permute-start.17 = (bf16[256,1536]{1,0:T(8,128)(2,1)}, bf16[256,1536]{1,0:T(8,128)(2,1)}, u32[]{:S(2)}, u32[]{:S(2)}) collective-permute-start(bf16[256,1536]{1,0:T(8,128)(2,1)} %pad_maximum_fusion.4), channel_id=1, source_target_pairs={{0,16},{16,0},{1,17},{17,1},{2,18},{18,2},{3,19},{19,3},{4,20},{20... | collective-permute-start | bytes 2359304 | tf_op jit(solution)/shard_map/ppermute | solution.py:531
  110.8 21.4 %collective-permute-start.16 = (bf16[256,1536]{1,0:T(8,128)(2,1)}, bf16[256,1536]{1,0:T(8,128)(2,1)}, u32[]{:S(2)}, u32[]{:S(2)}) collective-permute-start(bf16[256,1536]{1,0:T(8,128)(2,1)} %pad_maximum_fusion.3), channel_id=1, source_target_pairs={{0,1},{1,0},{2,3},{3,2},{4,5},{5,4},{6,7},{7,6},{8,9},{9,8},{10,11... | collective-permute-start | bytes 2359304 | tf_op jit(solution)/shard_map/ppermute | solution.py:531
  132.3 19.5 %collective-permute-start.18 = (bf16[256,1536]{1,0:T(8,128)(2,1)S(1)}, bf16[256,1536]{1,0:T(8,128)(2,1)S(1)}, u32[]{:S(2)}, u32[]{:S(2)}) collective-permute-start(bf16[256,1536]{1,0:T(8,128)(2,1)S(1)} %get-tuple-element.158), channel_id=1, source_target_pairs={{0,1},{1,0},{2,3},{3,2},{4,5},{5,4},{6,7},{7,6},{8,9},{9,8},{10,11... | collective-permute-start | bytes 2359304 | tf_op jit(solution)/shard_map/ppermute | solution.py:531
  132.9 18.9 %collective-permute-start.19 = (bf16[256,1536]{1,0:T(8,128)(2,1)S(1)}, bf16[256,1536]{1,0:T(8,128)(2,1)S(1)}, u32[]{:S(2)}, u32[]{:S(2)}) collective-permute-start(bf16[256,1536]{1,0:T(8,128)(2,1)S(1)} %get-tuple-element.159), channel_id=1, source_target_pairs={{0,16},{16,0},{1,17},{17,1},{2,18},{18,2},{3,19},{19,3},{4,20},{20... | collective-permute-start | bytes 2359304 | tf_op jit(solution)/shard_map/ppermute | solution.py:531
  133.5 18.2 %collective-permute-start.21 = (f32[256]{0:T(256)S(1)}, f32[256]{0:T(256)S(1)}, u32[]{:S(2)}, u32[]{:S(2)}) collective-permute-start(f32[256]{0:T(256)S(1)} %bitcast.286), channel_id=1, source_target_pairs={{0,16},{16,0},{1,17},{17,1},{2,18},{18,2},{3,19},{19,3},{4,20},{20... | collective-permute-start | bytes 3080 | tf_op jit(solution)/shard_map/ppermute | solution.py:531
  135.1 16.7 %collective-permute-start.20 = (f32[256]{0:T(256)S(1)}, f32[256]{0:T(256)S(1)}, u32[]{:S(2)}, u32[]{:S(2)}) collective-permute-start(f32[256]{0:T(256)S(1)} %bitcast.285), channel_id=1, source_target_pairs={{0,1},{1,0},{2,3},{3,2},{4,5},{5,4},{6,7},{7,6},{8,9},{9,8},{10,11... | collective-permute-start | bytes 3080 | tf_op jit(solution)/shard_map/ppermute | solution.py:531
  176.7 16.1 %collective-permute-start.29 = (bf16[256,1536]{1,0:T(8,128)(2,1)S(1)}, bf16[256,1536]{1,0:T(8,128)(2,1)S(1)}, u32[]{:S(2)}, u32[]{:S(2)}) collective-permute-start(bf16[256,1536]{1,0:T(8,128)(2,1)S(1)} %pad_maximum_fusion.6), channel_id=1, source_target_pairs={{0,16},{16,0},{1,17},{17,1},{2,18},{18,2},{3,19},{19,3},{4,20},{20... | collective-permute-start | bytes 2359304 | tf_op jit(solution)/shard_map/ppermute | solution.py:531
  178.5 14.8 %collective-permute-start.28 = (bf16[256,1536]{1,0:T(8,128)(2,1)S(1)}, bf16[256,1536]{1,0:T(8,128)(2,1)S(1)}, u32[]{:S(2)}, u32[]{:S(2)}) collective-permute-start(bf16[256,1536]{1,0:T(8,128)(2,1)S(1)} %pad_maximum_fusion.5), channel_id=1, source_target_pairs={{0,1},{1,0},{2,3},{3,2},{4,5},{5,4},{6,7},{7,6},{8,9},{9,8},{10,11... | collective-permute-start | bytes 2359304 | tf_op jit(solution)/shard_map/ppermute | solution.py:531
  244.1 115.0 %reduce-scatter.7.cloned.1.call-start = ((), (), s32[]{:S(2)}) async-start(), calls=%async_computation.9 | async-start | bytes 6635520 | tf_op jit(solution)/shard_map/reduce_scatter | solution.py:790
  288.3 128.5 %reduce-scatter.11.cloned.1.call-start = ((), (), s32[]{:S(2)}) async-start(), calls=%async_computation.11 | async-start | bytes 2654208 | tf_op jit(solution)/shard_map/reduce_scatter | solution.py:805
  289.1 13.0 %collective-permute-start.36 = (bf16[256,1536]{1,0:T(8,128)(2,1)S(1)}, bf16[256,1536]{1,0:T(8,128)(2,1)}, u32[]{:S(2)}, u32[]{:S(2)}) collective-permute-start(bf16[256,1536]{1,0:T(8,128)(2,1)S(1)} %get-tuple-element.192), channel_id=1, source_target_pairs={{0,1},{1,0},{2,3},{3,2},{4,5},{5,4},{6,7},{7,6},{8,9},{9,8},{10,11... | collective-permute-start | bytes 2359304 | tf_op jit(solution)/shard_map/ppermute | solution.py:531
  289.3 14.4 %collective-permute-start.37 = (bf16[256,1536]{1,0:T(8,128)(2,1)S(1)}, bf16[256,1536]{1,0:T(8,128)(2,1)}, u32[]{:S(2)}, u32[]{:S(2)}) collective-permute-start(bf16[256,1536]{1,0:T(8,128)(2,1)S(1)} %get-tuple-element.193), channel_id=1, source_target_pairs={{0,16},{16,0},{1,17},{17,1},{2,18},{18,2},{3,19},{19,3},{4,20},{20... | collective-permute-start | bytes 2359304 | tf_op jit(solution)/shard_map/ppermute | solution.py:531
  359.1 114.0 %reduce-scatter.9.cloned.1.call-start = ((), (), s32[]{:S(2)}) async-start(), calls=%async_computation.10 | async-start | bytes 6635520 | tf_op jit(solution)/shard_map/reduce_scatter | solution.py:826
  359.2 29.3 %collective-permute-start.48 = (bf16[256,1536]{1,0:T(8,128)(2,1)S(1)}, bf16[256,1536]{1,0:T(8,128)(2,1)}, u32[]{:S(2)}, u32[]{:S(2)}) collective-permute-start(bf16[256,1536]{1,0:T(8,128)(2,1)S(1)} %get-tuple-element.224), channel_id=1, source_target_pairs={{0,1},{1,0},{2,3},{3,2},{4,5},{5,4},{6,7},{7,6},{8,9},{9,8},{10,11... | collective-permute-start | bytes 2359304 | tf_op jit(solution)/shard_map/ppermute | solution.py:531
  360.0 28.5 %collective-permute-start.49 = (bf16[256,1536]{1,0:T(8,128)(2,1)S(1)}, bf16[256,1536]{1,0:T(8,128)(2,1)}, u32[]{:S(2)}, u32[]{:S(2)}) collective-permute-start(bf16[256,1536]{1,0:T(8,128)(2,1)S(1)} %get-tuple-element.225), channel_id=1, source_target_pairs={{0,16},{16,0},{1,17},{17,1},{2,18},{18,2},{3,19},{19,3},{4,20},{20... | collective-permute-start | bytes 2359304 | tf_op jit(solution)/shard_map/ppermute | solution.py:531
  401.1 14.9 %collective-permute-start.50 = (bf16[128,1536]{1,0:T(8,128)(2,1)S(1)}, bf16[128,1536]{1,0:T(8,128)(2,1)S(1)}, u32[]{:S(2)}, u32[]{:S(2)}) collective-permute-start(bf16[128,1536]{1,0:T(8,128)(2,1)S(1)} %slice.546), channel_id=1, source_target_pairs={{0,16},{16,0},{1,17},{17,1},{2,18},{18,2},{3,19},{19,3},{4,20},{20... | collective-permute-start | bytes 1179656 | tf_op jit(solution)/shard_map/ppermute | solution.py:531
  417.4 16.8 %collective-permute-start.53 = (bf16[256,1536]{1,0:T(8,128)(2,1)S(1)}, bf16[256,1536]{1,0:T(8,128)(2,1)}, u32[]{:S(2)}, u32[]{:S(2)}) collective-permute-start(bf16[256,1536]{1,0:T(8,128)(2,1)S(1)} %get-tuple-element.241), channel_id=1, source_target_pairs={{0,16},{16,0},{1,17},{17,1},{2,18},{18,2},{3,19},{19,3},{4,20},{20... | collective-permute-start | bytes 2359304 | tf_op jit(solution)/shard_map/ppermute | solution.py:531
  423.4 16.0 %collective-permute-start.64 = (bf16[192,768]{1,0:T(8,128)(2,1)S(1)}, bf16[192,768]{1,0:T(8,128)(2,1)S(1)}, u32[]{:S(2)}, u32[]{:S(2)}) collective-permute-start(bf16[192,768]{1,0:T(8,128)(2,1)S(1)} %broadcast_select_fusion.7), channel_id=1, source_target_pairs={{0,16},{16,0},{1,17},{17,1},{2,18},{18,2},{3,19},{19,3},{4,20},{20... | collective-permute-start | bytes 884744 | tf_op jit(solution)/shard_map/ppermute | solution.py:531
  453.4 15.4 %collective-permute-start.57 = (bf16[2,128,1536]{2,1,0:T(8,128)(2,1)S(1)}, bf16[2,128,1536]{2,1,0:T(8,128)(2,1)}, u32[]{:S(2)}, u32[]{:S(2)}) collective-permute-start(bf16[2,128,1536]{2,1,0:T(8,128)(2,1)S(1)} %get-tuple-element.316), channel_id=1, source_target_pairs={{0,16},{16,0},{1,17},{17,1},{2,18},{18,2},{3,19},{19,3},{4,20},{20... | collective-permute-start | bytes 2359304 | tf_op jit(solution)/shard_map/ppermute | solution.py:531
  474.3 14.9 %collective-permute-start.65 = (bf16[192,1920]{1,0:T(8,128)(2,1)S(1)}, bf16[192,1920]{1,0:T(8,128)(2,1)S(1)}, u32[]{:S(2)}, u32[]{:S(2)}) collective-permute-start(bf16[192,1920]{1,0:T(8,128)(2,1)S(1)} %get-tuple-element.331), channel_id=1, source_target_pairs={{0,16},{16,0},{1,17},{17,1},{2,18},{18,2},{3,19},{19,3},{4,20},{20... | collective-permute-start | bytes 2211848 | tf_op jit(solution)/shard_map/ppermute | solution.py:531
  (98 other events, 664.7 us)
Sparse Core Ops, SparseCore 0:
  30.5 62.9 all-gather.4
  95.2 30.2 all-gather.6
  127.1 60.6 all-gather.8
  189.3 30.2 all-gather.10
  244.3 33.6 reduce-scatter.4
  288.4 63.4 reduce-scatter.6
  359.2 36.1 reduce-scatter.10
  399.8 70.0 reduce-scatter.8

commit v4 on v3

--- a/solution.py
+++ b/solution.py
@@ -399,7 +399,7 @@
         compiler_params=pltpu.CompilerParams(vmem_limit_bytes=40 * 2**20),
         cost_estimate=pl.CostEstimate(flops=12 * 10**9, bytes_accessed=14 * 2**20, transcendentals=5 * 10**6),
         name="scan_forward",
-    )(order, *hbm(px, px, px), *small[:5], *hbm(*small[5:]))
+    )(order, px, px, px, *small)
 
 
 def scan_backward(order, px, conv_x, y, states, d_out, stats, row_steps, col_steps, layer, fixed_arrays):
@@ -748,7 +748,7 @@
             jnp.sum(part.astype(f32) * a[i * part.shape[0] : (i + 1) * part.shape[0]].astype(f32), axis=0)
             for i, part in enumerate(da_part)
         ) / layer["norm"][0]
-        return jnp.concatenate([acc_x.reshape(-1), acc_bc.reshape(-1), jnp.sum(acc_dt, axis=1), norm])
+        return jnp.concatenate([acc_x[:7].reshape(-1), acc_bc[:5].reshape(-1), jnp.sum(acc_dt, axis=1), norm])
 
     def sum_steps():
         devices = lax.axis_size("dp")
@@ -845,17 +845,17 @@
     other_row = jnp.stack(mine_and_partners(from_tensor, from_diagonal))
     mine = jnp.stack([jnp.where(yy == 0, own_row, other_row), jnp.where(yy == 0, other_row, own_row)], axis=1)
     mine = mine.reshape(4, -1)
-    end_x, end_bc = 8 * width, 8 * width + 8 * 2 * N
+    end_x, end_bc = 7 * width, 7 * width + 5 * 2 * N
     end_dt = end_bc + 2 * HP
     over_all = jnp.sum(mine, axis=0)
     halves = lax.dynamic_index_in_dim(mine.reshape(2, 2, -1), yy, 1, keepdims=False)
-    by_x = halves[:, :end_x].reshape(2, 8, width).transpose(1, 0, 2).reshape(8, 2 * width)
+    by_x = halves[:, :end_x].reshape(2, 7, width).transpose(1, 0, 2).reshape(7, 2 * width)
     by_dt = halves[:, end_bc:end_dt].reshape(2, 2, HP)[:, :, :head_count].transpose(1, 0, 2).reshape(2, 2 * head_count)
     grad_conv_value = by_x[:5]
     grad_gate_gain = by_x[5]
     grad_skip = jnp.sum(by_x[6].reshape(2 * head_count, P_SIZE), axis=1)
     grad_heads = jnp.stack([by_dt[1], by_dt[0] * -jnp.exp(head_params[0, 1]), grad_skip])
-    bc_all = over_all[end_x:end_bc].reshape(8, 2 * N)[:5]
+    bc_all = over_all[end_x:end_bc].reshape(5, 2 * N)
     grad_conv_shared = lax.dynamic_slice_in_dim(bc_all, yy * N, N, 1)
     grad_norm = over_all[end_dt:]
 

time: 507 us -> 504 us (level)
  waiting for transfers between devices: 151 us -> 160 us
  other arithmetic: 45.4 us -> 39.7 us
    all_gather x2, waiting for transfers between devices: 4.4 us -> 10.4 us  [local(): lax.all_gather(packed, 'dp', axis=0, tiled=True)]
    unnamed x141 -> x138, local copies, waits for them, and re-layouts: 20.2 us -> 24.3 us
  transfers between devices with their start and end apart: 76 -> 76, of which waited for: 36 -> 36; matrix products, arithmetic and copies ran while one was open for 23% -> 21% of each run, Pallas kernels for 24% -> 23%
where the time goes in v4:
time: 504 us; the launch traced here: 500 us
  waiting for transfers between devices  160 us (32%)
  Pallas kernels  114 us (23%)
  starting transfers between devices  77.5 us (15%)
  matrix products  55.2 us (11%)
  other arithmetic  39.7 us (8%)
  local copies, waits for them, and re-layouts  36.6 us (7%)
  between operations  16.7 us (3%)
    ppermute x56, waiting for transfers between devices, swap(): return lax.ppermute(value, axis, [(0, 1), (1, 0)])  130 us
    ppermute x56, starting transfers between devices, swap(): return lax.ppermute(value, axis, [(0, 1), (1, 0)])  62.4 us
    pallas_call x2, Pallas kernels, scan_backward(): pl.pallas_call(bwd_kernel, grid_spec=pltpu.PrefetchScalarGridSpec(num_sca...  51.2 us
    dot_general x4, matrix products, dot_tn(): lax.dot_general(a, b, (((0,), (0,)), ((), ())), preferred_element_type=f32)  31.3 us
    pallas_call x4, Pallas kernels, rows_product(): pl.pallas_call(rows_kernel, grid=(3,), in_specs=[pl.BlockSpec(rows.shape,...  30.8 us
    pallas_call x2, Pallas kernels, scan_forward(): pl.pallas_call(fwd_kernel, grid_spec=pltpu.PrefetchScalarGridSpec(num_sca...  25.6 us
    unnamed x138, local copies, waits for them, and re-layouts  24.3 us
    dot_general x3, matrix products, dot_nn(): lax.dot_general(a, b, (((1,), (0,)), ((), ())), preferred_element_type=f32)  23.8 us
  transfers between devices with their start and end apart: 76, of which 36 were waited for; matrix products, arithmetic and copies ran while one was open for 21% of the time, Pallas kernels for 23%

profile of v4, /device:TPU:0, one launch (start us, length us, event | category | flops | bytes accessed | tf_op | source)
XLA Modules:
  0.0 499.7 jit_solution(18403926685579422526)
XLA Ops:
  17.0 12.1 %collective-permute-done.7 = bf16[192,256]{1,0:T(8,128)(2,1)S(1)} collective-permute-done((bf16[192,256]{1,0:T(8,128)(2,1)S(1)}, bf16[192,256]{1,0:T(8,128)(2,1)S(1)}, u32[]{:S(2)}, u32[]{:S(2)}) %collective-permute-start.7) | collective-permute-done | bytes 98336 | tf_op jit(solution)/shard_map/ppermute | solution.py:531
  32.3 6.5 %collective-permute-done.15 = bf16[192,768]{1,0:T(8,128)(2,1)S(1)} collective-permute-done((bf16[192,768]{1,0:T(8,128)(2,1)S(1)}, bf16[192,768]{1,0:T(8,128)(2,1)S(1)}, u32[]{:S(2)}, u32[]{:S(2)}) %collective-permute-start.15) | collective-permute-done | bytes 294944 | tf_op jit(solution)/shard_map/ppermute | solution.py:531
  53.0 4.5 collective-permute-done.2
  65.3 10.1 %collective-permute-done.4 = bf16[256,1536]{1,0:T(8,128)(2,1)} collective-permute-done((bf16[256,1536]{1,0:T(8,128)(2,1)}, bf16[256,1536]{1,0:T(8,128)(2,1)}, u32[]{:S(2)}, u32[]{:S(2)}) %collective-permute-start.4) | collective-permute-done | bytes 786464 | tf_op jit(solution)/shard_map/ppermute | solution.py:531
  83.0 10.4 %all-gather.5.cloned.1.call-done.w = bf16[1536,1920]{1,0:T(8,128)(2,1)} async-done(((bf16[192,1920]{1,0:T(8,128)(2,1)}), bf16[1536,1920]{1,0:T(8,128)(2,1)}) %all-gather.5.cloned.1.call-update) | async-done | bytes 5898256 | tf_op jit(solution)/shard_map/all_gather | solution.py:621
  93.5 9.8 %fusion.52.px.halo.pre_dt = f32[1024,1920]{1,0:T(8,128)S(1)} fusion(bf16[1024,1536]{1,0:T(8,128)(2,1)} %constant_dynamic-update-slice_fusion, bf16[1536,1920]{1,0:T(8,128)(2,1)} %all-gather.5.cloned.1.call-done.w), kind=kOutput, calls=%fused_computation.291 | convolution fusion | flops 6039797760 | bytes 16908288 | tf_op jit(solution)/shard_map/dot_general | solution.py:23
  108.1 12.6 %scan_forward.2 = (bf16[1024,768]{1,0:T(8,128)(2,1)}, f32[1024,768]{1,0:T(8,128)}, f32[1024,768]{1,0:T(8,128)}, bf16[8,128,768]{2,1,0:T(8,128)(2,1)}, f32[8,8,12...) custom-call(s32[8]{0:T(128)S(1)} %pad_add_fusion.order, ...), custom_call_target="tpu_custom_call" | custom-call | flops 12000000000 | bytes 14680064 | tf_op jit(solution)/shard_map/scan_forward/pallas_call | solution.py:368
  125.5 4.9 rows_product.4
  136.0 15.5 %collective-permute-done.21 = f32[256]{0:T(256)S(1)} collective-permute-done((f32[256]{0:T(256)S(1)}, f32[256]{0:T(256)S(1)}, u32[]{:S(2)}, u32[]{:S(2)}) %collective-permute-start.21) | collective-permute-done | bytes 1056 | tf_op jit(solution)/shard_map/ppermute | solution.py:531
  156.4 7.2 %collective-permute-done.22 = bf16[128,1536]{1,0:T(8,128)(2,1)S(1)} collective-permute-done((bf16[128,1536]{1,0:T(8,128)(2,1)S(1)}, bf16[128,1536]{1,0:T(8,128)(2,1)S(1)}, u32[]{:S(2)}, u32[]{:S(2)}) %collective-permute-start.22) | collective-permute-done | bytes 393248 | tf_op jit(solution)/shard_map/ppermute | solution.py:531
  169.3 5.6 %collective-permute-done.27 = bf16[128,1536]{1,0:T(8,128)(2,1)S(1)} collective-permute-done((bf16[128,1536]{1,0:T(8,128)(2,1)S(1)}, bf16[128,1536]{1,0:T(8,128)(2,1)S(1)}, u32[]{:S(2)}, u32[]{:S(2)}) %collective-permute-start.27) | collective-permute-done | bytes 393248 | tf_op jit(solution)/shard_map/ppermute | solution.py:531
  181.0 11.9 %collective-permute-done.29 = bf16[256,1536]{1,0:T(8,128)(2,1)S(1)} collective-permute-done((bf16[256,1536]{1,0:T(8,128)(2,1)S(1)}, bf16[256,1536]{1,0:T(8,128)(2,1)S(1)}, u32[]{:S(2)}, u32[]{:S(2)}) %collective-permute-start.29) | collective-permute-done | bytes 786464 | tf_op jit(solution)/shard_map/ppermute | solution.py:531
  196.7 9.8 %fusion.53.px.halo.pre_dt = f32[1024,1920]{1,0:T(8,128)S(1)} fusion(bf16[1024,1536]{1,0:T(8,128)(2,1)} %constant_dynamic-update-slice_fusion.6, bf16[1536,1920]{1,0:T(8,128)(2,1)} %all-gather.9.cloned.1.call-done.w), kind=kOutput, calls=%fused_computation.292 | convolution fusion | flops 6039797760 | bytes 16908288 | tf_op jit(solution)/shard_map/dot_general | solution.py:23
  206.5 12.9 %scan_forward.3 = (bf16[1024,768]{1,0:T(8,128)(2,1)}, f32[1024,768]{1,0:T(8,128)}, f32[1024,768]{1,0:T(8,128)}, bf16[8,128,768]{2,1,0:T(8,128)(2,1)}, f32[8,8,12...) custom-call(s32[8]{0:T(128)S(1)} %pad_add_fusion.order, ...), custom_call_target="tpu_custom_call" | custom-call | flops 12000000000 | bytes 14680064 | tf_op jit(solution)/shard_map/scan_forward/pallas_call | solution.py:368
  223.0 6.6 %rows_and_dots.1 = (f32[1024,768]{1,0:T(8,128)}, f32[8,8,128]{2,1,0:T(8,128)S(1)}) custom-call(bf16[1024,1536]{1,0:T(8,128)(2,1)} %copy-done.38, bf16[1536,768]{1,0:T(8,128)(2,1)} %all-gather.11.cloned.1.call-done.w_out.w, bf16[1024,768]{1,0:T(8,128)(2,1)} %get-tuple-element.208.og.rows), custom_call_target="tpu_custom_call" | custom-call | flops 4000000000 | bytes 10485760 | tf_op jit(solution)/shard_map/rows_and_dots/pallas_call | solution.py:469
  229.9 5.7 %convolution_convert_fusion.3 = bf16[1536,768]{1,0:T(8,128)(2,1)} fusion(bf16[1024,1536]{1,0:T(8,128)(2,1)S(1)} %copy-done.39, bf16[1024,768]{1,0:T(8,128)(2,1)} %get-tuple-element.208.og.rows, f32[1024]{0:T(1024)S(1)} %bitcast.270), kind=kOutput, calls=%fused_computation.3 | convolution fusion | flops 2419458048 | bytes 7081984 | tf_op jit(solution)/shard_map/dot_general | solution.py:31
  242.0 25.3 %scan_backward.2 = (bf16[1024,1920]{1,0:T(8,128)(2,1)}, f32[8,768]{1,0:T(8,128)S(1)}, f32[8,256]{1,0:T(8,128)S(1)}, f32[32,128]{1,0:T(8,128)S(1)}) custom-call(s32[8]{0:T(128)S(1)} %pad_add_fusion.order, f32[1024,1920]{1,0:T(8,128)} %copy-done.3, f32[1024,1920]{1,0:T(8,128)} %copy-done.3, f32[1024,768]{1,0:T(8,128)} %get-tuple-element.170.conv_ref, ...), custom_call_target="tpu_custom_call" | custom-call | flops 24000000000 | bytes 25165824 | tf_op jit(solution)/shard_map/scan_backward/pallas_call | solution.py:413
  267.4 10.2 %rows_product.5 = (bf16[256,1536]{1,0:T(8,128)(2,1)S(1)}, bf16[256,1536]{1,0:T(8,128)(2,1)S(1)}, bf16[256,1536]{1,0:T(8,128)(2,1)S(1)}, bf16[256,1536]{1,0:T(8,128)(2,1)S(1)}) custom-call(bf16[1024,1920]{1,0:T(8,128)(2,1)} %get-tuple-element.194.rows, bf16[1536,1920]{1,0:T(8,128)(2,1)} %all-gather.9.cloned.1.call-done.w), custom_call_target="tpu_custom_call" | custom-call | flops 12079595520 | bytes 9830400 | tf_op jit(solution)/shard_map/rows_product/pallas_call | solution.py:498
  277.6 10.5 %convolution_convert_fusion.1 = bf16[1536,1920]{1,0:T(8,128)(2,1)} fusion(bf16[1024,1536]{1,0:T(8,128)(2,1)} %constant_dynamic-update-slice_fusion.6, bf16[1024,1920]{1,0:T(8,128)(2,1)S(1)} %copy-done.53), kind=kOutput, calls=%fused_computation.1 | convolution fusion | flops 6042746880 | bytes 12976128 | tf_op jit(solution)/shard_map/dot_general | solution.py:31
  293.2 10.1 %collective-permute-done.36 = bf16[256,1536]{1,0:T(8,128)(2,1)} collective-permute-done((bf16[256,1536]{1,0:T(8,128)(2,1)S(1)}, bf16[256,1536]{1,0:T(8,128)(2,1)}, u32[]{:S(2)}, u32[]{:S(2)}) %collective-permute-start.36) | collective-permute-done | bytes 786464 | tf_op jit(solution)/shard_map/ppermute | solution.py:531
  310.5 5.4 %rows_product.6 = (bf16[256,1536]{1,0:T(8,128)(2,1)S(1)}, bf16[256,1536]{1,0:T(8,128)(2,1)S(1)}, bf16[256,1536]{1,0:T(8,128)(2,1)S(1)}, bf16[256,1536]{1,0:T(8,128)(2,1)S(1)}) custom-call(bf16[1024,768]{1,0:T(8,128)(2,1)} %get-tuple-element.208.og.rows, bf16[1536,768]{1,0:T(8,128)(2,1)} %all-gather.11.cloned.1.call-done.w_out.w), custom_call_target="tpu_custom_call" | custom-call | flops 4831838208 | bytes 3932160 | tf_op jit(solution)/shard_map/rows_product/pallas_call | solution.py:498
  325.1 9.5 %collective-permute-done.41 = bf16[128,1536]{1,0:T(8,128)(2,1)S(1)} collective-permute-done((bf16[128,1536]{1,0:T(8,128)(2,1)S(1)}, bf16[128,1536]{1,0:T(8,128)(2,1)S(1)}, u32[]{:S(2)}, u32[]{:S(2)}) %collective-permute-start.41) | collective-permute-done | bytes 393248 | tf_op jit(solution)/shard_map/ppermute | solution.py:531
  340.8 7.7 %collective-permute-done.47 = f32[256]{0:T(256)S(1)} collective-permute-done((f32[256]{0:T(256)S(1)}, f32[256]{0:T(256)S(1)}, u32[]{:S(2)}, u32[]{:S(2)}) %collective-permute-start.47) | collective-permute-done | bytes 1056 | tf_op jit(solution)/shard_map/ppermute | solution.py:531
  351.0 4.3 fusion.54.d_ref
  355.3 4.0 convolution_convert_fusion.2
  361.8 25.8 %scan_backward.3 = (bf16[1024,1920]{1,0:T(8,128)(2,1)}, f32[8,768]{1,0:T(8,128)S(1)}, f32[8,256]{1,0:T(8,128)S(1)}, f32[32,128]{1,0:T(8,128)S(1)}) custom-call(s32[8]{0:T(128)S(1)} %pad_add_fusion.order, f32[1024,1920]{1,0:T(8,128)} %copy-done.2, f32[1024,1920]{1,0:T(8,128)} %copy-done.2, f32[1024,768]{1,0:T(8,128)} %get-tuple-element.147.conv_ref, ...), custom_call_target="tpu_custom_call" | custom-call | flops 24000000000 | bytes 25165824 | tf_op jit(solution)/shard_map/scan_backward/pallas_call | solution.py:413
  388.4 11.2 %convolution_convert_fusion = bf16[1536,1920]{1,0:T(8,128)(2,1)} fusion(bf16[1024,1536]{1,0:T(8,128)(2,1)} %constant_dynamic-update-slice_fusion, bf16[1024,1920]{1,0:T(8,128)(2,1)} %get-tuple-element.229.rows), kind=kOutput, calls=%fused_computation | convolution fusion | flops 6042746880 | bytes 12976128 | tf_op jit(solution)/shard_map/dot_general | solution.py:31
  405.2 10.2 %rows_product.7 = (bf16[256,1536]{1,0:T(8,128)(2,1)S(1)}, bf16[256,1536]{1,0:T(8,128)(2,1)S(1)}, bf16[256,1536]{1,0:T(8,128)(2,1)S(1)}, bf16[256,1536]{1,0:T(8,128)(2,1)S(1)}) custom-call(bf16[1024,1920]{1,0:T(8,128)(2,1)} %get-tuple-element.229.rows, bf16[1536,1920]{1,0:T(8,128)(2,1)} %all-gather.5.cloned.1.call-done.w), custom_call_target="tpu_custom_call" | custom-call | flops 12079595520 | bytes 9830400 | tf_op jit(solution)/shard_map/rows_product/pallas_call | solution.py:498
  425.6 4.0 collective-permute-done.52
  429.6 4.6 collective-permute-done.53
  464.6 4.1 collective-permute-done.63
  482.0 6.8 %collective-permute-done.67 = bf16[192,128]{1,0:T(8,128)(2,1)S(1)} collective-permute-done((bf16[192,128]{1,0:T(8,128)(2,1)S(1)}, bf16[192,128]{1,0:T(8,128)(2,1)S(1)}, u32[]{:S(2)}, u32[]{:S(2)}) %collective-permute-start.67) | collective-permute-done | bytes 49184 | tf_op jit(solution)/shard_map/ppermute | solution.py:876
  (493 shorter events, 183.2 us)
Async XLA Ops:
  7.2 86.3 %all-gather.5.cloned.1.call-start = ((), (), s32[]{:S(2)}) async-start(), calls=%async_computation.4 | async-start | bytes 6635520 | tf_op jit(solution)/shard_map/all_gather | solution.py:621
  9.5 19.5 %collective-permute-start.5 = (bf16[192,1664]{1,0:T(8,128)(2,1)S(1)}, bf16[192,1664]{1,0:T(8,128)(2,1)S(1)}, u32[]{:S(2)}, u32[]{:S(2)}) collective-permute-start(bf16[192,1664]{1,0:T(8,128)(2,1)S(1)} %fusion.28), channel_id=1, source_target_pairs={{0,16},{16,0},{1,17},{17,1},{2,18},{18,2},{3,19},{19,3},{4,20},{20... | collective-permute-start | bytes 1916936 | tf_op jit(solution)/shard_map/ppermute | solution.py:531
  30.3 95.1 %all-gather.7.cloned.1.call-start = ((), (), s32[]{:S(2)}) async-start(), calls=%async_computation.5 | async-start | bytes 2654208 | tf_op jit(solution)/shard_map/all_gather | solution.py:622
  39.8 156.9 %all-gather.9.cloned.1.call-start = ((), (), s32[]{:S(2)}) async-start(), calls=%async_computation.6 | async-start | bytes 6635520 | tf_op jit(solution)/shard_map/all_gather | solution.py:621
  41.0 182.0 %all-gather.11.cloned.1.call-start = ((), (), s32[]{:S(2)}) async-start(), calls=%async_computation.7 | async-start | bytes 2654208 | tf_op jit(solution)/shard_map/all_gather | solution.py:622
  46.2 18.1 %collective-permute-start.10 = (f32[8,768]{1,0:T(8,128)S(1)}, f32[8,768]{1,0:T(8,128)S(1)}, u32[]{:S(2)}, u32[]{:S(2)}) collective-permute-start(f32[8,768]{1,0:T(8,128)S(1)} %pad_dynamic-slice_fusion.2), channel_id=1, source_target_pairs={{0,16},{16,0},{1,17},{17,1},{2,18},{18,2},{3,19},{19,3},{4,20},{20... | collective-permute-start | bytes 73736 | tf_op jit(solution)/shard_map/ppermute | solution.py:531
  59.4 15.9 %collective-permute-start.4 = (bf16[256,1536]{1,0:T(8,128)(2,1)}, bf16[256,1536]{1,0:T(8,128)(2,1)}, u32[]{:S(2)}, u32[]{:S(2)}) collective-permute-start(bf16[256,1536]{1,0:T(8,128)(2,1)} %pad_maximum_fusion.2), channel_id=1, source_target_pairs={{0,16},{16,0},{1,17},{17,1},{2,18},{18,2},{3,19},{19,3},{4,20},{20... | collective-permute-start | bytes 2359304 | tf_op jit(solution)/shard_map/ppermute | solution.py:531
  62.0 14.4 %collective-permute-start.3 = (bf16[256,1536]{1,0:T(8,128)(2,1)}, bf16[256,1536]{1,0:T(8,128)(2,1)S(1)}, u32[]{:S(2)}, u32[]{:S(2)}) collective-permute-start(bf16[256,1536]{1,0:T(8,128)(2,1)} %pad_maximum_fusion.1), channel_id=1, source_target_pairs={{0,1},{1,0},{2,3},{3,2},{4,5},{5,4},{6,7},{7,6},{8,9},{9,8},{10,11... | collective-permute-start | bytes 2359304 | tf_op jit(solution)/shard_map/ppermute | solution.py:531
  64.3 240.2 %reduce-scatter.5.cloned.1.call-start = ((), (), s32[]{:S(2)}) async-start(), calls=%async_computation.8 | async-start | bytes 2654208 | tf_op jit(solution)/shard_map/reduce_scatter | solution.py:775
  80.9 22.4 %collective-permute-start.9 = (bf16[128,1536]{1,0:T(8,128)(2,1)S(1)}, bf16[128,1536]{1,0:T(8,128)(2,1)S(1)}, u32[]{:S(2)}, u32[]{:S(2)}) collective-permute-start(bf16[128,1536]{1,0:T(8,128)(2,1)S(1)} %get-tuple-element.365), channel_id=1, source_target_pairs={{0,1},{1,0},{2,3},{3,2},{4,5},{5,4},{6,7},{7,6},{8,9},{9,8},{10,11... | collective-permute-start | bytes 1179656 | tf_op jit(solution)/shard_map/ppermute | solution.py:531
  82.5 20.8 %collective-permute-start.8 = (bf16[128,1536]{1,0:T(8,128)(2,1)S(1)}, bf16[128,1536]{1,0:T(8,128)(2,1)S(1)}, u32[]{:S(2)}, u32[]{:S(2)}) collective-permute-start(bf16[128,1536]{1,0:T(8,128)(2,1)S(1)} %get-tuple-element.366), channel_id=1, source_target_pairs={{0,16},{16,0},{1,17},{17,1},{2,18},{18,2},{3,19},{19,3},{4,20},{20... | collective-permute-start | bytes 1179656 | tf_op jit(solution)/shard_map/ppermute | solution.py:531
  105.2 25.2 %collective-permute-start.17 = (bf16[256,1536]{1,0:T(8,128)(2,1)}, bf16[256,1536]{1,0:T(8,128)(2,1)S(1)}, u32[]{:S(2)}, u32[]{:S(2)}) collective-permute-start(bf16[256,1536]{1,0:T(8,128)(2,1)} %pad_maximum_fusion.4), channel_id=1, source_target_pairs={{0,16},{16,0},{1,17},{17,1},{2,18},{18,2},{3,19},{19,3},{4,20},{20... | collective-permute-start | bytes 2359304 | tf_op jit(solution)/shard_map/ppermute | solution.py:531
  106.7 23.8 %collective-permute-start.16 = (bf16[256,1536]{1,0:T(8,128)(2,1)}, bf16[256,1536]{1,0:T(8,128)(2,1)}, u32[]{:S(2)}, u32[]{:S(2)}) collective-permute-start(bf16[256,1536]{1,0:T(8,128)(2,1)} %pad_maximum_fusion.3), channel_id=1, source_target_pairs={{0,1},{1,0},{2,3},{3,2},{4,5},{5,4},{6,7},{7,6},{8,9},{9,8},{10,11... | collective-permute-start | bytes 2359304 | tf_op jit(solution)/shard_map/ppermute | solution.py:531
  130.4 21.0 %collective-permute-start.18 = (bf16[256,1536]{1,0:T(8,128)(2,1)S(1)}, bf16[256,1536]{1,0:T(8,128)(2,1)S(1)}, u32[]{:S(2)}, u32[]{:S(2)}) collective-permute-start(bf16[256,1536]{1,0:T(8,128)(2,1)S(1)} %get-tuple-element.158), channel_id=1, source_target_pairs={{0,1},{1,0},{2,3},{3,2},{4,5},{5,4},{6,7},{7,6},{8,9},{9,8},{10,11... | collective-permute-start | bytes 2359304 | tf_op jit(solution)/shard_map/ppermute | solution.py:531
  132.0 19.5 %collective-permute-start.19 = (bf16[256,1536]{1,0:T(8,128)(2,1)S(1)}, bf16[256,1536]{1,0:T(8,128)(2,1)S(1)}, u32[]{:S(2)}, u32[]{:S(2)}) collective-permute-start(bf16[256,1536]{1,0:T(8,128)(2,1)S(1)} %get-tuple-element.159), channel_id=1, source_target_pairs={{0,16},{16,0},{1,17},{17,1},{2,18},{18,2},{3,19},{19,3},{4,20},{20... | collective-permute-start | bytes 2359304 | tf_op jit(solution)/shard_map/ppermute | solution.py:531
  133.5 18.0 %collective-permute-start.21 = (f32[256]{0:T(256)S(1)}, f32[256]{0:T(256)S(1)}, u32[]{:S(2)}, u32[]{:S(2)}) collective-permute-start(f32[256]{0:T(256)S(1)} %bitcast.284), channel_id=1, source_target_pairs={{0,16},{16,0},{1,17},{17,1},{2,18},{18,2},{3,19},{19,3},{4,20},{20... | collective-permute-start | bytes 3080 | tf_op jit(solution)/shard_map/ppermute | solution.py:531
  134.1 17.3 %collective-permute-start.20 = (f32[256]{0:T(256)S(1)}, f32[256]{0:T(256)S(1)}, u32[]{:S(2)}, u32[]{:S(2)}) collective-permute-start(f32[256]{0:T(256)S(1)} %bitcast.283), channel_id=1, source_target_pairs={{0,1},{1,0},{2,3},{3,2},{4,5},{5,4},{6,7},{7,6},{8,9},{9,8},{10,11... | collective-permute-start | bytes 3080 | tf_op jit(solution)/shard_map/ppermute | solution.py:531
  177.0 16.0 %collective-permute-start.29 = (bf16[256,1536]{1,0:T(8,128)(2,1)S(1)}, bf16[256,1536]{1,0:T(8,128)(2,1)S(1)}, u32[]{:S(2)}, u32[]{:S(2)}) collective-permute-start(bf16[256,1536]{1,0:T(8,128)(2,1)S(1)} %pad_maximum_fusion.6), channel_id=1, source_target_pairs={{0,16},{16,0},{1,17},{17,1},{2,18},{18,2},{3,19},{19,3},{4,20},{20... | collective-permute-start | bytes 2359304 | tf_op jit(solution)/shard_map/ppermute | solution.py:531
  178.4 14.8 %collective-permute-start.28 = (bf16[256,1536]{1,0:T(8,128)(2,1)S(1)}, bf16[256,1536]{1,0:T(8,128)(2,1)S(1)}, u32[]{:S(2)}, u32[]{:S(2)}) collective-permute-start(bf16[256,1536]{1,0:T(8,128)(2,1)S(1)} %pad_maximum_fusion.5), channel_id=1, source_target_pairs={{0,1},{1,0},{2,3},{3,2},{4,5},{5,4},{6,7},{7,6},{8,9},{9,8},{10,11... | collective-permute-start | bytes 2359304 | tf_op jit(solution)/shard_map/ppermute | solution.py:531
  241.9 117.3 %reduce-scatter.7.cloned.1.call-start = ((), (), s32[]{:S(2)}) async-start(), calls=%async_computation.9 | async-start | bytes 6635520 | tf_op jit(solution)/shard_map/reduce_scatter | solution.py:790
  288.1 128.1 %reduce-scatter.11.cloned.1.call-start = ((), (), s32[]{:S(2)}) async-start(), calls=%async_computation.11 | async-start | bytes 2654208 | tf_op jit(solution)/shard_map/reduce_scatter | solution.py:805
  288.3 14.9 %collective-permute-start.36 = (bf16[256,1536]{1,0:T(8,128)(2,1)S(1)}, bf16[256,1536]{1,0:T(8,128)(2,1)}, u32[]{:S(2)}, u32[]{:S(2)}) collective-permute-start(bf16[256,1536]{1,0:T(8,128)(2,1)S(1)} %get-tuple-element.192), channel_id=1, source_target_pairs={{0,1},{1,0},{2,3},{3,2},{4,5},{5,4},{6,7},{7,6},{8,9},{9,8},{10,11... | collective-permute-start | bytes 2359304 | tf_op jit(solution)/shard_map/ppermute | solution.py:531
  289.2 15.3 %collective-permute-start.37 = (bf16[256,1536]{1,0:T(8,128)(2,1)S(1)}, bf16[256,1536]{1,0:T(8,128)(2,1)}, u32[]{:S(2)}, u32[]{:S(2)}) collective-permute-start(bf16[256,1536]{1,0:T(8,128)(2,1)S(1)} %get-tuple-element.193), channel_id=1, source_target_pairs={{0,16},{16,0},{1,17},{17,1},{2,18},{18,2},{3,19},{19,3},{4,20},{20... | collective-permute-start | bytes 2359304 | tf_op jit(solution)/shard_map/ppermute | solution.py:531
  359.3 114.3 %reduce-scatter.9.cloned.1.call-start = ((), (), s32[]{:S(2)}) async-start(), calls=%async_computation.10 | async-start | bytes 6635520 | tf_op jit(solution)/shard_map/reduce_scatter | solution.py:826
  359.3 29.0 %collective-permute-start.48 = (bf16[256,1536]{1,0:T(8,128)(2,1)S(1)}, bf16[256,1536]{1,0:T(8,128)(2,1)}, u32[]{:S(2)}, u32[]{:S(2)}) collective-permute-start(bf16[256,1536]{1,0:T(8,128)(2,1)S(1)} %get-tuple-element.224), channel_id=1, source_target_pairs={{0,1},{1,0},{2,3},{3,2},{4,5},{5,4},{6,7},{7,6},{8,9},{9,8},{10,11... | collective-permute-start | bytes 2359304 | tf_op jit(solution)/shard_map/ppermute | solution.py:531
  360.3 28.0 %collective-permute-start.49 = (bf16[256,1536]{1,0:T(8,128)(2,1)S(1)}, bf16[256,1536]{1,0:T(8,128)(2,1)}, u32[]{:S(2)}, u32[]{:S(2)}) collective-permute-start(bf16[256,1536]{1,0:T(8,128)(2,1)S(1)} %get-tuple-element.225), channel_id=1, source_target_pairs={{0,16},{16,0},{1,17},{17,1},{2,18},{18,2},{3,19},{19,3},{4,20},{20... | collective-permute-start | bytes 2359304 | tf_op jit(solution)/shard_map/ppermute | solution.py:531
  401.1 14.4 %collective-permute-start.50 = (bf16[128,1536]{1,0:T(8,128)(2,1)S(1)}, bf16[128,1536]{1,0:T(8,128)(2,1)S(1)}, u32[]{:S(2)}, u32[]{:S(2)}) collective-permute-start(bf16[128,1536]{1,0:T(8,128)(2,1)S(1)} %slice.554), channel_id=1, source_target_pairs={{0,16},{16,0},{1,17},{17,1},{2,18},{18,2},{3,19},{19,3},{4,20},{20... | collective-permute-start | bytes 1179656 | tf_op jit(solution)/shard_map/ppermute | solution.py:531
  416.2 13.4 %collective-permute-start.52 = (bf16[256,1536]{1,0:T(8,128)(2,1)S(1)}, bf16[256,1536]{1,0:T(8,128)(2,1)}, u32[]{:S(2)}, u32[]{:S(2)}) collective-permute-start(bf16[256,1536]{1,0:T(8,128)(2,1)S(1)} %get-tuple-element.240), channel_id=1, source_target_pairs={{0,1},{1,0},{2,3},{3,2},{4,5},{5,4},{6,7},{7,6},{8,9},{9,8},{10,11... | collective-permute-start | bytes 2359304 | tf_op jit(solution)/shard_map/ppermute | solution.py:531
  417.1 17.1 %collective-permute-start.53 = (bf16[256,1536]{1,0:T(8,128)(2,1)S(1)}, bf16[256,1536]{1,0:T(8,128)(2,1)}, u32[]{:S(2)}, u32[]{:S(2)}) collective-permute-start(bf16[256,1536]{1,0:T(8,128)(2,1)S(1)} %get-tuple-element.241), channel_id=1, source_target_pairs={{0,16},{16,0},{1,17},{17,1},{2,18},{18,2},{3,19},{19,3},{4,20},{20... | collective-permute-start | bytes 2359304 | tf_op jit(solution)/shard_map/ppermute | solution.py:531
  422.8 16.3 %collective-permute-start.64 = (bf16[192,768]{1,0:T(8,128)(2,1)S(1)}, bf16[192,768]{1,0:T(8,128)(2,1)S(1)}, u32[]{:S(2)}, u32[]{:S(2)}) collective-permute-start(bf16[192,768]{1,0:T(8,128)(2,1)S(1)} %broadcast_select_fusion.7), channel_id=1, source_target_pairs={{0,16},{16,0},{1,17},{17,1},{2,18},{18,2},{3,19},{19,3},{4,20},{20... | collective-permute-start | bytes 884744 | tf_op jit(solution)/shard_map/ppermute | solution.py:531
  453.5 15.2 %collective-permute-start.57 = (bf16[2,128,1536]{2,1,0:T(8,128)(2,1)S(1)}, bf16[2,128,1536]{2,1,0:T(8,128)(2,1)}, u32[]{:S(2)}, u32[]{:S(2)}) collective-permute-start(bf16[2,128,1536]{2,1,0:T(8,128)(2,1)S(1)} %get-tuple-element.338), channel_id=1, source_target_pairs={{0,16},{16,0},{1,17},{17,1},{2,18},{18,2},{3,19},{19,3},{4,20},{20... | collective-permute-start | bytes 2359304 | tf_op jit(solution)/shard_map/ppermute | solution.py:531
  474.8 13.9 %collective-permute-start.65 = (bf16[192,1920]{1,0:T(8,128)(2,1)S(1)}, bf16[192,1920]{1,0:T(8,128)(2,1)S(1)}, u32[]{:S(2)}, u32[]{:S(2)}) collective-permute-start(bf16[192,1920]{1,0:T(8,128)(2,1)S(1)} %get-tuple-element.353), channel_id=1, source_target_pairs={{0,16},{16,0},{1,17},{17,1},{2,18},{18,2},{3,19},{19,3},{4,20},{20... | collective-permute-start | bytes 2211848 | tf_op jit(solution)/shard_map/ppermute | solution.py:531
  (98 other events, 590.3 us)
Sparse Core Ops, SparseCore 0:
  30.4 62.9 all-gather.4
  95.1 30.2 all-gather.6
  127.1 60.6 all-gather.8
  189.3 30.2 all-gather.10
  242.1 34.3 reduce-scatter.4
  288.2 64.2 reduce-scatter.6
  359.4 34.8 reduce-scatter.10
  399.7 67.9 reduce-scatter.8

commit v5 on v4

--- a/solution.py
+++ b/solution.py
@@ -792,7 +792,14 @@
 
     do_own = (dv * r_first).astype(bf16)
     kappa = r_first[:, :, 0] ** 2 * jnp.sum(dv * o_first, axis=2) / DI
-    do, stat = spread_all(do_own, kappa)
+    stat_parts = [kappa] + [
+        lax.ppermute(kappa, ("section", "tensor"), list(enumerate(pairs)))
+        for pairs in ((2, 3, 0, 1), (1, 0, 3, 2), (3, 2, 1, 0))
+    ]
+    (do,) = spread_all(do_own)
+    do, stat_parts = tied((do, stat_parts))
+    places = ((0, 1, 2, 3), (0, 2, 1, 3))
+    stat = jnp.concatenate([stat_parts[i][s] for s in range(streams) for i in places[s]])
     do, o_part = tied((do, o_part))
     u, rho, a, pre, og, y, conv_x, states, sq, row_steps, col_steps = saved[0]
     w_in, w_out = weights[0]

time: 504 us -> 504 us (level)
    ppermute x56 -> x52, starting transfers between devices: 62.4 us -> 59.9 us  [swap(): return lax.ppermute(value, axis, [(0, 1), (1, 0)])]
    ppermute x56 -> x52, waiting for transfers between devices: 130 us -> 128 us  [swap(): return lax.ppermute(value, axis, [(0, 1), (1, 0)])]
    unnamed x138 -> x140, local copies, waits for them, and re-layouts: 24.3 us -> 25 us
  transfers between devices with their start and end apart: 76 -> 75, of which waited for: 36 -> 36; matrix products, arithmetic and copies ran while one was open for 21% -> 21% of each run, Pallas kernels for 23% -> 23%
where the time goes in v5:
time: 504 us; the launch traced here: 500 us
  waiting for transfers between devices  158 us (31%)
  Pallas kernels  114 us (23%)
  starting transfers between devices  78.4 us (16%)
  matrix products  55.3 us (11%)
  other arithmetic  39.7 us (8%)
  local copies, waits for them, and re-layouts  37.3 us (7%)
  between operations  16.7 us (3%)
    ppermute x52, waiting for transfers between devices, swap(): return lax.ppermute(value, axis, [(0, 1), (1, 0)])  128 us
    ppermute x52, starting transfers between devices, swap(): return lax.ppermute(value, axis, [(0, 1), (1, 0)])  59.9 us
    pallas_call x2, Pallas kernels, scan_backward(): pl.pallas_call(bwd_kernel, grid_spec=pltpu.PrefetchScalarGridSpec(num_sca...  51 us
    dot_general x4, matrix products, dot_tn(): lax.dot_general(a, b, (((0,), (0,)), ((), ())), preferred_element_type=f32)  31.4 us
    pallas_call x4, Pallas kernels, rows_product(): pl.pallas_call(rows_kernel, grid=(3,), in_specs=[pl.BlockSpec(rows.shape,...  30.5 us
    pallas_call x2, Pallas kernels, scan_forward(): pl.pallas_call(fwd_kernel, grid_spec=pltpu.PrefetchScalarGridSpec(num_sca...  25.8 us
    unnamed x140, local copies, waits for them, and re-layouts  25 us
    dot_general x3, matrix products, dot_nn(): lax.dot_general(a, b, (((1,), (0,)), ((), ())), preferred_element_type=f32)  23.9 us
  transfers between devices with their start and end apart: 75, of which 36 were waited for; matrix products, arithmetic and copies ran while one was open for 21% of the time, Pallas kernels for 23%

profile of v5, /device:TPU:0, one launch (start us, length us, event | category | flops | bytes accessed | tf_op | source)
XLA Modules:
  0.0 499.6 jit_solution(1337109935656413306)
XLA Ops:
  17.0 12.1 %collective-permute-done.7 = bf16[192,256]{1,0:T(8,128)(2,1)S(1)} collective-permute-done((bf16[192,256]{1,0:T(8,128)(2,1)S(1)}, bf16[192,256]{1,0:T(8,128)(2,1)S(1)}, u32[]{:S(2)}, u32[]{:S(2)}) %collective-permute-start.7) | collective-permute-done | bytes 98336 | tf_op jit(solution)/shard_map/ppermute | solution.py:531
  32.3 6.5 %collective-permute-done.15 = bf16[192,768]{1,0:T(8,128)(2,1)S(1)} collective-permute-done((bf16[192,768]{1,0:T(8,128)(2,1)S(1)}, bf16[192,768]{1,0:T(8,128)(2,1)S(1)}, u32[]{:S(2)}, u32[]{:S(2)}) %collective-permute-start.15) | collective-permute-done | bytes 294944 | tf_op jit(solution)/shard_map/ppermute | solution.py:531
  52.9 4.5 collective-permute-done.2
  65.3 10.1 %collective-permute-done.4 = bf16[256,1536]{1,0:T(8,128)(2,1)} collective-permute-done((bf16[256,1536]{1,0:T(8,128)(2,1)}, bf16[256,1536]{1,0:T(8,128)(2,1)}, u32[]{:S(2)}, u32[]{:S(2)}) %collective-permute-start.4) | collective-permute-done | bytes 786464 | tf_op jit(solution)/shard_map/ppermute | solution.py:531
  83.0 10.5 %all-gather.5.cloned.1.call-done.w = bf16[1536,1920]{1,0:T(8,128)(2,1)} async-done(((bf16[192,1920]{1,0:T(8,128)(2,1)}), bf16[1536,1920]{1,0:T(8,128)(2,1)}) %all-gather.5.cloned.1.call-update) | async-done | bytes 5898256 | tf_op jit(solution)/shard_map/all_gather | solution.py:621
  93.5 9.8 %fusion.52.px.halo.pre_dt = f32[1024,1920]{1,0:T(8,128)S(1)} fusion(bf16[1024,1536]{1,0:T(8,128)(2,1)} %constant_dynamic-update-slice_fusion, bf16[1536,1920]{1,0:T(8,128)(2,1)} %all-gather.5.cloned.1.call-done.w), kind=kOutput, calls=%fused_computation.289 | convolution fusion | flops 6039797760 | bytes 16908288 | tf_op jit(solution)/shard_map/dot_general | solution.py:23
  108.1 12.6 %scan_forward.2 = (bf16[1024,768]{1,0:T(8,128)(2,1)}, f32[1024,768]{1,0:T(8,128)}, f32[1024,768]{1,0:T(8,128)}, bf16[8,128,768]{2,1,0:T(8,128)(2,1)}, f32[8,8,12...) custom-call(s32[8]{0:T(128)S(1)} %pad_add_fusion.order, ...), custom_call_target="tpu_custom_call" | custom-call | flops 12000000000 | bytes 14680064 | tf_op jit(solution)/shard_map/scan_forward/pallas_call | solution.py:368
  125.5 4.9 rows_product.4
  136.0 15.5 %collective-permute-done.21 = f32[256]{0:T(256)S(1)} collective-permute-done((f32[256]{0:T(256)S(1)}, f32[256]{0:T(256)S(1)}, u32[]{:S(2)}, u32[]{:S(2)}) %collective-permute-start.21) | collective-permute-done | bytes 1056 | tf_op jit(solution)/shard_map/ppermute | solution.py:531
  156.4 7.2 %collective-permute-done.22 = bf16[128,1536]{1,0:T(8,128)(2,1)S(1)} collective-permute-done((bf16[128,1536]{1,0:T(8,128)(2,1)S(1)}, bf16[128,1536]{1,0:T(8,128)(2,1)S(1)}, u32[]{:S(2)}, u32[]{:S(2)}) %collective-permute-start.22) | collective-permute-done | bytes 393248 | tf_op jit(solution)/shard_map/ppermute | solution.py:531
  169.3 5.6 %collective-permute-done.27 = bf16[128,1536]{1,0:T(8,128)(2,1)S(1)} collective-permute-done((bf16[128,1536]{1,0:T(8,128)(2,1)S(1)}, bf16[128,1536]{1,0:T(8,128)(2,1)S(1)}, u32[]{:S(2)}, u32[]{:S(2)}) %collective-permute-start.27) | collective-permute-done | bytes 393248 | tf_op jit(solution)/shard_map/ppermute | solution.py:531
  181.0 11.9 %collective-permute-done.29 = bf16[256,1536]{1,0:T(8,128)(2,1)S(1)} collective-permute-done((bf16[256,1536]{1,0:T(8,128)(2,1)S(1)}, bf16[256,1536]{1,0:T(8,128)(2,1)S(1)}, u32[]{:S(2)}, u32[]{:S(2)}) %collective-permute-start.29) | collective-permute-done | bytes 786464 | tf_op jit(solution)/shard_map/ppermute | solution.py:531
  196.7 9.8 %fusion.53.px.halo.pre_dt = f32[1024,1920]{1,0:T(8,128)S(1)} fusion(bf16[1024,1536]{1,0:T(8,128)(2,1)} %constant_dynamic-update-slice_fusion.6, bf16[1536,1920]{1,0:T(8,128)(2,1)} %all-gather.9.cloned.1.call-done.w), kind=kOutput, calls=%fused_computation.290 | convolution fusion | flops 6039797760 | bytes 16908288 | tf_op jit(solution)/shard_map/dot_general | solution.py:23
  206.5 13.2 %scan_forward.3 = (bf16[1024,768]{1,0:T(8,128)(2,1)}, f32[1024,768]{1,0:T(8,128)}, f32[1024,768]{1,0:T(8,128)}, bf16[8,128,768]{2,1,0:T(8,128)(2,1)}, f32[8,8,12...) custom-call(s32[8]{0:T(128)S(1)} %pad_add_fusion.order, ...), custom_call_target="tpu_custom_call" | custom-call | flops 12000000000 | bytes 14680064 | tf_op jit(solution)/shard_map/scan_forward/pallas_call | solution.py:368
  223.3 6.6 %rows_and_dots.1 = (f32[1024,768]{1,0:T(8,128)}, f32[8,8,128]{2,1,0:T(8,128)S(1)}) custom-call(bf16[1024,1536]{1,0:T(8,128)(2,1)} %copy-done.38, bf16[1536,768]{1,0:T(8,128)(2,1)} %all-gather.11.cloned.1.call-done.w_out.w, bf16[1024,768]{1,0:T(8,128)(2,1)} %get-tuple-element.208.og.rows), custom_call_target="tpu_custom_call" | custom-call | flops 4000000000 | bytes 10485760 | tf_op jit(solution)/shard_map/rows_and_dots/pallas_call | solution.py:469
  230.1 5.7 %convolution_convert_fusion.3 = bf16[1536,768]{1,0:T(8,128)(2,1)} fusion(bf16[1024,1536]{1,0:T(8,128)(2,1)S(1)} %copy-done.39, bf16[1024,768]{1,0:T(8,128)(2,1)} %get-tuple-element.208.og.rows, f32[1024]{0:T(1024)S(1)} %bitcast.277), kind=kOutput, calls=%fused_computation.3 | convolution fusion | flops 2419458048 | bytes 7081984 | tf_op jit(solution)/shard_map/dot_general | solution.py:31
  242.2 25.3 %scan_backward.2 = (bf16[1024,1920]{1,0:T(8,128)(2,1)}, f32[8,768]{1,0:T(8,128)S(1)}, f32[8,256]{1,0:T(8,128)S(1)}, f32[32,128]{1,0:T(8,128)S(1)}) custom-call(s32[8]{0:T(128)S(1)} %pad_add_fusion.order, f32[1024,1920]{1,0:T(8,128)} %copy-done.3, f32[1024,1920]{1,0:T(8,128)} %copy-done.3, f32[1024,768]{1,0:T(8,128)} %get-tuple-element.171.conv_ref, ...), custom_call_target="tpu_custom_call" | custom-call | flops 24000000000 | bytes 25165824 | tf_op jit(solution)/shard_map/scan_backward/pallas_call | solution.py:413
  267.6 10.2 %rows_product.5 = (bf16[256,1536]{1,0:T(8,128)(2,1)S(1)}, bf16[256,1536]{1,0:T(8,128)(2,1)S(1)}, bf16[256,1536]{1,0:T(8,128)(2,1)S(1)}, bf16[256,1536]{1,0:T(8,128)(2,1)S(1)}) custom-call(bf16[1024,1920]{1,0:T(8,128)(2,1)} %get-tuple-element.195.rows, bf16[1536,1920]{1,0:T(8,128)(2,1)} %all-gather.9.cloned.1.call-done.w), custom_call_target="tpu_custom_call" | custom-call | flops 12079595520 | bytes 9830400 | tf_op jit(solution)/shard_map/rows_product/pallas_call | solution.py:498
  277.8 10.5 %convolution_convert_fusion.1 = bf16[1536,1920]{1,0:T(8,128)(2,1)} fusion(bf16[1024,1536]{1,0:T(8,128)(2,1)} %constant_dynamic-update-slice_fusion.6, bf16[1024,1920]{1,0:T(8,128)(2,1)S(1)} %copy-done.53), kind=kOutput, calls=%fused_computation.1 | convolution fusion | flops 6042746880 | bytes 12976128 | tf_op jit(solution)/shard_map/dot_general | solution.py:31
  293.5 9.9 %collective-permute-done.36 = bf16[256,1536]{1,0:T(8,128)(2,1)} collective-permute-done((bf16[256,1536]{1,0:T(8,128)(2,1)S(1)}, bf16[256,1536]{1,0:T(8,128)(2,1)}, u32[]{:S(2)}, u32[]{:S(2)}) %collective-permute-start.36) | collective-permute-done | bytes 786464 | tf_op jit(solution)/shard_map/ppermute | solution.py:531
  310.5 5.2 %collective-permute-done.38 = bf16[128,1536]{1,0:T(8,128)(2,1)S(1)} collective-permute-done((bf16[128,1536]{1,0:T(8,128)(2,1)S(1)}, bf16[128,1536]{1,0:T(8,128)(2,1)S(1)}, u32[]{:S(2)}, u32[]{:S(2)}) %collective-permute-start.38) | collective-permute-done | bytes 393248 | tf_op jit(solution)/shard_map/ppermute | solution.py:531
  323.7 5.2 %rows_product.6 = (bf16[256,1536]{1,0:T(8,128)(2,1)S(1)}, bf16[256,1536]{1,0:T(8,128)(2,1)S(1)}, bf16[256,1536]{1,0:T(8,128)(2,1)S(1)}, bf16[256,1536]{1,0:T(8,128)(2,1)S(1)}) custom-call(bf16[1024,768]{1,0:T(8,128)(2,1)} %get-tuple-element.208.og.rows, bf16[1536,768]{1,0:T(8,128)(2,1)} %all-gather.11.cloned.1.call-done.w_out.w), custom_call_target="tpu_custom_call" | custom-call | flops 4831838208 | bytes 3932160 | tf_op jit(solution)/shard_map/rows_product/pallas_call | solution.py:498
  341.0 5.4 %collective-permute-done.43 = bf16[256,1536]{1,0:T(8,128)(2,1)S(1)} collective-permute-done((bf16[256,1536]{1,0:T(8,128)(2,1)S(1)}, bf16[256,1536]{1,0:T(8,128)(2,1)S(1)}, u32[]{:S(2)}, u32[]{:S(2)}) %collective-permute-start.43) | collective-permute-done | bytes 786464 | tf_op jit(solution)/shard_map/ppermute | solution.py:531
  349.6 4.3 fusion.54.d_ref
  354.0 4.0 convolution_convert_fusion.2
  360.4 25.6 %scan_backward.3 = (bf16[1024,1920]{1,0:T(8,128)(2,1)}, f32[8,768]{1,0:T(8,128)S(1)}, f32[8,256]{1,0:T(8,128)S(1)}, f32[32,128]{1,0:T(8,128)S(1)}) custom-call(s32[8]{0:T(128)S(1)} %pad_add_fusion.order, f32[1024,1920]{1,0:T(8,128)} %copy-done.2, f32[1024,1920]{1,0:T(8,128)} %copy-done.2, f32[1024,768]{1,0:T(8,128)} %get-tuple-element.148.conv_ref, ...), custom_call_target="tpu_custom_call" | custom-call | flops 24000000000 | bytes 25165824 | tf_op jit(solution)/shard_map/scan_backward/pallas_call | solution.py:413
  386.8 11.2 %convolution_convert_fusion = bf16[1536,1920]{1,0:T(8,128)(2,1)} fusion(bf16[1024,1536]{1,0:T(8,128)(2,1)} %constant_dynamic-update-slice_fusion, bf16[1024,1920]{1,0:T(8,128)(2,1)} %get-tuple-element.231.rows), kind=kOutput, calls=%fused_computation | convolution fusion | flops 6042746880 | bytes 12976128 | tf_op jit(solution)/shard_map/dot_general | solution.py:31
  403.7 10.2 %rows_product.7 = (bf16[256,1536]{1,0:T(8,128)(2,1)S(1)}, bf16[256,1536]{1,0:T(8,128)(2,1)S(1)}, bf16[256,1536]{1,0:T(8,128)(2,1)S(1)}, bf16[256,1536]{1,0:T(8,128)(2,1)S(1)}) custom-call(bf16[1024,1920]{1,0:T(8,128)(2,1)} %get-tuple-element.231.rows, bf16[1536,1920]{1,0:T(8,128)(2,1)} %all-gather.5.cloned.1.call-done.w), custom_call_target="tpu_custom_call" | custom-call | flops 12079595520 | bytes 9830400 | tf_op jit(solution)/shard_map/rows_product/pallas_call | solution.py:498
  424.9 4.0 collective-permute-done.51
  428.9 5.4 %collective-permute-done.52 = bf16[256,1536]{1,0:T(8,128)(2,1)} collective-permute-done((bf16[256,1536]{1,0:T(8,128)(2,1)S(1)}, bf16[256,1536]{1,0:T(8,128)(2,1)}, u32[]{:S(2)}, u32[]{:S(2)}) %collective-permute-start.52) | collective-permute-done | bytes 786464 | tf_op jit(solution)/shard_map/ppermute | solution.py:531
  464.8 4.0 collective-permute-done.62
  482.1 6.5 %collective-permute-done.66 = bf16[192,128]{1,0:T(8,128)(2,1)S(1)} collective-permute-done((bf16[192,128]{1,0:T(8,128)(2,1)S(1)}, bf16[192,128]{1,0:T(8,128)(2,1)S(1)}, u32[]{:S(2)}, u32[]{:S(2)}) %collective-permute-start.66) | collective-permute-done | bytes 49184 | tf_op jit(solution)/shard_map/ppermute | solution.py:883
  (489 shorter events, 189.5 us)
Async XLA Ops:
  7.2 86.3 %all-gather.5.cloned.1.call-start = ((), (), s32[]{:S(2)}) async-start(), calls=%async_computation.4 | async-start | bytes 6635520 | tf_op jit(solution)/shard_map/all_gather | solution.py:621
  9.5 19.5 %collective-permute-start.5 = (bf16[192,1664]{1,0:T(8,128)(2,1)S(1)}, bf16[192,1664]{1,0:T(8,128)(2,1)S(1)}, u32[]{:S(2)}, u32[]{:S(2)}) collective-permute-start(bf16[192,1664]{1,0:T(8,128)(2,1)S(1)} %fusion.28), channel_id=1, source_target_pairs={{0,16},{16,0},{1,17},{17,1},{2,18},{18,2},{3,19},{19,3},{4,20},{20... | collective-permute-start | bytes 1916936 | tf_op jit(solution)/shard_map/ppermute | solution.py:531
  30.3 95.1 %all-gather.7.cloned.1.call-start = ((), (), s32[]{:S(2)}) async-start(), calls=%async_computation.5 | async-start | bytes 2654208 | tf_op jit(solution)/shard_map/all_gather | solution.py:622
  39.8 156.9 %all-gather.9.cloned.1.call-start = ((), (), s32[]{:S(2)}) async-start(), calls=%async_computation.6 | async-start | bytes 6635520 | tf_op jit(solution)/shard_map/all_gather | solution.py:621
  41.0 182.3 %all-gather.11.cloned.1.call-start = ((), (), s32[]{:S(2)}) async-start(), calls=%async_computation.7 | async-start | bytes 2654208 | tf_op jit(solution)/shard_map/all_gather | solution.py:622
  46.1 18.1 %collective-permute-start.10 = (f32[8,768]{1,0:T(8,128)S(1)}, f32[8,768]{1,0:T(8,128)S(1)}, u32[]{:S(2)}, u32[]{:S(2)}) collective-permute-start(f32[8,768]{1,0:T(8,128)S(1)} %pad_dynamic-slice_fusion.2), channel_id=1, source_target_pairs={{0,16},{16,0},{1,17},{17,1},{2,18},{18,2},{3,19},{19,3},{4,20},{20... | collective-permute-start | bytes 73736 | tf_op jit(solution)/shard_map/ppermute | solution.py:531
  59.4 15.9 %collective-permute-start.4 = (bf16[256,1536]{1,0:T(8,128)(2,1)}, bf16[256,1536]{1,0:T(8,128)(2,1)}, u32[]{:S(2)}, u32[]{:S(2)}) collective-permute-start(bf16[256,1536]{1,0:T(8,128)(2,1)} %pad_maximum_fusion.2), channel_id=1, source_target_pairs={{0,16},{16,0},{1,17},{17,1},{2,18},{18,2},{3,19},{19,3},{4,20},{20... | collective-permute-start | bytes 2359304 | tf_op jit(solution)/shard_map/ppermute | solution.py:531
  61.9 14.4 %collective-permute-start.3 = (bf16[256,1536]{1,0:T(8,128)(2,1)}, bf16[256,1536]{1,0:T(8,128)(2,1)S(1)}, u32[]{:S(2)}, u32[]{:S(2)}) collective-permute-start(bf16[256,1536]{1,0:T(8,128)(2,1)} %pad_maximum_fusion.1), channel_id=1, source_target_pairs={{0,1},{1,0},{2,3},{3,2},{4,5},{5,4},{6,7},{7,6},{8,9},{9,8},{10,11... | collective-permute-start | bytes 2359304 | tf_op jit(solution)/shard_map/ppermute | solution.py:531
  64.3 240.3 %reduce-scatter.5.cloned.1.call-start = ((), (), s32[]{:S(2)}) async-start(), calls=%async_computation.8 | async-start | bytes 2654208 | tf_op jit(solution)/shard_map/reduce_scatter | solution.py:775
  80.9 22.4 %collective-permute-start.9 = (bf16[128,1536]{1,0:T(8,128)(2,1)S(1)}, bf16[128,1536]{1,0:T(8,128)(2,1)S(1)}, u32[]{:S(2)}, u32[]{:S(2)}) collective-permute-start(bf16[128,1536]{1,0:T(8,128)(2,1)S(1)} %get-tuple-element.367), channel_id=1, source_target_pairs={{0,1},{1,0},{2,3},{3,2},{4,5},{5,4},{6,7},{7,6},{8,9},{9,8},{10,11... | collective-permute-start | bytes 1179656 | tf_op jit(solution)/shard_map/ppermute | solution.py:531
  82.5 20.8 %collective-permute-start.8 = (bf16[128,1536]{1,0:T(8,128)(2,1)S(1)}, bf16[128,1536]{1,0:T(8,128)(2,1)S(1)}, u32[]{:S(2)}, u32[]{:S(2)}) collective-permute-start(bf16[128,1536]{1,0:T(8,128)(2,1)S(1)} %get-tuple-element.368), channel_id=1, source_target_pairs={{0,16},{16,0},{1,17},{17,1},{2,18},{18,2},{3,19},{19,3},{4,20},{20... | collective-permute-start | bytes 1179656 | tf_op jit(solution)/shard_map/ppermute | solution.py:531
  105.2 25.2 %collective-permute-start.17 = (bf16[256,1536]{1,0:T(8,128)(2,1)}, bf16[256,1536]{1,0:T(8,128)(2,1)S(1)}, u32[]{:S(2)}, u32[]{:S(2)}) collective-permute-start(bf16[256,1536]{1,0:T(8,128)(2,1)} %pad_maximum_fusion.4), channel_id=1, source_target_pairs={{0,16},{16,0},{1,17},{17,1},{2,18},{18,2},{3,19},{19,3},{4,20},{20... | collective-permute-start | bytes 2359304 | tf_op jit(solution)/shard_map/ppermute | solution.py:531
  106.7 23.8 %collective-permute-start.16 = (bf16[256,1536]{1,0:T(8,128)(2,1)}, bf16[256,1536]{1,0:T(8,128)(2,1)}, u32[]{:S(2)}, u32[]{:S(2)}) collective-permute-start(bf16[256,1536]{1,0:T(8,128)(2,1)} %pad_maximum_fusion.3), channel_id=1, source_target_pairs={{0,1},{1,0},{2,3},{3,2},{4,5},{5,4},{6,7},{7,6},{8,9},{9,8},{10,11... | collective-permute-start | bytes 2359304 | tf_op jit(solution)/shard_map/ppermute | solution.py:531
  130.4 21.0 %collective-permute-start.18 = (bf16[256,1536]{1,0:T(8,128)(2,1)S(1)}, bf16[256,1536]{1,0:T(8,128)(2,1)S(1)}, u32[]{:S(2)}, u32[]{:S(2)}) collective-permute-start(bf16[256,1536]{1,0:T(8,128)(2,1)S(1)} %get-tuple-element.159), channel_id=1, source_target_pairs={{0,1},{1,0},{2,3},{3,2},{4,5},{5,4},{6,7},{7,6},{8,9},{9,8},{10,11... | collective-permute-start | bytes 2359304 | tf_op jit(solution)/shard_map/ppermute | solution.py:531
  132.0 19.5 %collective-permute-start.19 = (bf16[256,1536]{1,0:T(8,128)(2,1)S(1)}, bf16[256,1536]{1,0:T(8,128)(2,1)S(1)}, u32[]{:S(2)}, u32[]{:S(2)}) collective-permute-start(bf16[256,1536]{1,0:T(8,128)(2,1)S(1)} %get-tuple-element.160), channel_id=1, source_target_pairs={{0,16},{16,0},{1,17},{17,1},{2,18},{18,2},{3,19},{19,3},{4,20},{20... | collective-permute-start | bytes 2359304 | tf_op jit(solution)/shard_map/ppermute | solution.py:531
  133.5 18.0 %collective-permute-start.21 = (f32[256]{0:T(256)S(1)}, f32[256]{0:T(256)S(1)}, u32[]{:S(2)}, u32[]{:S(2)}) collective-permute-start(f32[256]{0:T(256)S(1)} %bitcast.290), channel_id=1, source_target_pairs={{0,16},{16,0},{1,17},{17,1},{2,18},{18,2},{3,19},{19,3},{4,20},{20... | collective-permute-start | bytes 3080 | tf_op jit(solution)/shard_map/ppermute | solution.py:531
  134.1 17.3 %collective-permute-start.20 = (f32[256]{0:T(256)S(1)}, f32[256]{0:T(256)S(1)}, u32[]{:S(2)}, u32[]{:S(2)}) collective-permute-start(f32[256]{0:T(256)S(1)} %bitcast.289), channel_id=1, source_target_pairs={{0,1},{1,0},{2,3},{3,2},{4,5},{5,4},{6,7},{7,6},{8,9},{9,8},{10,11... | collective-permute-start | bytes 3080 | tf_op jit(solution)/shard_map/ppermute | solution.py:531
  176.9 16.0 %collective-permute-start.29 = (bf16[256,1536]{1,0:T(8,128)(2,1)S(1)}, bf16[256,1536]{1,0:T(8,128)(2,1)S(1)}, u32[]{:S(2)}, u32[]{:S(2)}) collective-permute-start(bf16[256,1536]{1,0:T(8,128)(2,1)S(1)} %pad_maximum_fusion.6), channel_id=1, source_target_pairs={{0,16},{16,0},{1,17},{17,1},{2,18},{18,2},{3,19},{19,3},{4,20},{20... | collective-permute-start | bytes 2359304 | tf_op jit(solution)/shard_map/ppermute | solution.py:531
  178.4 14.8 %collective-permute-start.28 = (bf16[256,1536]{1,0:T(8,128)(2,1)S(1)}, bf16[256,1536]{1,0:T(8,128)(2,1)S(1)}, u32[]{:S(2)}, u32[]{:S(2)}) collective-permute-start(bf16[256,1536]{1,0:T(8,128)(2,1)S(1)} %pad_maximum_fusion.5), channel_id=1, source_target_pairs={{0,1},{1,0},{2,3},{3,2},{4,5},{5,4},{6,7},{7,6},{8,9},{9,8},{10,11... | collective-permute-start | bytes 2359304 | tf_op jit(solution)/shard_map/ppermute | solution.py:531
  242.1 115.8 %reduce-scatter.7.cloned.1.call-start = ((), (), s32[]{:S(2)}) async-start(), calls=%async_computation.9 | async-start | bytes 6635520 | tf_op jit(solution)/shard_map/reduce_scatter | solution.py:790
  288.3 126.3 %reduce-scatter.11.cloned.1.call-start = ((), (), s32[]{:S(2)}) async-start(), calls=%async_computation.11 | async-start | bytes 2654208 | tf_op jit(solution)/shard_map/reduce_scatter | solution.py:812
  288.6 14.7 %collective-permute-start.36 = (bf16[256,1536]{1,0:T(8,128)(2,1)S(1)}, bf16[256,1536]{1,0:T(8,128)(2,1)}, u32[]{:S(2)}, u32[]{:S(2)}) collective-permute-start(bf16[256,1536]{1,0:T(8,128)(2,1)S(1)} %get-tuple-element.193), channel_id=1, source_target_pairs={{0,1},{1,0},{2,3},{3,2},{4,5},{5,4},{6,7},{7,6},{8,9},{9,8},{10,11... | collective-permute-start | bytes 2359304 | tf_op jit(solution)/shard_map/ppermute | solution.py:531
  289.5 15.1 %collective-permute-start.37 = (bf16[256,1536]{1,0:T(8,128)(2,1)S(1)}, bf16[256,1536]{1,0:T(8,128)(2,1)}, u32[]{:S(2)}, u32[]{:S(2)}) collective-permute-start(bf16[256,1536]{1,0:T(8,128)(2,1)S(1)} %get-tuple-element.194), channel_id=1, source_target_pairs={{0,16},{16,0},{1,17},{17,1},{2,18},{18,2},{3,19},{19,3},{4,20},{20... | collective-permute-start | bytes 2359304 | tf_op jit(solution)/shard_map/ppermute | solution.py:531
  358.0 115.6 %reduce-scatter.9.cloned.1.call-start = ((), (), s32[]{:S(2)}) async-start(), calls=%async_computation.10 | async-start | bytes 6635520 | tf_op jit(solution)/shard_map/reduce_scatter | solution.py:833
  358.1 28.7 %collective-permute-start.47 = (bf16[256,1536]{1,0:T(8,128)(2,1)S(1)}, bf16[256,1536]{1,0:T(8,128)(2,1)}, u32[]{:S(2)}, u32[]{:S(2)}) collective-permute-start(bf16[256,1536]{1,0:T(8,128)(2,1)S(1)} %get-tuple-element.226), channel_id=1, source_target_pairs={{0,1},{1,0},{2,3},{3,2},{4,5},{5,4},{6,7},{7,6},{8,9},{9,8},{10,11... | collective-permute-start | bytes 2359304 | tf_op jit(solution)/shard_map/ppermute | solution.py:531
  359.7 27.1 %collective-permute-start.48 = (bf16[256,1536]{1,0:T(8,128)(2,1)S(1)}, bf16[256,1536]{1,0:T(8,128)(2,1)}, u32[]{:S(2)}, u32[]{:S(2)}) collective-permute-start(bf16[256,1536]{1,0:T(8,128)(2,1)S(1)} %get-tuple-element.227), channel_id=1, source_target_pairs={{0,16},{16,0},{1,17},{17,1},{2,18},{18,2},{3,19},{19,3},{4,20},{20... | collective-permute-start | bytes 2359304 | tf_op jit(solution)/shard_map/ppermute | solution.py:531
  399.5 14.4 %collective-permute-start.49 = (bf16[128,1536]{1,0:T(8,128)(2,1)S(1)}, bf16[128,1536]{1,0:T(8,128)(2,1)S(1)}, u32[]{:S(2)}, u32[]{:S(2)}) collective-permute-start(bf16[128,1536]{1,0:T(8,128)(2,1)S(1)} %slice.578), channel_id=1, source_target_pairs={{0,16},{16,0},{1,17},{17,1},{2,18},{18,2},{3,19},{19,3},{4,20},{20... | collective-permute-start | bytes 1179656 | tf_op jit(solution)/shard_map/ppermute | solution.py:531
  414.7 14.3 %collective-permute-start.51 = (bf16[256,1536]{1,0:T(8,128)(2,1)S(1)}, bf16[256,1536]{1,0:T(8,128)(2,1)}, u32[]{:S(2)}, u32[]{:S(2)}) collective-permute-start(bf16[256,1536]{1,0:T(8,128)(2,1)S(1)} %get-tuple-element.242), channel_id=1, source_target_pairs={{0,1},{1,0},{2,3},{3,2},{4,5},{5,4},{6,7},{7,6},{8,9},{9,8},{10,11... | collective-permute-start | bytes 2359304 | tf_op jit(solution)/shard_map/ppermute | solution.py:531
  416.5 17.9 %collective-permute-start.52 = (bf16[256,1536]{1,0:T(8,128)(2,1)S(1)}, bf16[256,1536]{1,0:T(8,128)(2,1)}, u32[]{:S(2)}, u32[]{:S(2)}) collective-permute-start(bf16[256,1536]{1,0:T(8,128)(2,1)S(1)} %get-tuple-element.243), channel_id=1, source_target_pairs={{0,16},{16,0},{1,17},{17,1},{2,18},{18,2},{3,19},{19,3},{4,20},{20... | collective-permute-start | bytes 2359304 | tf_op jit(solution)/shard_map/ppermute | solution.py:531
  421.2 18.2 %collective-permute-start.63 = (bf16[192,768]{1,0:T(8,128)(2,1)S(1)}, bf16[192,768]{1,0:T(8,128)(2,1)S(1)}, u32[]{:S(2)}, u32[]{:S(2)}) collective-permute-start(bf16[192,768]{1,0:T(8,128)(2,1)S(1)} %broadcast_select_fusion.7), channel_id=1, source_target_pairs={{0,16},{16,0},{1,17},{17,1},{2,18},{18,2},{3,19},{19,3},{4,20},{20... | collective-permute-start | bytes 884744 | tf_op jit(solution)/shard_map/ppermute | solution.py:531
  453.6 15.2 %collective-permute-start.56 = (bf16[2,128,1536]{2,1,0:T(8,128)(2,1)S(1)}, bf16[2,128,1536]{2,1,0:T(8,128)(2,1)}, u32[]{:S(2)}, u32[]{:S(2)}) collective-permute-start(bf16[2,128,1536]{2,1,0:T(8,128)(2,1)S(1)} %get-tuple-element.340), channel_id=1, source_target_pairs={{0,16},{16,0},{1,17},{17,1},{2,18},{18,2},{3,19},{19,3},{4,20},{20... | collective-permute-start | bytes 2359304 | tf_op jit(solution)/shard_map/ppermute | solution.py:531
  474.9 13.7 %collective-permute-start.64 = (bf16[192,1920]{1,0:T(8,128)(2,1)S(1)}, bf16[192,1920]{1,0:T(8,128)(2,1)S(1)}, u32[]{:S(2)}, u32[]{:S(2)}) collective-permute-start(bf16[192,1920]{1,0:T(8,128)(2,1)S(1)} %get-tuple-element.355), channel_id=1, source_target_pairs={{0,16},{16,0},{1,17},{17,1},{2,18},{18,2},{3,19},{19,3},{4,20},{20... | collective-permute-start | bytes 2211848 | tf_op jit(solution)/shard_map/ppermute | solution.py:531
  (97 other events, 594.4 us)
Sparse Core Ops, SparseCore 0:
  30.4 62.9 all-gather.4
  95.1 30.2 all-gather.6
  127.1 60.6 all-gather.8
  189.3 30.3 all-gather.10
  242.3 34.3 reduce-scatter.4
  288.5 64.2 reduce-scatter.6
  358.1 34.8 reduce-scatter.10
  398.2 68.1 reduce-scatter.8
